TPU v7x, 512 devices: a whole 4x8x8 slice. The times are simulated.
512 devices in a mesh: tour: 128 (over z, y_lo, x, core), width: 4 (over y_hi).
Axes of the slice: x: 4, y: 8 (y_hi: 4, y_lo: 2; y = y_hi * 2 + y_lo), z: 8, core: 2. Of those that a mesh axis runs over, the one named last changes fastest.
Arguments:
- images: bfloat16 [32768, 1152], P('tour', 'width'), may hold values from -1.1953125 to 1.1953125
- texts: bfloat16 [32768, 1152], P('tour', 'width'), may hold values from -1.1953125 to 1.1953125
- matches: int32 [128, 256], P('tour'), may hold values from 0 to 255, each once within a row
- scale: float32 [1], replicated, may hold values from 0.7 to 2.5
- shift_bias: float32 [1], replicated, may hold values from -3 to 0
Outputs:
- grad_images: float32 [32768, 1152], P('tour', 'width')
- grad_texts: float32 [32768, 1152], P('tour', 'width')
All inputs are finite; a program needn't handle non-finite values.
Results may differ from a plain program's by a relative error of at most 0.0025.
Values may be sent and summed in bfloat16 or wider, within the bound.
No kernel may reach another device: no remote copies, remote signals or barrier semaphores. Data moves between devices by JAX's collectives and lax.ppermute only.
A program may use at most 64 MiB of HBM per device.

v0:
```python
import jax
import jax.numpy as jnp
from jax import lax
from jax.sharding import PartitionSpec as P

REACH = 7


def shifted(block, axis, distance):
    devices = range(lax.axis_size(axis))
    route = [((i - distance) % len(devices), i) for i in devices]
    return lax.ppermute(block, axis, route)


def cross_rows(left, right):
    return lax.dot_general(
        left, right, (((1,), (1,)), ((), ())), preferred_element_type=jnp.float32
    )


def cross_cols(weights, right):
    return lax.dot_general(
        weights, right, (((0,), (0,)), ((), ())), preferred_element_type=jnp.float32
    )


def per_device(images, texts, matches, scale, shift_bias):
    temper = scale[0]
    offset_bias = shift_bias[0]
    rows = images.shape[0]
    columns = lax.broadcasted_iota(jnp.int32, (rows, rows), 1)
    positive = (columns == matches[0][:, None]).astype(jnp.float32)

    def to_weights(total, label):
        probs = jax.nn.sigmoid(temper * total + offset_bias)
        if label is not None:
            probs = probs - label
        return probs.astype(jnp.bfloat16)

    def finish(parts, labels):
        totals = lax.psum(parts, "width")
        return tuple((to_weights(total, label) for total, label in zip(totals, labels)))

    own = finish((cross_rows(images, texts),), (positive,))[0]
    grad_image = jnp.dot(own, texts, preferred_element_type=jnp.float32)
    grad_text = cross_cols(own, images)
    for step in range(1, REACH + 1):
        lower = shifted(texts, "tour", step)
        upper = shifted(texts, "tour", -step)
        weight_low, weight_up = finish(
            (cross_rows(images, lower), cross_rows(images, upper)), (None, None)
        )
        grad_image = grad_image + jnp.dot(weight_low, lower, preferred_element_type=jnp.float32)
        grad_image = grad_image + jnp.dot(weight_up, upper, preferred_element_type=jnp.float32)
        back_low = shifted(cross_cols(weight_low, images), "tour", -step)
        back_up = shifted(cross_cols(weight_up, images), "tour", step)
        grad_text = grad_text + back_low + back_up
    return (temper * grad_image, temper * grad_text)


def solution(mesh):
    placed = (P("tour", "width"), P("tour", "width"), P("tour", None), P(), P())
    return jax.shard_map(
        per_device,
        mesh=mesh,
        in_specs=placed,
        out_specs=(P("tour", "width"), P("tour", "width")),
        check_vma=False,
    )
```

profile of v0, /device:TPU:16, one launch (start us, length us, event | category | flops | bytes accessed | tf_op | source)
XLA Modules:
  0.0 355.9 jit_solution(9492157760198567002)
XLA Ops:
  7.2 11.5 %collective-permute-start.13 = (bf16[256,288]{0,1:T(8,128)(2,1)}, bf16[256,288]{0,1:T(8,128)(2,1)S(1)}, u32[]{:S(2)}, u32[]{:S(2)}) collective-permute-start(bf16[256,288]{0,1:T(8,128)(2,1)} %param.6), channel_id=1, source_target_pairs={{28,0},{32,4},{36,8},{40,12},{44,16},{48,20},{52,24},{56,28},{60,3... | collective-permute-start | bytes 442376 | tf_op jit(solution)/shard_map/ppermute | solution.py:12
  18.8 1.9 collective-permute-start.12
  20.7 8.1 %collective-permute-start.11 = (bf16[256,288]{0,1:T(8,128)(2,1)}, bf16[256,288]{0,1:T(8,128)(2,1)S(1)}, u32[]{:S(2)}, u32[]{:S(2)}) collective-permute-start(bf16[256,288]{0,1:T(8,128)(2,1)} %param.6), channel_id=1, source_target_pairs={{24,0},{28,4},{32,8},{36,12},{40,16},{44,20},{48,24},{52,28},{56,3... | collective-permute-start | bytes 442376 | tf_op jit(solution)/shard_map/ppermute | solution.py:12
  28.8 1.9 collective-permute-start.10
  30.8 4.9 %collective-permute-start.9 = (bf16[256,288]{0,1:T(8,128)(2,1)}, bf16[256,288]{0,1:T(8,128)(2,1)S(1)}, u32[]{:S(2)}, u32[]{:S(2)}) collective-permute-start(bf16[256,288]{0,1:T(8,128)(2,1)} %param.6), channel_id=1, source_target_pairs={{20,0},{24,4},{28,8},{32,12},{36,16},{40,20},{44,24},{48,28},{52,3... | collective-permute-start | bytes 442376 | tf_op jit(solution)/shard_map/ppermute | solution.py:12
  35.7 1.9 fusion.54
  37.6 2.1 collective-permute-start.8
  40.7 11.5 %collective-permute-start.7 = (bf16[256,288]{0,1:T(8,128)(2,1)S(1)}, bf16[256,288]{0,1:T(8,128)(2,1)S(1)}, u32[]{:S(2)}, u32[]{:S(2)}) collective-permute-start(bf16[256,288]{0,1:T(8,128)(2,1)S(1)} %copy-done.3), channel_id=1, source_target_pairs={{16,0},{20,4},{24,8},{28,12},{32,16},{36,20},{40,24},{44,28},{48,3... | collective-permute-start | bytes 442376 | tf_op jit(solution)/shard_map/ppermute | solution.py:12
  53.1 1.9 collective-permute-start.6
  56.0 4.3 %collective-permute-start.5 = (bf16[256,288]{0,1:T(8,128)(2,1)S(1)}, bf16[256,288]{0,1:T(8,128)(2,1)S(1)}, u32[]{:S(2)}, u32[]{:S(2)}) collective-permute-start(bf16[256,288]{0,1:T(8,128)(2,1)S(1)} %copy-done.3), channel_id=1, source_target_pairs={{12,0},{16,4},{20,8},{24,12},{28,16},{32,20},{36,24},{40,28},{44,3... | collective-permute-start | bytes 442376 | tf_op jit(solution)/shard_map/ppermute | solution.py:12
  61.4 1.9 collective-permute-start.4
  64.3 11.7 %collective-permute-start.3 = (bf16[256,288]{0,1:T(8,128)(2,1)S(1)}, bf16[256,288]{0,1:T(8,128)(2,1)S(1)}, u32[]{:S(2)}, u32[]{:S(2)}) collective-permute-start(bf16[256,288]{0,1:T(8,128)(2,1)S(1)} %copy-done.3), channel_id=1, source_target_pairs={{8,0},{12,4},{16,8},{20,12},{24,16},{28,20},{32,24},{36,28},{40,32... | collective-permute-start | bytes 442376 | tf_op jit(solution)/shard_map/ppermute | solution.py:12
  76.9 1.9 collective-permute-start.2
  79.9 1.9 collective-permute-start
  82.8 7.8 %collective-permute-start.1 = (bf16[256,288]{0,1:T(8,128)(2,1)S(1)}, bf16[256,288]{0,1:T(8,128)(2,1)S(1)}, u32[]{:S(2)}, u32[]{:S(2)}) collective-permute-start(bf16[256,288]{0,1:T(8,128)(2,1)S(1)} %copy-done.3), channel_id=1, source_target_pairs={{4,0},{8,4},{12,8},{16,12},{20,16},{24,20},{28,24},{32,28},{36,32}... | collective-permute-start | bytes 442376 | tf_op jit(solution)/shard_map/ppermute | solution.py:12
  97.8 163.2 %all-reduce.3.cloned.1.call-done = (f32[256,256]{1,0:T(8,128)}, f32[256,256]{1,0:T(8,128)}, f32[256,256]{1,0:T(8,128)}, f32[256,256]{1,0:T(8,128)}, f32[256,256]...) async-done(((f32[256,256]{1,0:T(8,128)}, ...) | async-done | bytes 3932176 | tf_op jit(solution)/shard_map/psum | solution.py:41
  261.0 1.2 fusion.51
  262.2 1.9 collective-permute-start.27
  264.4 5.7 %collective-permute-start.26 = (f32[256,288]{0,1:T(8,128)S(1)}, f32[256,288]{0,1:T(8,128)S(1)}, u32[]{:S(2)}, u32[]{:S(2)}) collective-permute-start(f32[256,288]{0,1:T(8,128)S(1)} %fusion.49), channel_id=1, source_target_pairs={{28,0},{32,4},{36,8},{40,12},{44,16},{48,20},{52,24},{56,28},{60,3... | collective-permute-start | bytes 884744 | tf_op jit(solution)/shard_map/ppermute | solution.py:12
  270.4 4.4 %collective-permute-start.25 = (f32[256,288]{0,1:T(8,128)S(1)}, f32[256,288]{0,1:T(8,128)S(1)}, u32[]{:S(2)}, u32[]{:S(2)}) collective-permute-start(f32[256,288]{0,1:T(8,128)S(1)} %fusion.47), channel_id=1, source_target_pairs={{488,0},{492,4},{496,8},{500,12},{504,16},{508,20},{0,24},{4,28},{... | collective-permute-start | bytes 884744 | tf_op jit(solution)/shard_map/ppermute | solution.py:12
  275.0 4.5 %collective-permute-start.24 = (f32[256,288]{0,1:T(8,128)S(1)}, f32[256,288]{0,1:T(8,128)S(1)}, u32[]{:S(2)}, u32[]{:S(2)}) collective-permute-start(f32[256,288]{0,1:T(8,128)S(1)} %fusion.45), channel_id=1, source_target_pairs={{24,0},{28,4},{32,8},{36,12},{40,16},{44,20},{48,24},{52,28},{56,3... | collective-permute-start | bytes 884744 | tf_op jit(solution)/shard_map/ppermute | solution.py:12
  279.8 4.8 %collective-permute-start.23 = (f32[256,288]{0,1:T(8,128)S(1)}, f32[256,288]{0,1:T(8,128)S(1)}, u32[]{:S(2)}, u32[]{:S(2)}) collective-permute-start(f32[256,288]{0,1:T(8,128)S(1)} %fusion.43), channel_id=1, source_target_pairs={{492,0},{496,4},{500,8},{504,12},{508,16},{0,20},{4,24},{8,28},{12... | collective-permute-start | bytes 884744 | tf_op jit(solution)/shard_map/ppermute | solution.py:12
  296.9 3.8 %collective-permute-start.22 = (f32[256,288]{0,1:T(8,128)S(1)}, f32[256,288]{0,1:T(8,128)S(1)}, u32[]{:S(2)}, u32[]{:S(2)}) collective-permute-start(f32[256,288]{0,1:T(8,128)S(1)} %fusion.41), channel_id=1, source_target_pairs={{20,0},{24,4},{28,8},{32,12},{36,16},{40,20},{44,24},{48,28},{52,3... | collective-permute-start | bytes 884744 | tf_op jit(solution)/shard_map/ppermute | solution.py:12
  300.7 4.7 %collective-permute-start.21 = (f32[256,288]{0,1:T(8,128)S(1)}, f32[256,288]{0,1:T(8,128)S(1)}, u32[]{:S(2)}, u32[]{:S(2)}) collective-permute-start(f32[256,288]{0,1:T(8,128)S(1)} %fusion.39), channel_id=1, source_target_pairs={{496,0},{500,4},{504,8},{508,12},{0,16},{4,20},{8,24},{12,28},{16,... | collective-permute-start | bytes 884744 | tf_op jit(solution)/shard_map/ppermute | solution.py:12
  305.4 5.7 %collective-permute-start.20 = (f32[256,288]{0,1:T(8,128)S(1)}, f32[256,288]{0,1:T(8,128)S(1)}, u32[]{:S(2)}, u32[]{:S(2)}) collective-permute-start(f32[256,288]{0,1:T(8,128)S(1)} %fusion.37), channel_id=1, source_target_pairs={{16,0},{20,4},{24,8},{28,12},{32,16},{36,20},{40,24},{44,28},{48,3... | collective-permute-start | bytes 884744 | tf_op jit(solution)/shard_map/ppermute | solution.py:12
  311.1 4.5 %collective-permute-start.19 = (f32[256,288]{0,1:T(8,128)S(1)}, f32[256,288]{0,1:T(8,128)S(1)}, u32[]{:S(2)}, u32[]{:S(2)}) collective-permute-start(f32[256,288]{0,1:T(8,128)S(1)} %fusion.35), channel_id=1, source_target_pairs={{500,0},{504,4},{508,8},{0,12},{4,16},{8,20},{12,24},{16,28},{20,3... | collective-permute-start | bytes 884744 | tf_op jit(solution)/shard_map/ppermute | solution.py:12
  316.1 5.6 %collective-permute-start.18 = (f32[256,288]{0,1:T(8,128)S(1)}, f32[256,288]{0,1:T(8,128)S(1)}, u32[]{:S(2)}, u32[]{:S(2)}) collective-permute-start(f32[256,288]{0,1:T(8,128)S(1)} %fusion.33), channel_id=1, source_target_pairs={{12,0},{16,4},{20,8},{24,12},{28,16},{32,20},{36,24},{40,28},{44,3... | collective-permute-start | bytes 884744 | tf_op jit(solution)/shard_map/ppermute | solution.py:12
  321.7 3.1 collective-permute-start.17
  324.8 7.0 %collective-permute-start.16 = (f32[256,288]{0,1:T(8,128)S(1)}, f32[256,288]{0,1:T(8,128)S(1)}, u32[]{:S(2)}, u32[]{:S(2)}) collective-permute-start(f32[256,288]{0,1:T(8,128)S(1)} %fusion.29), channel_id=1, source_target_pairs={{8,0},{12,4},{16,8},{20,12},{24,16},{28,20},{32,24},{36,28},{40,32... | collective-permute-start | bytes 884744 | tf_op jit(solution)/shard_map/ppermute | solution.py:12
  331.8 2.5 collective-permute-start.15
  334.4 9.3 %collective-permute-start.14 = (f32[256,288]{0,1:T(8,128)S(1)}, f32[256,288]{0,1:T(8,128)S(1)}, u32[]{:S(2)}, u32[]{:S(2)}) collective-permute-start(f32[256,288]{0,1:T(8,128)S(1)} %fusion.28), channel_id=1, source_target_pairs={{4,0},{8,4},{12,8},{16,12},{20,16},{24,20},{28,24},{32,28},{36,32}... | collective-permute-start | bytes 884744 | tf_op jit(solution)/shard_map/ppermute | solution.py:12
  344.8 3.1 collective-permute-done.14
  (108 shorter events, 29.6 us)
Async XLA Ops:
  7.2 28.5 %copy-start = (bf16[256,288]{0,1:T(8,128)(2,1)S(1)}, bf16[256,288]{0,1:T(8,128)(2,1)}, u32[]{:S(2)}) copy-start(bf16[256,288]{0,1:T(8,128)(2,1)} %param.5) | copy-start | bytes 442372
  7.2 30.4 %copy-start.3 = (bf16[256,288]{0,1:T(8,128)(2,1)S(1)}, bf16[256,288]{0,1:T(8,128)(2,1)}, u32[]{:S(2)}) copy-start(bf16[256,288]{0,1:T(8,128)(2,1)} %param.6) | copy-start | bytes 442372
  7.2 253.8 %all-reduce.3.cloned.1.call-start = ((), (), s32[]{:S(2)}) async-start(), calls=%async_computation | async-start | bytes 7864320 | tf_op jit(solution)/shard_map/psum | solution.py:41
  7.2 30.3 %collective-permute-start.13 = (bf16[256,288]{0,1:T(8,128)(2,1)}, bf16[256,288]{0,1:T(8,128)(2,1)S(1)}, u32[]{:S(2)}, u32[]{:S(2)}) collective-permute-start(bf16[256,288]{0,1:T(8,128)(2,1)} %param.6), channel_id=1, source_target_pairs={{28,0},{32,4},{36,8},{40,12},{44,16},{48,20},{52,24},{56,28},{60,3... | collective-permute-start | bytes 442376 | tf_op jit(solution)/shard_map/ppermute | solution.py:12
  18.8 21.9 %collective-permute-start.12 = (bf16[256,288]{0,1:T(8,128)(2,1)}, bf16[256,288]{0,1:T(8,128)(2,1)S(1)}, u32[]{:S(2)}, u32[]{:S(2)}) collective-permute-start(bf16[256,288]{0,1:T(8,128)(2,1)} %param.6), channel_id=1, source_target_pairs={{484,0},{488,4},{492,8},{496,12},{500,16},{504,20},{508,24},{0,28}... | collective-permute-start | bytes 442376 | tf_op jit(solution)/shard_map/ppermute | solution.py:12
  20.7 32.4 %collective-permute-start.11 = (bf16[256,288]{0,1:T(8,128)(2,1)}, bf16[256,288]{0,1:T(8,128)(2,1)S(1)}, u32[]{:S(2)}, u32[]{:S(2)}) collective-permute-start(bf16[256,288]{0,1:T(8,128)(2,1)} %param.6), channel_id=1, source_target_pairs={{24,0},{28,4},{32,8},{36,12},{40,16},{44,20},{48,24},{52,28},{56,3... | collective-permute-start | bytes 442376 | tf_op jit(solution)/shard_map/ppermute | solution.py:12
  28.8 27.2 %collective-permute-start.10 = (bf16[256,288]{0,1:T(8,128)(2,1)}, bf16[256,288]{0,1:T(8,128)(2,1)S(1)}, u32[]{:S(2)}, u32[]{:S(2)}) collective-permute-start(bf16[256,288]{0,1:T(8,128)(2,1)} %param.6), channel_id=1, source_target_pairs={{488,0},{492,4},{496,8},{500,12},{504,16},{508,20},{0,24},{4,28},{... | collective-permute-start | bytes 442376 | tf_op jit(solution)/shard_map/ppermute | solution.py:12
  30.8 30.6 %collective-permute-start.9 = (bf16[256,288]{0,1:T(8,128)(2,1)}, bf16[256,288]{0,1:T(8,128)(2,1)S(1)}, u32[]{:S(2)}, u32[]{:S(2)}) collective-permute-start(bf16[256,288]{0,1:T(8,128)(2,1)} %param.6), channel_id=1, source_target_pairs={{20,0},{24,4},{28,8},{32,12},{36,16},{40,20},{44,24},{48,28},{52,3... | collective-permute-start | bytes 442376 | tf_op jit(solution)/shard_map/ppermute | solution.py:12
  37.6 26.7 %collective-permute-start.8 = (bf16[256,288]{0,1:T(8,128)(2,1)S(1)}, bf16[256,288]{0,1:T(8,128)(2,1)S(1)}, u32[]{:S(2)}, u32[]{:S(2)}) collective-permute-start(bf16[256,288]{0,1:T(8,128)(2,1)S(1)} %copy-done.3), channel_id=1, source_target_pairs={{492,0},{496,4},{500,8},{504,12},{508,16},{0,20},{4,24},{8,28},{12... | collective-permute-start | bytes 442376 | tf_op jit(solution)/shard_map/ppermute | solution.py:12
  40.7 36.2 %collective-permute-start.7 = (bf16[256,288]{0,1:T(8,128)(2,1)S(1)}, bf16[256,288]{0,1:T(8,128)(2,1)S(1)}, u32[]{:S(2)}, u32[]{:S(2)}) collective-permute-start(bf16[256,288]{0,1:T(8,128)(2,1)S(1)} %copy-done.3), channel_id=1, source_target_pairs={{16,0},{20,4},{24,8},{28,12},{32,16},{36,20},{40,24},{44,28},{48,3... | collective-permute-start | bytes 442376 | tf_op jit(solution)/shard_map/ppermute | solution.py:12
  53.1 26.7 %collective-permute-start.6 = (bf16[256,288]{0,1:T(8,128)(2,1)S(1)}, bf16[256,288]{0,1:T(8,128)(2,1)S(1)}, u32[]{:S(2)}, u32[]{:S(2)}) collective-permute-start(bf16[256,288]{0,1:T(8,128)(2,1)S(1)} %copy-done.3), channel_id=1, source_target_pairs={{496,0},{500,4},{504,8},{508,12},{0,16},{4,20},{8,24},{12,28},{16,... | collective-permute-start | bytes 442376 | tf_op jit(solution)/shard_map/ppermute | solution.py:12
  56.0 26.7 %collective-permute-start.5 = (bf16[256,288]{0,1:T(8,128)(2,1)S(1)}, bf16[256,288]{0,1:T(8,128)(2,1)S(1)}, u32[]{:S(2)}, u32[]{:S(2)}) collective-permute-start(bf16[256,288]{0,1:T(8,128)(2,1)S(1)} %copy-done.3), channel_id=1, source_target_pairs={{12,0},{16,4},{20,8},{24,12},{28,16},{32,20},{36,24},{40,28},{44,3... | collective-permute-start | bytes 442376 | tf_op jit(solution)/shard_map/ppermute | solution.py:12
  61.4 30.2 %collective-permute-start.4 = (bf16[256,288]{0,1:T(8,128)(2,1)S(1)}, bf16[256,288]{0,1:T(8,128)(2,1)S(1)}, u32[]{:S(2)}, u32[]{:S(2)}) collective-permute-start(bf16[256,288]{0,1:T(8,128)(2,1)S(1)} %copy-done.3), channel_id=1, source_target_pairs={{500,0},{504,4},{508,8},{0,12},{4,16},{8,20},{12,24},{16,28},{20,3... | collective-permute-start | bytes 442376 | tf_op jit(solution)/shard_map/ppermute | solution.py:12
  64.3 28.3 %collective-permute-start.3 = (bf16[256,288]{0,1:T(8,128)(2,1)S(1)}, bf16[256,288]{0,1:T(8,128)(2,1)S(1)}, u32[]{:S(2)}, u32[]{:S(2)}) collective-permute-start(bf16[256,288]{0,1:T(8,128)(2,1)S(1)} %copy-done.3), channel_id=1, source_target_pairs={{8,0},{12,4},{16,8},{20,12},{24,16},{28,20},{32,24},{36,28},{40,32... | collective-permute-start | bytes 442376 | tf_op jit(solution)/shard_map/ppermute | solution.py:12
  76.9 16.6 %collective-permute-start.2 = (bf16[256,288]{0,1:T(8,128)(2,1)S(1)}, bf16[256,288]{0,1:T(8,128)(2,1)S(1)}, u32[]{:S(2)}, u32[]{:S(2)}) collective-permute-start(bf16[256,288]{0,1:T(8,128)(2,1)S(1)} %copy-done.3), channel_id=1, source_target_pairs={{504,0},{508,4},{0,8},{4,12},{8,16},{12,20},{16,24},{20,28},{24,32... | collective-permute-start | bytes 442376 | tf_op jit(solution)/shard_map/ppermute | solution.py:12
  79.9 14.7 %collective-permute-start = (bf16[256,288]{0,1:T(8,128)(2,1)S(1)}, bf16[256,288]{0,1:T(8,128)(2,1)S(1)}, u32[]{:S(2)}, u32[]{:S(2)}) collective-permute-start(bf16[256,288]{0,1:T(8,128)(2,1)S(1)} %copy-done.3), channel_id=1, source_target_pairs={{508,0},{0,4},{4,8},{8,12},{12,16},{16,20},{20,24},{24,28},{28,32}... | collective-permute-start | bytes 442376 | tf_op jit(solution)/shard_map/ppermute | solution.py:12
  82.8 12.7 %collective-permute-start.1 = (bf16[256,288]{0,1:T(8,128)(2,1)S(1)}, bf16[256,288]{0,1:T(8,128)(2,1)S(1)}, u32[]{:S(2)}, u32[]{:S(2)}) collective-permute-start(bf16[256,288]{0,1:T(8,128)(2,1)S(1)} %copy-done.3), channel_id=1, source_target_pairs={{4,0},{8,4},{12,8},{16,12},{20,16},{24,20},{28,24},{32,28},{36,32}... | collective-permute-start | bytes 442376 | tf_op jit(solution)/shard_map/ppermute | solution.py:12
  262.2 34.7 %collective-permute-start.27 = (f32[256,288]{0,1:T(8,128)S(1)}, f32[256,288]{0,1:T(8,128)S(1)}, u32[]{:S(2)}, u32[]{:S(2)}) collective-permute-start(f32[256,288]{0,1:T(8,128)S(1)} %fusion.51), channel_id=1, source_target_pairs={{484,0},{488,4},{492,8},{496,12},{500,16},{504,20},{508,24},{0,28}... | collective-permute-start | bytes 884744 | tf_op jit(solution)/shard_map/ppermute | solution.py:12
  264.1 6.0 %copy-start.15 = (f32[256,256]{1,0:T(8,128)S(1)}, f32[256,256]{1,0:T(8,128)}, u32[]{:S(2)}) copy-start(f32[256,256]{1,0:T(8,128)} %get-tuple-element.4) | copy-start | bytes 786436
  264.4 36.3 %collective-permute-start.26 = (f32[256,288]{0,1:T(8,128)S(1)}, f32[256,288]{0,1:T(8,128)S(1)}, u32[]{:S(2)}, u32[]{:S(2)}) collective-permute-start(f32[256,288]{0,1:T(8,128)S(1)} %fusion.49), channel_id=1, source_target_pairs={{28,0},{32,4},{36,8},{40,12},{44,16},{48,20},{52,24},{56,28},{60,3... | collective-permute-start | bytes 884744 | tf_op jit(solution)/shard_map/ppermute | solution.py:12
  270.4 35.0 %collective-permute-start.25 = (f32[256,288]{0,1:T(8,128)S(1)}, f32[256,288]{0,1:T(8,128)S(1)}, u32[]{:S(2)}, u32[]{:S(2)}) collective-permute-start(f32[256,288]{0,1:T(8,128)S(1)} %fusion.47), channel_id=1, source_target_pairs={{488,0},{492,4},{496,8},{500,12},{504,16},{508,20},{0,24},{4,28},{... | collective-permute-start | bytes 884744 | tf_op jit(solution)/shard_map/ppermute | solution.py:12
  275.0 36.1 %collective-permute-start.24 = (f32[256,288]{0,1:T(8,128)S(1)}, f32[256,288]{0,1:T(8,128)S(1)}, u32[]{:S(2)}, u32[]{:S(2)}) collective-permute-start(f32[256,288]{0,1:T(8,128)S(1)} %fusion.45), channel_id=1, source_target_pairs={{24,0},{28,4},{32,8},{36,12},{40,16},{44,20},{48,24},{52,28},{56,3... | collective-permute-start | bytes 884744 | tf_op jit(solution)/shard_map/ppermute | solution.py:12
  279.8 36.3 %collective-permute-start.23 = (f32[256,288]{0,1:T(8,128)S(1)}, f32[256,288]{0,1:T(8,128)S(1)}, u32[]{:S(2)}, u32[]{:S(2)}) collective-permute-start(f32[256,288]{0,1:T(8,128)S(1)} %fusion.43), channel_id=1, source_target_pairs={{492,0},{496,4},{500,8},{504,12},{508,16},{0,20},{4,24},{8,28},{12... | collective-permute-start | bytes 884744 | tf_op jit(solution)/shard_map/ppermute | solution.py:12
  296.9 24.8 %collective-permute-start.22 = (f32[256,288]{0,1:T(8,128)S(1)}, f32[256,288]{0,1:T(8,128)S(1)}, u32[]{:S(2)}, u32[]{:S(2)}) collective-permute-start(f32[256,288]{0,1:T(8,128)S(1)} %fusion.41), channel_id=1, source_target_pairs={{20,0},{24,4},{28,8},{32,12},{36,16},{40,20},{44,24},{48,28},{52,3... | collective-permute-start | bytes 884744 | tf_op jit(solution)/shard_map/ppermute | solution.py:12
  300.7 24.1 %collective-permute-start.21 = (f32[256,288]{0,1:T(8,128)S(1)}, f32[256,288]{0,1:T(8,128)S(1)}, u32[]{:S(2)}, u32[]{:S(2)}) collective-permute-start(f32[256,288]{0,1:T(8,128)S(1)} %fusion.39), channel_id=1, source_target_pairs={{496,0},{500,4},{504,8},{508,12},{0,16},{4,20},{8,24},{12,28},{16,... | collective-permute-start | bytes 884744 | tf_op jit(solution)/shard_map/ppermute | solution.py:12
  305.4 26.4 %collective-permute-start.20 = (f32[256,288]{0,1:T(8,128)S(1)}, f32[256,288]{0,1:T(8,128)S(1)}, u32[]{:S(2)}, u32[]{:S(2)}) collective-permute-start(f32[256,288]{0,1:T(8,128)S(1)} %fusion.37), channel_id=1, source_target_pairs={{16,0},{20,4},{24,8},{28,12},{32,16},{36,20},{40,24},{44,28},{48,3... | collective-permute-start | bytes 884744 | tf_op jit(solution)/shard_map/ppermute | solution.py:12
  311.1 23.2 %collective-permute-start.19 = (f32[256,288]{0,1:T(8,128)S(1)}, f32[256,288]{0,1:T(8,128)S(1)}, u32[]{:S(2)}, u32[]{:S(2)}) collective-permute-start(f32[256,288]{0,1:T(8,128)S(1)} %fusion.35), channel_id=1, source_target_pairs={{500,0},{504,4},{508,8},{0,12},{4,16},{8,20},{12,24},{16,28},{20,3... | collective-permute-start | bytes 884744 | tf_op jit(solution)/shard_map/ppermute | solution.py:12
  316.1 28.7 %collective-permute-start.18 = (f32[256,288]{0,1:T(8,128)S(1)}, f32[256,288]{0,1:T(8,128)S(1)}, u32[]{:S(2)}, u32[]{:S(2)}) collective-permute-start(f32[256,288]{0,1:T(8,128)S(1)} %fusion.33), channel_id=1, source_target_pairs={{12,0},{16,4},{20,8},{24,12},{28,16},{32,20},{36,24},{40,28},{44,3... | collective-permute-start | bytes 884744 | tf_op jit(solution)/shard_map/ppermute | solution.py:12
  321.7 23.1 %collective-permute-start.17 = (f32[256,288]{0,1:T(8,128)S(1)}, f32[256,288]{0,1:T(8,128)S(1)}, u32[]{:S(2)}, u32[]{:S(2)}) collective-permute-start(f32[256,288]{0,1:T(8,128)S(1)} %fusion.31), channel_id=1, source_target_pairs={{504,0},{508,4},{0,8},{4,12},{8,16},{12,20},{16,24},{20,28},{24,32... | collective-permute-start | bytes 884744 | tf_op jit(solution)/shard_map/ppermute | solution.py:12
  324.8 20.0 %collective-permute-start.16 = (f32[256,288]{0,1:T(8,128)S(1)}, f32[256,288]{0,1:T(8,128)S(1)}, u32[]{:S(2)}, u32[]{:S(2)}) collective-permute-start(f32[256,288]{0,1:T(8,128)S(1)} %fusion.29), channel_id=1, source_target_pairs={{8,0},{12,4},{16,8},{20,12},{24,16},{28,20},{32,24},{36,28},{40,32... | collective-permute-start | bytes 884744 | tf_op jit(solution)/shard_map/ppermute | solution.py:12
  331.8 13.0 %collective-permute-start.15 = (f32[256,288]{0,1:T(8,128)S(1)}, f32[256,288]{0,1:T(8,128)S(1)}, u32[]{:S(2)}, u32[]{:S(2)}) collective-permute-start(f32[256,288]{0,1:T(8,128)S(1)} %fusion.27), channel_id=1, source_target_pairs={{508,0},{0,4},{4,8},{8,12},{12,16},{16,20},{20,24},{24,28},{28,32}... | collective-permute-start | bytes 884744 | tf_op jit(solution)/shard_map/ppermute | solution.py:12
  334.4 13.5 %collective-permute-start.14 = (f32[256,288]{0,1:T(8,128)S(1)}, f32[256,288]{0,1:T(8,128)S(1)}, u32[]{:S(2)}, u32[]{:S(2)}) collective-permute-start(f32[256,288]{0,1:T(8,128)S(1)} %fusion.28), channel_id=1, source_target_pairs={{4,0},{8,4},{12,8},{16,12},{20,16},{24,20},{28,24},{32,28},{36,32}... | collective-permute-start | bytes 884744 | tf_op jit(solution)/shard_map/ppermute | solution.py:12
  (15 other events, 27.7 us)
Sparse Core Ops, SparseCore 0:
  96.6 164.3 all-reduce.2
where the time goes:
time: 357 us; the launch traced here: 356 us
  waiting for transfers between devices  166 us (46%)
  starting transfers between devices  141 us (39%)
  matrix products  25.4 us (7%)
  between operations  16 us (4%)
  local copies, waits for them, and re-layouts  7.14 us (2%)
    psum x1, waiting for transfers between devices, finish(): totals = lax.psum(parts, 'width')  163 us
    ppermute x28, starting transfers between devices, shifted(): return lax.ppermute(block, axis, route)  141 us
    dot_general x15, matrix products, cross_rows(): lax.dot_general(left, right, (((1,), (1,)), ((), ())), preferred_element_...  15.5 us
  transfers between devices with their start and end apart: 29, of which 2 were waited for; matrix products, arithmetic and copies ran while one was open for 6% of the time, Pallas kernels for 0%

commit v1 on v0

v1 whole, which is shorter than its diff:
```python
import jax
import jax.numpy as jnp
from jax import lax
from jax.sharding import Mesh, PartitionSpec as P

CORES = 2
WIDTH = 4
NEAR = 3


def from_chip(block, distance):
    chips = lax.axis_size("chip")
    route = [((i + distance) % chips, i) for i in range(chips)]
    return lax.ppermute(block, "chip", route)


def from_far_chip(block):
    chips = lax.axis_size("chip")
    route = []
    for i in range(chips):
        for w in range(WIDTH):
            source = (i + (NEAR + 1 if w < WIDTH // 2 else -NEAR - 1)) % chips
            route.append((source * WIDTH + w, i * WIDTH + w))
    return lax.ppermute(block, ("chip", "width"), route)


def swap_cores(block):
    return lax.ppermute(block, "core", [(0, 1), (1, 0)])


def from_width(block, distance):
    route = [((i + distance) % WIDTH, i) for i in range(WIDTH)]
    return lax.ppermute(block, "width", route)


def gather_width(block):
    rows = block.shape[0]
    w = lax.axis_index("width")
    parts = [block] + [from_width(block, d) for d in (1, -1, 2)]
    order = [0, 1, 3, 2]
    return parts


def per_device(images, texts, matches, scale, shift_bias):
    temper = scale[0]
    offset_bias = shift_bias[0]
    first = lax.axis_index("core") == 0
    w = lax.axis_index("width")
    features, rows = images.shape[1], images.shape[0]
    quarter = CORES * rows // WIDTH

    image, text = images.T, texts.T
    marks = jnp.pad(matches.astype(jnp.bfloat16), ((0, 15), (0, rows)))
    mine = jnp.concatenate([jnp.concatenate([image, text], 1), marks], 0)
    other = swap_cores(mine)
    other_image, other_text = other[:features, :rows], other[:features, rows:]
    other_matches = other[features : features + 1, :rows].astype(jnp.int32)

    part0 = jnp.where(first, image, other_text)
    part1 = jnp.where(first, other_image, text)
    full = jnp.concatenate(
        [jnp.where(first, text, other_image), jnp.where(first, other_text, image)], 1
    )
    chunks = jnp.stack(
        [part0[:, :quarter], part0[:, quarter:], part1[:, :quarter], part1[:, quarter:]]
    )
    own = lax.all_to_all(chunks, "width", 0, 0).reshape(WIDTH * features, quarter)

    pieces = [own]
    for step in range(1, NEAR + 1):
        pieces += [from_chip(own, step), from_chip(own, -step)]
    pieces.append(from_far_chip(own))
    held = lax.all_gather(full, "width", axis=0, tiled=True)

    both = jnp.concatenate(
        [jnp.where(first, matches, other_matches), jnp.where(first, other_matches, matches)], 1
    )
    lane = lax.broadcasted_iota(jnp.int32, (1, CORES * rows), 1)
    sub = lax.broadcasted_iota(jnp.int32, (quarter, 1), 0)
    block_of = w // CORES
    goal = jnp.where(first, lane % rows, both)
    goal = jnp.where(lane // rows == block_of, goal, -1)
    mark = lax.dynamic_slice(both, (0, w * quarter), (1, quarter)).reshape(quarter, 1)
    have = jnp.where(first, mark, sub + (w % CORES) * quarter)
    label = (goal == have).astype(jnp.float32)
    kept = (lane // rows != block_of).astype(jnp.float32)

    table = jnp.concatenate(pieces, 1)
    logits = lax.dot_general(
        table, held, (((0,), (0,)), ((), ())), preferred_element_type=jnp.float32
    )
    probs = jax.nn.sigmoid(temper * logits + offset_bias)
    n = table.shape[1]
    probs = jnp.concatenate(
        [probs[:quarter] - label, probs[quarter : n - quarter], probs[n - quarter :] * kept], 0
    )
    weights = probs.astype(jnp.bfloat16)
    partial = jnp.dot(table, weights, preferred_element_type=jnp.float32).astype(jnp.bfloat16)
    partial = partial.reshape(WIDTH, features, CORES, rows).transpose(2, 0, 1, 3)
    partial = partial.reshape(CORES * WIDTH, features, rows)
    terms = lax.all_to_all(partial, ("core", "width"), 0, 0).astype(jnp.float32)
    grad_text = terms[0] + terms[1] + terms[2] + terms[3]
    grad_image = terms[4] + terms[5] + terms[6] + terms[7]
    return (temper * grad_image).T, (temper * grad_text).T


def solution(mesh):
    chips = mesh.shape["tour"] // CORES
    fine = Mesh(mesh.devices.reshape(chips, CORES, WIDTH), ("chip", "core", "width"))
    rows, split = ("chip", "core"), "width"
    return jax.shard_map(
        per_device,
        mesh=fine,
        in_specs=(P(rows, split), P(rows, split), P(rows, None), P(), P()),
        out_specs=(P(rows, split), P(rows, split)),
        check_vma=False,
    )
```

time: 357 us -> 147 us (0.41)
  the two profiles are of different devices: /device:TPU:16 before, /device:TPU:3 now
where the time goes in v1:
time: 147 us; the launch traced here: 146 us
  starting transfers between devices  43.1 us (29%)
  blocking collectives  37.6 us (26%)
  waiting for transfers between devices  35.6 us (24%)
  between operations  15.6 us (11%)
  matrix products  6.99 us (5%)
  other arithmetic  5.59 us (4%)
    all_to_all x1, blocking collectives, per_device(): terms = lax.all_to_all(partial, ('core', 'width'), 0, 0).astype(jnp.float32)  37.6 us
    ppermute x6, starting transfers between devices, from_chip(): return lax.ppermute(block, 'chip', route)  29.4 us
    ppermute x6, waiting for transfers between devices, from_chip(): return lax.ppermute(block, 'chip', route)  23.6 us
    all_to_all x1, waiting for transfers between devices, per_device(): lax.all_to_all(chunks, 'width', 0, 0).reshape(WIDTH * features, quarter)  9.14 us
    all_to_all x1, starting transfers between devices, per_device(): lax.all_to_all(chunks, 'width', 0, 0).reshape(WIDTH * features, quarter)  6.81 us
    ppermute x1, starting transfers between devices, from_far_chip(): return lax.ppermute(block, ('chip', 'width'), route)  4.3 us
    dot_general x1, matrix products, per_device(): lax.dot_general(table, held, (((0,), (0,)), ((), ())), preferred_element_...  3.94 us
    dot_general x1, matrix products, per_device(): jnp.dot(table, weights, preferred_element_type=jnp.float32)  3.05 us
  transfers between devices with their start and end apart: 10, of which 5 were waited for; matrix products, arithmetic and copies ran while one was open for 1% of the time, Pallas kernels for 0%

profile of v1, /device:TPU:3, one launch (start us, length us, event | category | flops | bytes accessed | tf_op | source)
XLA Modules:
  0.0 145.9 jit_solution(16358816280381245504)
XLA Ops:
  7.2 0.7 convert_element_type.26
  7.9 1.0 fusion.6
  8.9 2.6 %collective-permute-start = (bf16[304,512]{1,0:T(8,128)(2,1)S(1)}, bf16[304,512]{1,0:T(8,128)(2,1)S(1)}, u32[]{:S(2)}, u32[]{:S(2)}) collective-permute-start(bf16[304,512]{1,0:T(8,128)(2,1)S(1)} %fusion.6), channel_id=1, source_target_pairs={{0,4},{4,0},{1,5},{5,1},{2,6},{6,2},{3,7},{7,3},{8,12},{12,8},{9,1... | collective-permute-start | bytes 933896 | tf_op jit(solution)/shard_map/ppermute | solution.py:28
  12.9 1.0 broadcast_select_fusion.1
  14.0 0.8 pad_maximum_fusion
  14.7 6.8 %all-to-all-start = ((bf16[4,288,128]{2,1,0:T(8,128)(2,1)}), bf16[4,288,128]{2,1,0:T(8,128)(2,1)S(1)}, u32[]{:S(2)}, u32[]{:S(2)}) async-start(bf16[4,288,128]{2,1,0:T(8,128)(2,1)} %pad_maximum_fusion), calls=%async_computation | async-start | bytes 589824 | tf_op jit(solution)/shard_map/all_to_all | solution.py:67
  21.5 0.7 pad_maximum_fusion.1
  22.3 9.1 %all-to-all-done = bf16[4,288,128]{2,1,0:T(8,128)(2,1)S(1)} async-done(((bf16[4,288,128]{2,1,0:T(8,128)(2,1)}), bf16[4,288,128]{2,1,0:T(8,128)(2,1)S(1)}, u32[]{:S(2)}, u32[]{:S(2)}) %all-to-all-start) | async-done | bytes 294944 | tf_op jit(solution)/shard_map/all_to_all | solution.py:67
  31.5 4.9 %collective-permute-start.1 = (bf16[1152,128]{1,0:T(8,128)(2,1)S(1)}, bf16[1152,128]{1,0:T(8,128)(2,1)S(1)}, u32[]{:S(2)}, u32[]{:S(2)}) collective-permute-start(bf16[1152,128]{1,0:T(8,128)(2,1)S(1)} %bitcast.39), channel_id=1, source_target_pairs={{8,0},{16,8},{24,16},{32,24},{40,32},{48,40},{56,48},{64,56},{72,6... | collective-permute-start | bytes 884744 | tf_op jit(solution)/shard_map/ppermute | solution.py:14
  36.4 1.9 %collective-permute-start.2 = (bf16[1152,128]{1,0:T(8,128)(2,1)S(1)}, bf16[1152,128]{1,0:T(8,128)(2,1)S(1)}, u32[]{:S(2)}, u32[]{:S(2)}) collective-permute-start(bf16[1152,128]{1,0:T(8,128)(2,1)S(1)} %bitcast.40), channel_id=1, source_target_pairs={{504,0},{0,8},{8,16},{16,24},{24,32},{32,40},{40,48},{48,56},{56,6... | collective-permute-start | bytes 884744 | tf_op jit(solution)/shard_map/ppermute | solution.py:14
  38.5 14.4 %collective-permute-start.3 = (bf16[1152,128]{1,0:T(8,128)(2,1)S(1)}, bf16[1152,128]{1,0:T(8,128)(2,1)S(1)}, u32[]{:S(2)}, u32[]{:S(2)}) collective-permute-start(bf16[1152,128]{1,0:T(8,128)(2,1)S(1)} %bitcast.42), channel_id=1, source_target_pairs={{16,0},{24,8},{32,16},{40,24},{48,32},{56,40},{64,48},{72,56},{80,... | collective-permute-start | bytes 884744 | tf_op jit(solution)/shard_map/ppermute | solution.py:14
  52.9 1.9 %collective-permute-start.4 = (bf16[1152,128]{1,0:T(8,128)(2,1)S(1)}, bf16[1152,128]{1,0:T(8,128)(2,1)S(1)}, u32[]{:S(2)}, u32[]{:S(2)}) collective-permute-start(bf16[1152,128]{1,0:T(8,128)(2,1)S(1)} %bitcast.43), channel_id=1, source_target_pairs={{496,0},{504,8},{0,16},{8,24},{16,32},{24,40},{32,48},{40,56},{48,... | collective-permute-start | bytes 884744 | tf_op jit(solution)/shard_map/ppermute | solution.py:14
  54.8 3.0 %collective-permute-start.5 = (bf16[1152,128]{1,0:T(8,128)(2,1)S(1)}, bf16[1152,128]{1,0:T(8,128)(2,1)S(1)}, u32[]{:S(2)}, u32[]{:S(2)}) collective-permute-start(bf16[1152,128]{1,0:T(8,128)(2,1)S(1)} %bitcast.44), channel_id=1, source_target_pairs={{24,0},{32,8},{40,16},{48,24},{56,32},{64,40},{72,48},{80,56},{88,... | collective-permute-start | bytes 884744 | tf_op jit(solution)/shard_map/ppermute | solution.py:14
  57.8 3.2 %collective-permute-start.6 = (bf16[1152,128]{1,0:T(8,128)(2,1)S(1)}, bf16[1152,128]{1,0:T(8,128)(2,1)S(1)}, u32[]{:S(2)}, u32[]{:S(2)}) collective-permute-start(bf16[1152,128]{1,0:T(8,128)(2,1)S(1)} %bitcast.45), channel_id=1, source_target_pairs={{488,0},{496,8},{504,16},{0,24},{8,32},{16,40},{24,48},{32,56},{40... | collective-permute-start | bytes 884744 | tf_op jit(solution)/shard_map/ppermute | solution.py:14
  61.0 0.1 constant_dynamic-update-slice_fusion.6
  61.1 4.3 %collective-permute-start.7 = (bf16[1152,128]{1,0:T(8,128)(2,1)S(1)}, bf16[1152,128]{1,0:T(8,128)(2,1)S(1)}, u32[]{:S(2)}, u32[]{:S(2)}) collective-permute-start(bf16[1152,128]{1,0:T(8,128)(2,1)S(1)} %bitcast.46), channel_id=1, source_target_pairs={{32,0},{33,1},{482,2},{483,3},{40,8},{41,9},{490,10},{491,11},{48,... | collective-permute-start | bytes 884744 | tf_op jit(solution)/shard_map/ppermute | solution.py:24
  65.4 0.1 constant_dynamic-update-slice_fusion.5
  65.5 6.5 %collective-permute-done.3 = bf16[1152,128]{1,0:T(8,128)(2,1)S(1)} collective-permute-done((bf16[1152,128]{1,0:T(8,128)(2,1)S(1)}, bf16[1152,128]{1,0:T(8,128)(2,1)S(1)}, u32[]{:S(2)}, u32[]{:S(2)}) %collective-permute-start.3) | collective-permute-done | bytes 294944 | tf_op jit(solution)/shard_map/ppermute | solution.py:14
  72.1 10.7 %collective-permute-done.4 = bf16[1152,128]{1,0:T(8,128)(2,1)S(1)} collective-permute-done((bf16[1152,128]{1,0:T(8,128)(2,1)S(1)}, bf16[1152,128]{1,0:T(8,128)(2,1)S(1)}, u32[]{:S(2)}, u32[]{:S(2)}) %collective-permute-start.4) | collective-permute-done | bytes 294944 | tf_op jit(solution)/shard_map/ppermute | solution.py:14
  82.8 0.1 constant_dynamic-update-slice_fusion.3
  83.0 0.1 constant_dynamic-update-slice_fusion.2
  83.1 6.4 %collective-permute-done.6 = bf16[1152,128]{1,0:T(8,128)(2,1)S(1)} collective-permute-done((bf16[1152,128]{1,0:T(8,128)(2,1)S(1)}, bf16[1152,128]{1,0:T(8,128)(2,1)S(1)}, u32[]{:S(2)}, u32[]{:S(2)}) %collective-permute-start.6) | collective-permute-done | bytes 294944 | tf_op jit(solution)/shard_map/ppermute | solution.py:14
  89.5 2.9 %collective-permute-done.7 = bf16[1152,128]{1,0:T(8,128)(2,1)S(1)} collective-permute-done((bf16[1152,128]{1,0:T(8,128)(2,1)S(1)}, bf16[1152,128]{1,0:T(8,128)(2,1)S(1)}, u32[]{:S(2)}, u32[]{:S(2)}) %collective-permute-start.7) | collective-permute-done | bytes 294944 | tf_op jit(solution)/shard_map/ppermute | solution.py:24
  92.5 3.9 %add_divide_fusion = f32[1024,512]{1,0:T(8,128)S(1)} fusion(bf16[1152,1024]{1,0:T(8,128)(2,1)S(1)} %constant_dynamic-update-slice_fusion, bf16[1152,512]{1,0:T(8,128)(2,1)} %all-gather.2.cloned.1.call-done, f32[]{:T(128)} %bitcast.36, f32[]{:T(128)} %bitcast.35), kind=kOutput, calls=%fused_computation.1 | convolution fusion | flops 1210580992 | bytes 5636104 | tf_op jit(solution)/shard_map/dot_general | solution.py:89
  96.5 0.1 slice.135
  96.6 0.1 fusion.12
  96.7 3.1 %convolution_convert_fusion = bf16[1152,512]{1,0:T(8,128)(2,1)S(1)} fusion(bf16[1152,1024]{1,0:T(8,128)(2,1)} %copy-done, bf16[128,512]{1,0:T(8,128)(2,1)S(1)} %get-tuple-element.5, bf16[768,512]{1,0:T(8,128)(2,1)S(1)} %slice.135, bf16[128,512]{1,0:T(8,128)(2,1)S(1)} %get-tuple-element.4), kind=kOutput, calls=%fused_computation | convolution fusion | flops 1211695104 | bytes 4587520 | tf_op jit(solution)/shard_map/dot_general | solution.py:98
  99.8 0.3 reshape.118
  100.1 0.2 copy.7
  100.3 37.6 %all_to_all.10 = bf16[8,288,256]{2,1,0:T(8,128)(2,1)S(1)} all-to-all(bf16[8,288,256]{2,1,0:T(8,128)(2,1)S(1)} %bitcast.38), channel_id=1, replica_groups=mesh['chip'=64,'core'=2,'width'=4] {'core','width'}, dimensions={0} | all-to-all | bytes 2359296 | tf_op jit(solution)/shard_map/all_to_all | solution.py:101
  137.9 0.2 convert_element_type.31
  138.1 1.0 fusion.8
  (20 shorter events, 0.5 us)
Async XLA Ops:
  7.2 15.1 %copy-start.1 = (s32[1,256]{1,0:T(1,128)S(1)}, s32[1,256]{1,0:T(1,128)}, u32[]{:S(2)}) copy-start(s32[1,256]{1,0:T(1,128)} %param.7) | copy-start | bytes 3076
  8.9 3.9 %collective-permute-start = (bf16[304,512]{1,0:T(8,128)(2,1)S(1)}, bf16[304,512]{1,0:T(8,128)(2,1)S(1)}, u32[]{:S(2)}, u32[]{:S(2)}) collective-permute-start(bf16[304,512]{1,0:T(8,128)(2,1)S(1)} %fusion.6), channel_id=1, source_target_pairs={{0,4},{4,0},{1,5},{5,1},{2,6},{6,2},{3,7},{7,3},{8,12},{12,8},{9,1... | collective-permute-start | bytes 933896 | tf_op jit(solution)/shard_map/ppermute | solution.py:28
  14.7 16.8 %all-to-all-start = ((bf16[4,288,128]{2,1,0:T(8,128)(2,1)}), bf16[4,288,128]{2,1,0:T(8,128)(2,1)S(1)}, u32[]{:S(2)}, u32[]{:S(2)}) async-start(bf16[4,288,128]{2,1,0:T(8,128)(2,1)} %pad_maximum_fusion), calls=%async_computation | async-start | bytes 589824 | tf_op jit(solution)/shard_map/all_to_all | solution.py:67
  21.5 71.0 %all-gather.2.cloned.1.call-start = ((), (), s32[]{:S(2)}) async-start(), calls=%async_computation.2 | async-start | bytes 1474560 | tf_op jit(solution)/shard_map/all_gather | solution.py:73
  31.5 26.4 %collective-permute-start.1 = (bf16[1152,128]{1,0:T(8,128)(2,1)S(1)}, bf16[1152,128]{1,0:T(8,128)(2,1)S(1)}, u32[]{:S(2)}, u32[]{:S(2)}) collective-permute-start(bf16[1152,128]{1,0:T(8,128)(2,1)S(1)} %bitcast.39), channel_id=1, source_target_pairs={{8,0},{16,8},{24,16},{32,24},{40,32},{48,40},{56,48},{64,56},{72,6... | collective-permute-start | bytes 884744 | tf_op jit(solution)/shard_map/ppermute | solution.py:14
  36.4 24.7 %collective-permute-start.2 = (bf16[1152,128]{1,0:T(8,128)(2,1)S(1)}, bf16[1152,128]{1,0:T(8,128)(2,1)S(1)}, u32[]{:S(2)}, u32[]{:S(2)}) collective-permute-start(bf16[1152,128]{1,0:T(8,128)(2,1)S(1)} %bitcast.40), channel_id=1, source_target_pairs={{504,0},{0,8},{8,16},{16,24},{24,32},{32,40},{40,48},{48,56},{56,6... | collective-permute-start | bytes 884744 | tf_op jit(solution)/shard_map/ppermute | solution.py:14
  38.5 33.6 %collective-permute-start.3 = (bf16[1152,128]{1,0:T(8,128)(2,1)S(1)}, bf16[1152,128]{1,0:T(8,128)(2,1)S(1)}, u32[]{:S(2)}, u32[]{:S(2)}) collective-permute-start(bf16[1152,128]{1,0:T(8,128)(2,1)S(1)} %bitcast.42), channel_id=1, source_target_pairs={{16,0},{24,8},{32,16},{40,24},{48,32},{56,40},{64,48},{72,56},{80,... | collective-permute-start | bytes 884744 | tf_op jit(solution)/shard_map/ppermute | solution.py:14
  52.9 30.0 %collective-permute-start.4 = (bf16[1152,128]{1,0:T(8,128)(2,1)S(1)}, bf16[1152,128]{1,0:T(8,128)(2,1)S(1)}, u32[]{:S(2)}, u32[]{:S(2)}) collective-permute-start(bf16[1152,128]{1,0:T(8,128)(2,1)S(1)} %bitcast.43), channel_id=1, source_target_pairs={{496,0},{504,8},{0,16},{8,24},{16,32},{24,40},{32,48},{40,56},{48,... | collective-permute-start | bytes 884744 | tf_op jit(solution)/shard_map/ppermute | solution.py:14
  54.8 28.1 %collective-permute-start.5 = (bf16[1152,128]{1,0:T(8,128)(2,1)S(1)}, bf16[1152,128]{1,0:T(8,128)(2,1)S(1)}, u32[]{:S(2)}, u32[]{:S(2)}) collective-permute-start(bf16[1152,128]{1,0:T(8,128)(2,1)S(1)} %bitcast.44), channel_id=1, source_target_pairs={{24,0},{32,8},{40,16},{48,24},{56,32},{64,40},{72,48},{80,56},{88,... | collective-permute-start | bytes 884744 | tf_op jit(solution)/shard_map/ppermute | solution.py:14
  57.8 31.6 %collective-permute-start.6 = (bf16[1152,128]{1,0:T(8,128)(2,1)S(1)}, bf16[1152,128]{1,0:T(8,128)(2,1)S(1)}, u32[]{:S(2)}, u32[]{:S(2)}) collective-permute-start(bf16[1152,128]{1,0:T(8,128)(2,1)S(1)} %bitcast.45), channel_id=1, source_target_pairs={{488,0},{496,8},{504,16},{0,24},{8,32},{16,40},{24,48},{32,56},{40... | collective-permute-start | bytes 884744 | tf_op jit(solution)/shard_map/ppermute | solution.py:14
  61.1 31.3 %collective-permute-start.7 = (bf16[1152,128]{1,0:T(8,128)(2,1)S(1)}, bf16[1152,128]{1,0:T(8,128)(2,1)S(1)}, u32[]{:S(2)}, u32[]{:S(2)}) collective-permute-start(bf16[1152,128]{1,0:T(8,128)(2,1)S(1)} %bitcast.46), channel_id=1, source_target_pairs={{32,0},{33,1},{482,2},{483,3},{40,8},{41,9},{490,10},{491,11},{48,... | collective-permute-start | bytes 884744 | tf_op jit(solution)/shard_map/ppermute | solution.py:24
  92.5 4.0 %copy-start = (bf16[1152,1024]{1,0:T(8,128)(2,1)}, bf16[1152,1024]{1,0:T(8,128)(2,1)S(1)}, u32[]{:S(2)}) copy-start(bf16[1152,1024]{1,0:T(8,128)(2,1)S(1)} %constant_dynamic-update-slice_fusion) | copy-start | bytes 7077892
Sparse Core Ops, SparseCore 0:
  25.0 50.1 all-gather.1

commit v2 on v1

v2 whole, which is shorter than its diff:
```python
import jax
import jax.numpy as jnp
from jax import lax
from jax.experimental import pallas as pl
from jax.experimental.pallas import tpu as pltpu
from jax.sharding import Mesh, PartitionSpec as P

CORES = 2
WIDTH = 4
LEVELS = 2
LINE = 4
BF16 = jnp.bfloat16
F32 = jnp.float32
SMEM = pl.BlockSpec(memory_space=pltpu.SMEM)
HBM = pl.BlockSpec(memory_space=pl.ANY)
LOCAL = pl.BlockSpec(memory_space=pltpu.VMEM)
PIECES = 2 * LINE
MARKS = 16


def swap_cores(block):
    return lax.ppermute(block, "core", [(0, 1), (1, 0)])


def along_line(block, distance):
    return lax.ppermute(block, "x", [((i + distance) % LINE, i) for i in range(LINE)])


def far_route(rows):
    route = []
    for i in range(rows):
        route += [(2 * i, 2 * ((i + 1) % rows)), (2 * i + 1, 2 * ((i - 1) % rows) + 1)]
    return route


def pack_kernel(image, text, matches, out):
    features, rows = image.shape
    out[:features, :rows] = image[...]
    out[:features, rows:] = text[...]
    marks = jnp.broadcast_to(matches[...], (MARKS, rows)).astype(F32).astype(BF16)
    out[features:, :rows] = marks
    out[features:, rows:] = marks


def deal_kernel(mine, other, chunks, full):
    rows = full.shape[1] // CORES
    features = full.shape[0]
    n = chunks.shape[2]
    first = lax.axis_index("core") == 0
    image, text = mine[:features, :rows], mine[:features, rows:]
    other_image, other_text = other[:features, :rows], other[:features, rows:]
    parts = (
        jnp.where(first, image, other_text),
        jnp.where(first, other_image, text),
    )
    for i in range(LEVELS * WIDTH):
        q = i % WIDTH
        chunks[i] = parts[q // 2][:, (q % 2) * n : (q % 2 + 1) * n]
    full[:, :rows] = jnp.where(first, text, other_image)
    full[:, rows:] = jnp.where(first, other_text, image)


def core_kernel(scalars, have, goal, dealt, far, l1, l2, l3, h1, h2, h3, held, out, pieces, sems):
    span = held.shape[1]
    whole, n = l1.shape
    rows = span // CORES
    features = whole // WIDTH
    w, level = lax.axis_index("width"), lax.axis_index("level")
    block = w // 2
    from_pair = (w < 2) == (level == 0)

    def put(source, p):
        return pltpu.make_async_copy(source, pieces.at[:, pl.ds(p * n, n)], sems.at[p])

    copies = [put(part, p) for p, part in enumerate((dealt.at[level], l1, l2, l3, h1, h2, h3))]
    for copy in copies:
        copy.start()

    @pl.when(from_pair)
    def _():
        last = put(dealt.at[1 - level], PIECES - 1)
        last.start()
        last.wait()

    @pl.when(jnp.logical_not(from_pair))
    def _():
        last = put(far, PIECES - 1)
        last.start()
        last.wait()

    for copy in copies:
        copy.wait()
    logits = lax.dot_general(
        pieces[...], held[...], (((0,), (0,)), ((), ())), preferred_element_type=F32
    )
    probs = jax.nn.sigmoid(scalars[0] * logits + scalars[1])
    label = (have[...] == goal[...]).astype(F32)
    lane = lax.broadcasted_iota(jnp.int32, (n, span), 1)
    last = probs.shape[0] - n
    weights = jnp.concatenate(
        [
            (probs[:n] - label).astype(BF16),
            probs[n:last].astype(BF16),
            jnp.where(lane // rows != block, probs[last:], 0.0).astype(BF16),
        ],
        0,
    )
    for to in range(WIDTH):
        total = jnp.dot(
            pieces[to * features : (to + 1) * features, :], weights, preferred_element_type=F32
        ).astype(BF16)
        for core in range(CORES):
            out[core * WIDTH + to] = total[:, core * rows : (core + 1) * rows]


def per_device(images, texts, matches, scale, shift_bias):
    first = lax.axis_index("core") == 0
    w = lax.axis_index("width")
    x = lax.axis_index("x")
    level = lax.axis_index("level")
    features, rows = images.shape[1], images.shape[0]
    span = CORES * rows
    quarter = span // WIDTH
    whole = WIDTH * features
    block = w // 2
    scalars = jnp.concatenate([scale, shift_bias])

    image, text = images.T, texts.T
    mine = pl.pallas_call(
        pack_kernel,
        out_shape=jax.ShapeDtypeStruct((features + MARKS, CORES * rows), BF16),
        in_specs=[LOCAL] * 3,
        out_specs=LOCAL,
        compiler_params=pltpu.CompilerParams(vmem_limit_bytes=6 << 20),
    )(image, text, matches)
    other = swap_cores(mine)
    other_matches = other[features : features + 1, :rows].astype(jnp.int32)
    chunks, full = pl.pallas_call(
        deal_kernel,
        out_shape=[
            jax.ShapeDtypeStruct((LEVELS * WIDTH, features, quarter), BF16),
            jax.ShapeDtypeStruct((features, span), BF16),
        ],
        in_specs=[LOCAL] * 2,
        out_specs=[LOCAL] * 2,
        compiler_params=pltpu.CompilerParams(vmem_limit_bytes=6 << 20),
    )(mine, other)
    dealt = lax.all_to_all(chunks, ("level", "width"), 0, 0).reshape(LEVELS, whole, quarter)
    own = lax.dynamic_index_in_dim(dealt, level, 0, False)
    pair = lax.dynamic_index_in_dim(dealt, 1 - level, 0, False)

    held = lax.all_to_all(jnp.broadcast_to(full[None], (WIDTH,) + full.shape), "width", 0, 0)
    held = held.reshape(whole, span)
    far = lax.ppermute(pair, ("row", "level"), far_route(lax.axis_size("row")))
    l1, l2, l3 = (along_line(own, d) for d in (1, 2, 3))

    def to_send(d):
        higher = (x + d) % LINE > x
        return jnp.where(higher == (level == 0), pair, far)

    h1, h2, h3 = (along_line(to_send(LINE - d), d) for d in (1, 2, 3))

    both = jnp.concatenate(
        [jnp.where(first, matches, other_matches), jnp.where(first, other_matches, matches)], 1
    )
    lane = lax.broadcasted_iota(jnp.int32, (1, span), 1)
    sub = lax.broadcasted_iota(jnp.int32, (quarter, 1), 0)
    goal = jnp.where(first, lane % rows, both)
    goal = jnp.where(lane // rows == block, goal, -1)
    mark = lax.dynamic_slice(both, (0, w * quarter), (1, quarter)).reshape(quarter, 1)
    have = jnp.where(first, mark, sub + (w % CORES) * quarter)

    partial = pl.pallas_call(
        core_kernel,
        out_shape=jax.ShapeDtypeStruct((CORES * WIDTH, features, rows), BF16),
        in_specs=[SMEM, LOCAL, LOCAL] + [LOCAL] * 9,
        out_specs=LOCAL,
        scratch_shapes=[
            pltpu.VMEM((whole, PIECES * quarter), BF16),
            pltpu.SemaphoreType.DMA((PIECES,)),
        ],
        compiler_params=pltpu.CompilerParams(vmem_limit_bytes=14 << 20),
        cost_estimate=pl.CostEstimate(
            flops=4 * whole * PIECES * quarter * span, bytes_accessed=6 << 20, transcendentals=0
        ),
    )(scalars, have, goal, dealt, far, l1, l2, l3, h1, h2, h3, held)
    terms = lax.all_to_all(partial, ("core", "width"), 0, 0).astype(F32)
    grad_text = terms[0] + terms[1] + terms[2] + terms[3]
    grad_image = terms[4] + terms[5] + terms[6] + terms[7]
    return (scale[0] * grad_image).T, (scale[0] * grad_text).T


def solution(mesh):
    deep = mesh.shape["tour"] // (LEVELS * LINE * CORES)
    fine = Mesh(
        mesh.devices.reshape(deep, LEVELS, LINE, CORES, WIDTH),
        ("row", "level", "x", "core", "width"),
    )
    rows, split = ("row", "level", "x", "core"), "width"
    return jax.shard_map(
        per_device,
        mesh=fine,
        in_specs=(P(rows, split), P(rows, split), P(rows, None), P(), P()),
        out_specs=(P(rows, split), P(rows, split)),
        check_vma=False,
    )
```

time: 147 us -> 127 us (0.86)
  the two profiles are of different devices: /device:TPU:3 before, /device:TPU:9 now
where the time goes in v2:
time: 127 us
  blocking collectives  58.1 us (46%)
  starting transfers between devices  34 us (27%)
  waiting for transfers between devices  17.4 us (14%)
  local copies, waits for them, and re-layouts  8.91 us (7%)
  Pallas kernels  4.24 us (3%)
  between operations  2.22 us (2%)
  other arithmetic  1.89 us (1%)
    all_to_all x1, blocking collectives, per_device(): terms = lax.all_to_all(partial, ('core', 'width'), 0, 0).astype(F32)  32.7 us
    all_to_all x1, blocking collectives, per_device(): lax.all_to_all(chunks, ('level', 'width'), 0, 0)  25.4 us
    ppermute x6, starting transfers between devices, along_line(): lax.ppermute(block, 'x', [((i + distance) % LINE, i) for i in range(LINE)])  18.5 us
    ppermute x6, waiting for transfers between devices, along_line(): lax.ppermute(block, 'x', [((i + distance) % LINE, i) for i in range(LINE)])  16.2 us
    ppermute x1, starting transfers between devices, per_device(): far = lax.ppermute(pair, ('row', 'level'), far_route(lax.axis_size('row')))  9.36 us
    unnamed x26, local copies, waits for them, and re-layouts  6.9 us
    pallas_call x1, Pallas kernels, per_device(): pl.pallas_call(core_kernel, out_shape=jax.ShapeDtypeStruct((CORES * WIDTH...  4.1 us
    all_to_all x1, starting transfers between devices, per_device(): lax.all_to_all(jnp.broadcast_to(full[None], (WIDTH,) + full.shape), 'widt...  3.53 us
  transfers between devices with their start and end apart: 9, of which 4 were waited for; matrix products, arithmetic and copies ran while one was open for 1% of the time, Pallas kernels for 0%

profile of v2, /device:TPU:9, one launch (start us, length us, event | category | flops | bytes accessed | tf_op | source)
XLA Modules:
  0.0 126.7 jit_solution(1432693543758178247)
XLA Ops:
  0.6 0.9 copy-done
  1.5 0.9 copy-done.1
  2.5 0.7 copy-done.2
  3.2 2.6 %collective-permute-start = (bf16[304,512]{1,0:T(8,128)(2,1)S(1)}, bf16[304,512]{1,0:T(8,128)(2,1)S(1)}, u32[]{:S(2)}, u32[]{:S(2)}) collective-permute-start(bf16[304,512]{1,0:T(8,128)(2,1)S(1)} %shard_map.68.mine), channel_id=1, source_target_pairs={{0,4},{4,0},{1,5},{5,1},{2,6},{6,2},{3,7},{7,3},{8,12},{12,8},{9,1... | collective-permute-start | bytes 933896 | tf_op jit(solution)/shard_map/ppermute | solution.py:22
  5.7 1.2 collective-permute-done.other
  7.0 0.1 shard_map.69
  7.1 25.4 %all_to_all.15 = bf16[8,288,128]{2,1,0:T(8,128)(2,1)S(1)} all-to-all(bf16[8,288,128]{2,1,0:T(8,128)(2,1)S(1)} %get-tuple-element.4), channel_id=1, replica_groups=mesh['row'=8,'level'=2,'x'=4,'core'=2,'width'=4] {'level','width'}, dimensions={0} | all-to-all | bytes 1179648 | tf_op jit(solution)/shard_map/all_to_all | solution.py:148
  32.5 1.1 broadcast_in_dim.3
  33.6 3.5 %all-to-all-start.1 = ((bf16[4,288,512]{2,1,0:T(8,128)(2,1)}), bf16[4,288,512]{2,1,0:T(8,128)(2,1)S(1)}, u32[]{:S(2)}, u32[]{:S(2)}) async-start(bf16[4,288,512]{2,1,0:T(8,128)(2,1)} %broadcast_in_dim.3), calls=%async_computation.1 | async-start | bytes 2359296 | tf_op jit(solution)/shard_map/all_to_all | solution.py:152
  38.5 0.6 pad_maximum_fusion.scalars
  39.1 0.8 dynamic-slice_bitcast_fusion
  39.9 9.4 %collective-permute-start.1 = (bf16[1152,128]{1,0:T(8,128)(2,1)S(1)}, bf16[1152,128]{1,0:T(8,128)(2,1)S(1)}, u32[]{:S(2)}, u32[]{:S(2)}) collective-permute-start(bf16[1152,128]{1,0:T(8,128)(2,1)S(1)} %get-tuple-element.12), channel_id=1, source_target_pairs={{0,64},{32,480},{64,128},{96,32},{128,192},{160,96},{192,256},{224... | collective-permute-start | bytes 884744 | tf_op jit(solution)/shard_map/ppermute | solution.py:154
  49.3 0.1 copy.7
  49.4 0.4 copy-done.9
  49.9 4.5 %collective-permute-start.2 = (bf16[1152,128]{1,0:T(8,128)(2,1)}, bf16[1152,128]{1,0:T(8,128)(2,1)S(1)}, u32[]{:S(2)}, u32[]{:S(2)}) collective-permute-start(bf16[1152,128]{1,0:T(8,128)(2,1)} %get-tuple-element.11), channel_id=1, source_target_pairs={{8,0},{16,8},{24,16},{0,24},{9,1},{17,9},{25,17},{1,25},{10,2},{18... | collective-permute-start | bytes 884744 | tf_op jit(solution)/shard_map/ppermute | solution.py:26
  54.4 2.4 %collective-permute-start.3 = (bf16[1152,128]{1,0:T(8,128)(2,1)}, bf16[1152,128]{1,0:T(8,128)(2,1)S(1)}, u32[]{:S(2)}, u32[]{:S(2)}) collective-permute-start(bf16[1152,128]{1,0:T(8,128)(2,1)} %get-tuple-element.11), channel_id=1, source_target_pairs={{16,0},{24,8},{0,16},{8,24},{17,1},{25,9},{1,17},{9,25},{18,2},{26... | collective-permute-start | bytes 884744 | tf_op jit(solution)/shard_map/ppermute | solution.py:26
  56.8 2.5 %collective-permute-start.4 = (bf16[1152,128]{1,0:T(8,128)(2,1)}, bf16[1152,128]{1,0:T(8,128)(2,1)S(1)}, u32[]{:S(2)}, u32[]{:S(2)}) collective-permute-start(bf16[1152,128]{1,0:T(8,128)(2,1)} %get-tuple-element.11), channel_id=1, source_target_pairs={{24,0},{0,8},{8,16},{16,24},{25,1},{1,9},{9,17},{17,25},{26,2},{2,... | collective-permute-start | bytes 884744 | tf_op jit(solution)/shard_map/ppermute | solution.py:26
  59.4 4.0 %collective-permute-start.5 = (bf16[1152,128]{1,0:T(8,128)(2,1)S(1)}, bf16[1152,128]{1,0:T(8,128)(2,1)S(1)}, u32[]{:S(2)}, u32[]{:S(2)}) collective-permute-start(bf16[1152,128]{1,0:T(8,128)(2,1)S(1)} %get-tuple-element.10), channel_id=1, source_target_pairs={{8,0},{16,8},{24,16},{0,24},{9,1},{17,9},{25,17},{1,25},{10,2},{18... | collective-permute-start | bytes 884744 | tf_op jit(solution)/shard_map/ppermute | solution.py:26
  63.4 3.1 %collective-permute-start.6 = (bf16[1152,128]{1,0:T(8,128)(2,1)S(1)}, bf16[1152,128]{1,0:T(8,128)(2,1)S(1)}, u32[]{:S(2)}, u32[]{:S(2)}) collective-permute-start(bf16[1152,128]{1,0:T(8,128)(2,1)S(1)} %get-tuple-element.9), channel_id=1, source_target_pairs={{16,0},{24,8},{0,16},{8,24},{17,1},{25,9},{1,17},{9,25},{18,2},{26... | collective-permute-start | bytes 884744 | tf_op jit(solution)/shard_map/ppermute | solution.py:26
  66.6 1.9 %collective-permute-start.7 = (bf16[1152,128]{1,0:T(8,128)(2,1)S(1)}, bf16[1152,128]{1,0:T(8,128)(2,1)S(1)}, u32[]{:S(2)}, u32[]{:S(2)}) collective-permute-start(bf16[1152,128]{1,0:T(8,128)(2,1)S(1)} %get-tuple-element.8), channel_id=1, source_target_pairs={{24,0},{0,8},{8,16},{16,24},{25,1},{1,9},{9,17},{17,25},{26,2},{2,... | collective-permute-start | bytes 884744 | tf_op jit(solution)/shard_map/ppermute | solution.py:26
  68.6 6.1 %collective-permute-done.4.l3 = bf16[1152,128]{1,0:T(8,128)(2,1)S(1)} collective-permute-done((bf16[1152,128]{1,0:T(8,128)(2,1)}, bf16[1152,128]{1,0:T(8,128)(2,1)S(1)}, u32[]{:S(2)}, u32[]{:S(2)}) %collective-permute-start.4) | collective-permute-done | bytes 294944 | tf_op jit(solution)/shard_map/ppermute | solution.py:26
  74.7 2.6 %collective-permute-done.6.h2 = bf16[1152,128]{1,0:T(8,128)(2,1)S(1)} collective-permute-done((bf16[1152,128]{1,0:T(8,128)(2,1)S(1)}, bf16[1152,128]{1,0:T(8,128)(2,1)S(1)}, u32[]{:S(2)}, u32[]{:S(2)}) %collective-permute-start.6) | collective-permute-done | bytes 294944 | tf_op jit(solution)/shard_map/ppermute | solution.py:26
  77.3 0.7 copy-done.4
  78.0 7.4 %collective-permute-done.7.h3 = bf16[1152,128]{1,0:T(8,128)(2,1)S(1)} collective-permute-done((bf16[1152,128]{1,0:T(8,128)(2,1)S(1)}, bf16[1152,128]{1,0:T(8,128)(2,1)S(1)}, u32[]{:S(2)}, u32[]{:S(2)}) %collective-permute-start.7) | collective-permute-done | bytes 294944 | tf_op jit(solution)/shard_map/ppermute | solution.py:26
  85.4 0.7 copy-done.6
  86.2 1.0 copy-done.5
  87.1 1.0 copy-done.7
  88.1 0.6 copy-done.8
  88.7 4.1 %shard_map.70 = bf16[8,288,256]{2,1,0:T(8,128)(2,1)S(1)} custom-call(f32[2]{0:T(128)S(1)} %copy-done.8, s32[128,1]{1,0:T(8,128)S(1)} %add_select_fusion.have, s32[1,512]{1,0:T(1,128)S(1)} %compare_select_fusion.goal, bf16[2,1152,128]{2,1,0:T(8,128)(2,1)S(1)} %bitcast.21, bf16[1152,128]{1,0:T(8,128)(2,1)S(1)} %collective-permute-done.1.far, ...), custom_call_target="tpu_custom_call" | custom-call | flops 2415919104 | bytes 6291456 | tf_op jit(solution)/shard_map/pallas_call | solution.py:173
  92.8 32.7 %all_to_all.16 = bf16[8,288,256]{2,1,0:T(8,128)(2,1)S(1)} all-to-all(bf16[8,288,256]{2,1,0:T(8,128)(2,1)S(1)} %shard_map.70), channel_id=1, replica_groups=mesh['row'=8,'level'=2,'x'=4,'core'=2,'width'=4] {'core','width'}, dimensions={0} | all-to-all | bytes 2359296 | tf_op jit(solution)/shard_map/all_to_all | solution.py:187
  125.5 0.2 convert_element_type.7
  125.7 1.0 fusion.1
  (28 shorter events, 0.2 us)
Async XLA Ops:
  0.6 0.9 copy-start
  1.5 0.9 copy-start.1
  2.5 0.7 copy-start.2
  3.2 3.8 %collective-permute-start = (bf16[304,512]{1,0:T(8,128)(2,1)S(1)}, bf16[304,512]{1,0:T(8,128)(2,1)S(1)}, u32[]{:S(2)}, u32[]{:S(2)}) collective-permute-start(bf16[304,512]{1,0:T(8,128)(2,1)S(1)} %shard_map.68.mine), channel_id=1, source_target_pairs={{0,4},{4,0},{1,5},{5,1},{2,6},{6,2},{3,7},{7,3},{8,12},{12,8},{9,1... | collective-permute-start | bytes 933896 | tf_op jit(solution)/shard_map/ppermute | solution.py:22
  33.6 52.5 %all-to-all-start.1 = ((bf16[4,288,512]{2,1,0:T(8,128)(2,1)}), bf16[4,288,512]{2,1,0:T(8,128)(2,1)S(1)}, u32[]{:S(2)}, u32[]{:S(2)}) async-start(bf16[4,288,512]{2,1,0:T(8,128)(2,1)} %broadcast_in_dim.3), calls=%async_computation.1 | async-start | bytes 2359296 | tf_op jit(solution)/shard_map/all_to_all | solution.py:152
  37.2 12.1 %copy-start.3 = (s32[1,256]{1,0:T(1,128)S(1)}, s32[1,256]{1,0:T(1,128)}, u32[]{:S(2)}) copy-start(s32[1,256]{1,0:T(1,128)} %matches.1) | copy-start | bytes 3076
  39.9 19.5 %collective-permute-start.1 = (bf16[1152,128]{1,0:T(8,128)(2,1)S(1)}, bf16[1152,128]{1,0:T(8,128)(2,1)S(1)}, u32[]{:S(2)}, u32[]{:S(2)}) collective-permute-start(bf16[1152,128]{1,0:T(8,128)(2,1)S(1)} %get-tuple-element.12), channel_id=1, source_target_pairs={{0,64},{32,480},{64,128},{96,32},{128,192},{160,96},{192,256},{224... | collective-permute-start | bytes 884744 | tf_op jit(solution)/shard_map/ppermute | solution.py:154
  49.3 0.6 copy-start.9
  49.3 0.6 copy-start.11
  49.9 18.6 %copy-start.10 = (s32[1,256]{1,0:T(1,128)S(1)}, s32[1,256]{1,0:T(1,128)}, u32[]{:S(2)}) copy-start(s32[1,256]{1,0:T(1,128)} %copy-done.9) | copy-start | bytes 3076
  49.9 18.7 %copy-start.12 = (s32[1,256]{1,0:T(1,128)S(1)}, s32[1,256]{1,0:T(1,128)}, u32[]{:S(2)}) copy-start(s32[1,256]{1,0:T(1,128)} %copy-done.11) | copy-start | bytes 3076
  49.9 16.7 %collective-permute-start.2 = (bf16[1152,128]{1,0:T(8,128)(2,1)}, bf16[1152,128]{1,0:T(8,128)(2,1)S(1)}, u32[]{:S(2)}, u32[]{:S(2)}) collective-permute-start(bf16[1152,128]{1,0:T(8,128)(2,1)} %get-tuple-element.11), channel_id=1, source_target_pairs={{8,0},{16,8},{24,16},{0,24},{9,1},{17,9},{25,17},{1,25},{10,2},{18... | collective-permute-start | bytes 884744 | tf_op jit(solution)/shard_map/ppermute | solution.py:26
  54.4 14.2 %collective-permute-start.3 = (bf16[1152,128]{1,0:T(8,128)(2,1)}, bf16[1152,128]{1,0:T(8,128)(2,1)S(1)}, u32[]{:S(2)}, u32[]{:S(2)}) collective-permute-start(bf16[1152,128]{1,0:T(8,128)(2,1)} %get-tuple-element.11), channel_id=1, source_target_pairs={{16,0},{24,8},{0,16},{8,24},{17,1},{25,9},{1,17},{9,25},{18,2},{26... | collective-permute-start | bytes 884744 | tf_op jit(solution)/shard_map/ppermute | solution.py:26
  56.8 17.9 %collective-permute-start.4 = (bf16[1152,128]{1,0:T(8,128)(2,1)}, bf16[1152,128]{1,0:T(8,128)(2,1)S(1)}, u32[]{:S(2)}, u32[]{:S(2)}) collective-permute-start(bf16[1152,128]{1,0:T(8,128)(2,1)} %get-tuple-element.11), channel_id=1, source_target_pairs={{24,0},{0,8},{8,16},{16,24},{25,1},{1,9},{9,17},{17,25},{26,2},{2,... | collective-permute-start | bytes 884744 | tf_op jit(solution)/shard_map/ppermute | solution.py:26
  59.4 15.3 %collective-permute-start.5 = (bf16[1152,128]{1,0:T(8,128)(2,1)S(1)}, bf16[1152,128]{1,0:T(8,128)(2,1)S(1)}, u32[]{:S(2)}, u32[]{:S(2)}) collective-permute-start(bf16[1152,128]{1,0:T(8,128)(2,1)S(1)} %get-tuple-element.10), channel_id=1, source_target_pairs={{8,0},{16,8},{24,16},{0,24},{9,1},{17,9},{25,17},{1,25},{10,2},{18... | collective-permute-start | bytes 884744 | tf_op jit(solution)/shard_map/ppermute | solution.py:26
  63.4 13.9 %collective-permute-start.6 = (bf16[1152,128]{1,0:T(8,128)(2,1)S(1)}, bf16[1152,128]{1,0:T(8,128)(2,1)S(1)}, u32[]{:S(2)}, u32[]{:S(2)}) collective-permute-start(bf16[1152,128]{1,0:T(8,128)(2,1)S(1)} %get-tuple-element.9), channel_id=1, source_target_pairs={{16,0},{24,8},{0,16},{8,24},{17,1},{25,9},{1,17},{9,25},{18,2},{26... | collective-permute-start | bytes 884744 | tf_op jit(solution)/shard_map/ppermute | solution.py:26
  66.6 18.9 %collective-permute-start.7 = (bf16[1152,128]{1,0:T(8,128)(2,1)S(1)}, bf16[1152,128]{1,0:T(8,128)(2,1)S(1)}, u32[]{:S(2)}, u32[]{:S(2)}) collective-permute-start(bf16[1152,128]{1,0:T(8,128)(2,1)S(1)} %get-tuple-element.8), channel_id=1, source_target_pairs={{24,0},{0,8},{8,16},{16,24},{25,1},{1,9},{9,17},{17,25},{26,2},{2,... | collective-permute-start | bytes 884744 | tf_op jit(solution)/shard_map/ppermute | solution.py:26
  77.3 0.7 copy-start.4
  85.4 0.7 copy-start.6
  86.2 1.0 copy-start.5
  87.1 1.0 copy-start.7
  88.1 0.6 copy-start.8

commit v3 on v2

v3 whole, which is shorter than its diff:
```python
import jax
import jax.numpy as jnp
from jax import lax
from jax.experimental import pallas as pl
from jax.experimental.pallas import tpu as pltpu
from jax.sharding import Mesh, PartitionSpec as P

CORES = 2
WIDTH = 4
LEVELS = 2
LINE = 4
BF16 = jnp.bfloat16
F32 = jnp.float32
SMEM = pl.BlockSpec(memory_space=pltpu.SMEM)
HBM = pl.BlockSpec(memory_space=pltpu.HBM)
LOCAL = pl.BlockSpec(memory_space=pltpu.VMEM)
PIECES = 2 * LINE
MARKS = 16


def swap_cores(block):
    return lax.ppermute(block, "core", [(0, 1), (1, 0)])


def along_line(block, distance):
    return lax.ppermute(block, "x", [((i + distance) % LINE, i) for i in range(LINE)])


def far_route(rows):
    route = []
    for i in range(rows):
        route += [(2 * i, 2 * ((i + 1) % rows)), (2 * i + 1, 2 * ((i - 1) % rows) + 1)]
    return route


def pack_kernel(image, text, matches, out, sems):
    features, rows = image.shape
    copies = [
        pltpu.make_async_copy(
            source, out.at[pl.ds(0, features), pl.ds(i * rows, rows)], sems.at[i]
        )
        for i, source in enumerate((image, text))
    ]
    for copy in copies:
        copy.start()
    marks = jnp.broadcast_to(matches[...], (MARKS, rows)).astype(F32).astype(BF16)
    out[features:, :rows] = marks
    out[features:, rows:] = marks
    for copy in copies:
        copy.wait()


def deal_kernel(mine, other, chunks, spread, marks):
    rows = spread.shape[2] // CORES
    features = spread.shape[1]
    n = chunks.shape[2]
    first = lax.axis_index("core") == 0
    image, text = mine[:features, :rows], mine[:features, rows:]
    other_image, other_text = other[:features, :rows], other[:features, rows:]
    parts = (
        jnp.where(first, image, other_text),
        jnp.where(first, other_image, text),
    )
    for i in range(LEVELS * WIDTH):
        q = i % WIDTH
        chunks[i] = parts[q // 2][:, (q % 2) * n : (q % 2 + 1) * n]
    own_marks, other_marks = mine[features:, :rows].astype(F32), other[features:, :rows].astype(F32)
    marks[:, :rows] = jnp.where(first, own_marks, other_marks)
    marks[:, rows:] = jnp.where(first, other_marks, own_marks)
    full = (jnp.where(first, text, other_image), jnp.where(first, other_text, image))
    for i in range(WIDTH):
        spread[i, :, :rows] = full[0]
        spread[i, :, rows:] = full[1]


def weighed(pieces, held, scale, bias):
    logits = lax.dot_general(
        pieces, held[...], (((0,), (0,)), ((), ())), preferred_element_type=F32
    )
    return jax.nn.sigmoid(scale[0] * logits + bias[0])


def label_of(marks, n):
    span = marks.shape[1]
    rows = span // CORES
    first, w = lax.axis_index("core") == 0, lax.axis_index("width")
    mark = marks[0:1, pl.ds(pl.multiple_of(w * n, n), n)]
    down = lax.broadcasted_iota(jnp.int32, (n, n), 0)
    across = lax.broadcasted_iota(jnp.int32, (n, n), 1)
    mark = jnp.sum(jnp.where(down == across, mark, 0.0), axis=1, keepdims=True)
    row = lax.broadcasted_iota(jnp.int32, (n, 1), 0) + lax.rem(w, CORES) * n
    have = jnp.where(first, mark, row.astype(F32))
    lane = lax.broadcasted_iota(jnp.int32, (1, span), 1)
    goal = jnp.where(first, (lane % rows).astype(F32), marks[0:1, :])
    goal = jnp.where(lane // rows == w // CORES, goal, -1.0)
    return (have == goal).astype(F32)


def near_kernel(scale, bias, marks, dealt, l1, l2, l3, held, out):
    n = l1.shape[1]
    own = dealt[lax.axis_index("level")]
    pieces = jnp.concatenate([own, l1[...], l2[...], l3[...]], 1)
    probs = weighed(pieces, held, scale, bias)
    weights = jnp.concatenate([(probs[:n] - label_of(marks, n)).astype(BF16), probs[n:].astype(BF16)], 0)
    out[...] = jnp.dot(pieces, weights, preferred_element_type=F32)


def far_kernel(scale, bias, dealt, far, h1, h2, h3, held, near, out):
    whole, n = h1.shape
    span = held.shape[1]
    rows = span // CORES
    features = whole // WIDTH
    w, level = lax.axis_index("width"), lax.axis_index("level")
    last = jnp.where((w < 2) == (level == 0), dealt[1 - level], far[...])
    pieces = jnp.concatenate([last, h1[...], h2[...], h3[...]], 1)
    probs = weighed(pieces, held, scale, bias)
    lane = lax.broadcasted_iota(jnp.int32, (n, span), 1)
    weights = jnp.concatenate(
        [
            jnp.where(lane // rows != w // 2, probs[:n], 0.0).astype(BF16),
            probs[n:].astype(BF16),
        ],
        0,
    )
    for to in range(WIDTH):
        at = slice(to * features, (to + 1) * features)
        total = near[at, :] + jnp.dot(pieces[at], weights, preferred_element_type=F32)
        total = total.astype(BF16)
        for core in range(CORES):
            out[core * WIDTH + to] = total[:, core * rows : (core + 1) * rows]


def per_device(images, texts, matches, scale, shift_bias):
    x = lax.axis_index("x")
    level = lax.axis_index("level")
    features, rows = images.shape[1], images.shape[0]
    span = CORES * rows
    quarter = span // WIDTH
    whole = WIDTH * features

    image, text = images.T, texts.T
    mine = pl.pallas_call(
        pack_kernel,
        out_shape=jax.ShapeDtypeStruct((features + MARKS, CORES * rows), BF16),
        in_specs=[HBM, HBM, LOCAL],
        out_specs=LOCAL,
        scratch_shapes=[pltpu.SemaphoreType.DMA((2,))],
        compiler_params=pltpu.CompilerParams(vmem_limit_bytes=6 << 20),
    )(image, text, matches)
    other = swap_cores(mine)
    chunks, spread, marks = pl.pallas_call(
        deal_kernel,
        out_shape=[
            jax.ShapeDtypeStruct((LEVELS * WIDTH, features, quarter), BF16),
            jax.ShapeDtypeStruct((WIDTH, features, span), BF16),
            jax.ShapeDtypeStruct((MARKS, span), F32),
        ],
        in_specs=[LOCAL] * 2,
        out_specs=[LOCAL] * 3,
        compiler_params=pltpu.CompilerParams(vmem_limit_bytes=6 << 20),
    )(mine, other)
    dealt = lax.all_to_all(chunks, ("level", "width"), 0, 0).reshape(LEVELS, whole, quarter)
    own = lax.dynamic_index_in_dim(dealt, level, 0, False)
    pair = lax.dynamic_index_in_dim(dealt, 1 - level, 0, False)

    held = lax.all_to_all(spread, "width", 0, 0)
    held = held.reshape(whole, span)
    far = lax.ppermute(pair, ("row", "level"), far_route(lax.axis_size("row")))
    l1, l2, l3 = (along_line(own, d) for d in (1, 2, 3))

    def to_send(d):
        higher = (x + d) % LINE > x
        return jnp.where(higher == (level == 0), pair, far)

    h1, h2, h3 = (along_line(to_send(LINE - d), d) for d in (1, 2, 3))

    cost = pl.CostEstimate(
        flops=2 * whole * PIECES * quarter * span, bytes_accessed=5 << 20, transcendentals=0
    )
    params = pltpu.CompilerParams(vmem_limit_bytes=12 << 20)
    near = pl.pallas_call(
        near_kernel,
        out_shape=jax.ShapeDtypeStruct((whole, span), F32),
        in_specs=[SMEM, SMEM] + [LOCAL] * 6,
        out_specs=LOCAL,
        compiler_params=params,
        cost_estimate=cost,
    )(scale, shift_bias, marks, dealt, l1, l2, l3, held)
    partial = pl.pallas_call(
        far_kernel,
        out_shape=jax.ShapeDtypeStruct((CORES * WIDTH, features, rows), BF16),
        in_specs=[SMEM, SMEM] + [LOCAL] * 7,
        out_specs=LOCAL,
        compiler_params=params,
        cost_estimate=cost,
    )(scale, shift_bias, dealt, far, h1, h2, h3, held, near)
    terms = lax.all_to_all(partial, ("core", "width"), 0, 0).astype(F32)
    grad_text = terms[0] + terms[1] + terms[2] + terms[3]
    grad_image = terms[4] + terms[5] + terms[6] + terms[7]
    return (scale[0] * grad_image).T, (scale[0] * grad_text).T


def solution(mesh):
    deep = mesh.shape["tour"] // (LEVELS * LINE * CORES)
    fine = Mesh(
        mesh.devices.reshape(deep, LEVELS, LINE, CORES, WIDTH),
        ("row", "level", "x", "core", "width"),
    )
    rows, split = ("row", "level", "x", "core"), "width"
    return jax.shard_map(
        per_device,
        mesh=fine,
        in_specs=(P(rows, split), P(rows, split), P(rows, None), P(), P()),
        out_specs=(P(rows, split), P(rows, split)),
        check_vma=False,
    )
```

time: 127 us -> 119 us (0.937)
  the two profiles are of different devices: /device:TPU:9 before, /device:TPU:11 now
where the time goes in v3:
time: 119 us; the launch traced here: 118 us
  blocking collectives  56.5 us (47%)
  starting transfers between devices  35.1 us (29%)
  waiting for transfers between devices  12.8 us (11%)
  Pallas kernels  5.36 us (5%)
  local copies, waits for them, and re-layouts  4.01 us (3%)
  other arithmetic  2.16 us (2%)
  between operations  2.13 us (2%)
    all_to_all x1, blocking collectives, per_device(): terms = lax.all_to_all(partial, ('core', 'width'), 0, 0).astype(F32)  32.4 us
    all_to_all x1, blocking collectives, per_device(): lax.all_to_all(chunks, ('level', 'width'), 0, 0)  24.1 us
    ppermute x6, starting transfers between devices, along_line(): lax.ppermute(block, 'x', [((i + distance) % LINE, i) for i in range(LINE)])  18.3 us
    ppermute x6, waiting for transfers between devices, along_line(): lax.ppermute(block, 'x', [((i + distance) % LINE, i) for i in range(LINE)])  11.6 us
    ppermute x1, starting transfers between devices, per_device(): far = lax.ppermute(pair, ('row', 'level'), far_route(lax.axis_size('row')))  10.7 us
    all_to_all x1, starting transfers between devices, per_device(): held = lax.all_to_all(spread, 'width', 0, 0)  3.53 us
    unnamed x10, local copies, waits for them, and re-layouts  3.25 us
    ppermute x1, starting transfers between devices, swap_cores(): return lax.ppermute(block, 'core', [(0, 1), (1, 0)])  2.58 us
  transfers between devices with their start and end apart: 9, of which 3 were waited for; matrix products, arithmetic and copies ran while one was open for 1% of the time, Pallas kernels for 1%

profile of v3, /device:TPU:11, one launch (start us, length us, event | category | flops | bytes accessed | tf_op | source)
XLA Modules:
  0.0 118.0 jit_solution(17885602776009683367)
XLA Ops:
  0.6 0.9 copy-done
  1.5 0.9 copy-done.1
  2.5 0.7 copy-done.4
  3.2 2.6 %collective-permute-start = (bf16[304,512]{1,0:T(8,128)(2,1)S(1)}, bf16[304,512]{1,0:T(8,128)(2,1)S(1)}, u32[]{:S(2)}, u32[]{:S(2)}) collective-permute-start(bf16[304,512]{1,0:T(8,128)(2,1)S(1)} %shard_map.68.mine), channel_id=1, source_target_pairs={{0,4},{4,0},{1,5},{5,1},{2,6},{6,2},{3,7},{7,3},{8,12},{12,8},{9,1... | collective-permute-start | bytes 933896 | tf_op jit(solution)/shard_map/ppermute | solution.py:22
  5.8 1.2 %collective-permute-done.other = bf16[304,512]{1,0:T(8,128)(2,1)S(1)} collective-permute-done((bf16[304,512]{1,0:T(8,128)(2,1)S(1)}, bf16[304,512]{1,0:T(8,128)(2,1)S(1)}, u32[]{:S(2)}, u32[]{:S(2)}) %collective-permute-start) | collective-permute-done | bytes 311328 | tf_op jit(solution)/shard_map/ppermute | solution.py:22
  7.0 1.2 shard_map.69
  8.2 24.1 %all_to_all.15 = bf16[8,288,128]{2,1,0:T(8,128)(2,1)S(1)} all-to-all(bf16[8,288,128]{2,1,0:T(8,128)(2,1)S(1)} %get-tuple-element.5), channel_id=1, replica_groups=mesh['row'=8,'level'=2,'x'=4,'core'=2,'width'=4] {'level','width'}, dimensions={0} | all-to-all | bytes 1179648 | tf_op jit(solution)/shard_map/all_to_all | solution.py:162
  32.3 0.0 copy-done.2
  32.3 3.5 %all-to-all-start.1 = ((bf16[4,288,512]{2,1,0:T(8,128)(2,1)}), bf16[4,288,512]{2,1,0:T(8,128)(2,1)S(1)}, u32[]{:S(2)}, u32[]{:S(2)}) async-start(bf16[4,288,512]{2,1,0:T(8,128)(2,1)} %get-tuple-element.6), calls=%async_computation.1 | async-start | bytes 2359296 | tf_op jit(solution)/shard_map/all_to_all | solution.py:166
  35.8 0.8 dynamic-slice_bitcast_fusion
  36.6 10.7 %collective-permute-start.1 = (bf16[1152,128]{1,0:T(8,128)(2,1)S(1)}, bf16[1152,128]{1,0:T(8,128)(2,1)S(1)}, u32[]{:S(2)}, u32[]{:S(2)}) collective-permute-start(bf16[1152,128]{1,0:T(8,128)(2,1)S(1)} %get-tuple-element.11), channel_id=1, source_target_pairs={{0,64},{32,480},{64,128},{96,32},{128,192},{160,96},{192,256},{224... | collective-permute-start | bytes 884744 | tf_op jit(solution)/shard_map/ppermute | solution.py:168
  47.3 3.1 %collective-permute-start.7 = (bf16[1152,128]{1,0:T(8,128)(2,1)}, bf16[1152,128]{1,0:T(8,128)(2,1)S(1)}, u32[]{:S(2)}, u32[]{:S(2)}) collective-permute-start(bf16[1152,128]{1,0:T(8,128)(2,1)} %get-tuple-element.10), channel_id=1, source_target_pairs={{24,0},{0,8},{8,16},{16,24},{25,1},{1,9},{9,17},{17,25},{26,2},{2,... | collective-permute-start | bytes 884744 | tf_op jit(solution)/shard_map/ppermute | solution.py:26
  50.4 2.7 %collective-permute-start.6 = (bf16[1152,128]{1,0:T(8,128)(2,1)}, bf16[1152,128]{1,0:T(8,128)(2,1)S(1)}, u32[]{:S(2)}, u32[]{:S(2)}) collective-permute-start(bf16[1152,128]{1,0:T(8,128)(2,1)} %get-tuple-element.10), channel_id=1, source_target_pairs={{16,0},{24,8},{0,16},{8,24},{17,1},{25,9},{1,17},{9,25},{18,2},{26... | collective-permute-start | bytes 884744 | tf_op jit(solution)/shard_map/ppermute | solution.py:26
  53.1 3.8 %collective-permute-start.5 = (bf16[1152,128]{1,0:T(8,128)(2,1)}, bf16[1152,128]{1,0:T(8,128)(2,1)S(1)}, u32[]{:S(2)}, u32[]{:S(2)}) collective-permute-start(bf16[1152,128]{1,0:T(8,128)(2,1)} %get-tuple-element.10), channel_id=1, source_target_pairs={{8,0},{16,8},{24,16},{0,24},{9,1},{17,9},{25,17},{1,25},{10,2},{18... | collective-permute-start | bytes 884744 | tf_op jit(solution)/shard_map/ppermute | solution.py:26
  56.9 0.0 collective-permute-done.1.far
  56.9 1.0 broadcast_select_fusion
  57.9 1.9 %collective-permute-start.4 = (bf16[1152,128]{1,0:T(8,128)(2,1)}, bf16[1152,128]{1,0:T(8,128)(2,1)S(1)}, u32[]{:S(2)}, u32[]{:S(2)}) collective-permute-start(bf16[1152,128]{1,0:T(8,128)(2,1)} %get-tuple-element.12), channel_id=1, source_target_pairs={{24,0},{0,8},{8,16},{16,24},{25,1},{1,9},{9,17},{17,25},{26,2},{2,... | collective-permute-start | bytes 884744 | tf_op jit(solution)/shard_map/ppermute | solution.py:26
  59.8 4.8 %collective-permute-start.3 = (bf16[1152,128]{1,0:T(8,128)(2,1)}, bf16[1152,128]{1,0:T(8,128)(2,1)S(1)}, u32[]{:S(2)}, u32[]{:S(2)}) collective-permute-start(bf16[1152,128]{1,0:T(8,128)(2,1)} %get-tuple-element.13), channel_id=1, source_target_pairs={{16,0},{24,8},{0,16},{8,24},{17,1},{25,9},{1,17},{9,25},{18,2},{26... | collective-permute-start | bytes 884744 | tf_op jit(solution)/shard_map/ppermute | solution.py:26
  64.7 0.0 collective-permute-done.7.l3
  64.7 1.9 %collective-permute-start.2 = (bf16[1152,128]{1,0:T(8,128)(2,1)}, bf16[1152,128]{1,0:T(8,128)(2,1)}, u32[]{:S(2)}, u32[]{:S(2)}) collective-permute-start(bf16[1152,128]{1,0:T(8,128)(2,1)} %get-tuple-element.14), channel_id=1, source_target_pairs={{8,0},{16,8},{24,16},{0,24},{9,1},{17,9},{25,17},{1,25},{10,2},{18... | collective-permute-start | bytes 884744 | tf_op jit(solution)/shard_map/ppermute | solution.py:26
  67.9 0.0 collective-permute-done.6.l2
  67.9 3.6 %collective-permute-done.5.l1 = bf16[1152,128]{1,0:T(8,128)(2,1)S(1)} collective-permute-done((bf16[1152,128]{1,0:T(8,128)(2,1)}, bf16[1152,128]{1,0:T(8,128)(2,1)S(1)}, u32[]{:S(2)}, u32[]{:S(2)}) %collective-permute-start.5) | collective-permute-done | bytes 294944 | tf_op jit(solution)/shard_map/ppermute | solution.py:26
  71.5 0.0 all-to-all-done.1
  71.6 0.8 copy-done.3
  72.3 1.6 %shard_map.70.near = f32[1152,512]{1,0:T(8,128)S(1)} custom-call(f32[1]{0:T(128)} %copy.7.scale, f32[1]{0:T(128)S(6)} %copy.8.bias, f32[16,512]{1,0:T(8,128)S(1)} %copy-done.3, bf16[2,1152,128]{2,1,0:T(8,128)(2,1)S(1)} %bitcast.21, bf16[1152,128]{1,0:T(8,128)(2,1)S(1)} %collective-permute-done.5.l1, bf16[1152,128]{1,0:T(8,128)(2,1)S(1)} %collective-permute-done.6.l2, ...), custom_call_target="tpu_custom_call" | custom-call | flops 1207959552 | bytes 5242880 | tf_op jit(solution)/shard_map/pallas_call | solution.py:181
  73.9 0.0 collective-permute-done.4.h3
  73.9 0.0 collective-permute-done.3.h2
  73.9 8.0 %collective-permute-done.2.h1 = bf16[1152,128]{1,0:T(8,128)(2,1)} collective-permute-done((bf16[1152,128]{1,0:T(8,128)(2,1)}, bf16[1152,128]{1,0:T(8,128)(2,1)}, u32[]{:S(2)}, u32[]{:S(2)}) %collective-permute-start.2) | collective-permute-done | bytes 294944 | tf_op jit(solution)/shard_map/ppermute | solution.py:26
  81.9 2.6 %shard_map.71 = bf16[8,288,256]{2,1,0:T(8,128)(2,1)S(1)} custom-call(f32[1]{0:T(128)} %copy.7.scale, f32[1]{0:T(128)S(6)} %copy.8.bias, bf16[2,1152,128]{2,1,0:T(8,128)(2,1)S(1)} %bitcast.22, bf16[1152,128]{1,0:T(8,128)(2,1)S(1)} %collective-permute-done.1.far, bf16[1152,128]{1,0:T(8,128)(2,1)} %collective-permute-done.2.h1, ...), custom_call_target="tpu_custom_call" | custom-call | flops 1207959552 | bytes 5242880 | tf_op jit(solution)/shard_map/pallas_call | solution.py:189
  84.5 32.4 %all_to_all.16 = bf16[8,288,256]{2,1,0:T(8,128)(2,1)S(1)} all-to-all(bf16[8,288,256]{2,1,0:T(8,128)(2,1)S(1)} %shard_map.71), channel_id=1, replica_groups=mesh['row'=8,'level'=2,'x'=4,'core'=2,'width'=4] {'core','width'}, dimensions={0} | all-to-all | bytes 2359296 | tf_op jit(solution)/shard_map/all_to_all | solution.py:197
  116.8 0.2 convert_element_type.3
  117.1 1.0 fusion.1
  (6 shorter events, 0.1 us)
Async XLA Ops:
  0.6 0.9 copy-start
  1.5 0.9 copy-start.1
  2.5 0.7 copy-start.4
  3.2 3.8 %collective-permute-start = (bf16[304,512]{1,0:T(8,128)(2,1)S(1)}, bf16[304,512]{1,0:T(8,128)(2,1)S(1)}, u32[]{:S(2)}, u32[]{:S(2)}) collective-permute-start(bf16[304,512]{1,0:T(8,128)(2,1)S(1)} %shard_map.68.mine), channel_id=1, source_target_pairs={{0,4},{4,0},{1,5},{5,1},{2,6},{6,2},{3,7},{7,3},{8,12},{12,8},{9,1... | collective-permute-start | bytes 933896 | tf_op jit(solution)/shard_map/ppermute | solution.py:22
  8.2 24.1 %copy-start.2 = (f32[16,512]{1,0:T(8,128)}, f32[16,512]{1,0:T(8,128)S(1)}, u32[]{:S(2)}) copy-start(f32[16,512]{1,0:T(8,128)S(1)} %get-tuple-element.7.marks) | copy-start | bytes 98308
  32.3 39.3 %all-to-all-start.1 = ((bf16[4,288,512]{2,1,0:T(8,128)(2,1)}), bf16[4,288,512]{2,1,0:T(8,128)(2,1)S(1)}, u32[]{:S(2)}, u32[]{:S(2)}) async-start(bf16[4,288,512]{2,1,0:T(8,128)(2,1)} %get-tuple-element.6), calls=%async_computation.1 | async-start | bytes 2359296 | tf_op jit(solution)/shard_map/all_to_all | solution.py:166
  36.6 20.4 %collective-permute-start.1 = (bf16[1152,128]{1,0:T(8,128)(2,1)S(1)}, bf16[1152,128]{1,0:T(8,128)(2,1)S(1)}, u32[]{:S(2)}, u32[]{:S(2)}) collective-permute-start(bf16[1152,128]{1,0:T(8,128)(2,1)S(1)} %get-tuple-element.11), channel_id=1, source_target_pairs={{0,64},{32,480},{64,128},{96,32},{128,192},{160,96},{192,256},{224... | collective-permute-start | bytes 884744 | tf_op jit(solution)/shard_map/ppermute | solution.py:168
  47.3 17.4 %collective-permute-start.7 = (bf16[1152,128]{1,0:T(8,128)(2,1)}, bf16[1152,128]{1,0:T(8,128)(2,1)S(1)}, u32[]{:S(2)}, u32[]{:S(2)}) collective-permute-start(bf16[1152,128]{1,0:T(8,128)(2,1)} %get-tuple-element.10), channel_id=1, source_target_pairs={{24,0},{0,8},{8,16},{16,24},{25,1},{1,9},{9,17},{17,25},{26,2},{2,... | collective-permute-start | bytes 884744 | tf_op jit(solution)/shard_map/ppermute | solution.py:26
  50.4 17.5 %collective-permute-start.6 = (bf16[1152,128]{1,0:T(8,128)(2,1)}, bf16[1152,128]{1,0:T(8,128)(2,1)S(1)}, u32[]{:S(2)}, u32[]{:S(2)}) collective-permute-start(bf16[1152,128]{1,0:T(8,128)(2,1)} %get-tuple-element.10), channel_id=1, source_target_pairs={{16,0},{24,8},{0,16},{8,24},{17,1},{25,9},{1,17},{9,25},{18,2},{26... | collective-permute-start | bytes 884744 | tf_op jit(solution)/shard_map/ppermute | solution.py:26
  53.1 18.4 %collective-permute-start.5 = (bf16[1152,128]{1,0:T(8,128)(2,1)}, bf16[1152,128]{1,0:T(8,128)(2,1)S(1)}, u32[]{:S(2)}, u32[]{:S(2)}) collective-permute-start(bf16[1152,128]{1,0:T(8,128)(2,1)} %get-tuple-element.10), channel_id=1, source_target_pairs={{8,0},{16,8},{24,16},{0,24},{9,1},{17,9},{25,17},{1,25},{10,2},{18... | collective-permute-start | bytes 884744 | tf_op jit(solution)/shard_map/ppermute | solution.py:26
  57.9 16.0 %collective-permute-start.4 = (bf16[1152,128]{1,0:T(8,128)(2,1)}, bf16[1152,128]{1,0:T(8,128)(2,1)S(1)}, u32[]{:S(2)}, u32[]{:S(2)}) collective-permute-start(bf16[1152,128]{1,0:T(8,128)(2,1)} %get-tuple-element.12), channel_id=1, source_target_pairs={{24,0},{0,8},{8,16},{16,24},{25,1},{1,9},{9,17},{17,25},{26,2},{2,... | collective-permute-start | bytes 884744 | tf_op jit(solution)/shard_map/ppermute | solution.py:26
  59.8 14.1 %collective-permute-start.3 = (bf16[1152,128]{1,0:T(8,128)(2,1)}, bf16[1152,128]{1,0:T(8,128)(2,1)S(1)}, u32[]{:S(2)}, u32[]{:S(2)}) collective-permute-start(bf16[1152,128]{1,0:T(8,128)(2,1)} %get-tuple-element.13), channel_id=1, source_target_pairs={{16,0},{24,8},{0,16},{8,24},{17,1},{25,9},{1,17},{9,25},{18,2},{26... | collective-permute-start | bytes 884744 | tf_op jit(solution)/shard_map/ppermute | solution.py:26
  64.7 17.2 %collective-permute-start.2 = (bf16[1152,128]{1,0:T(8,128)(2,1)}, bf16[1152,128]{1,0:T(8,128)(2,1)}, u32[]{:S(2)}, u32[]{:S(2)}) collective-permute-start(bf16[1152,128]{1,0:T(8,128)(2,1)} %get-tuple-element.14), channel_id=1, source_target_pairs={{8,0},{16,8},{24,16},{0,24},{9,1},{17,9},{25,17},{1,25},{10,2},{18... | collective-permute-start | bytes 884744 | tf_op jit(solution)/shard_map/ppermute | solution.py:26
  71.5 0.8 copy-start.3

commit v4 on v3

--- a/solution.py
+++ b/solution.py
@@ -12,7 +12,6 @@
 BF16 = jnp.bfloat16
 F32 = jnp.float32
 SMEM = pl.BlockSpec(memory_space=pltpu.SMEM)
-HBM = pl.BlockSpec(memory_space=pltpu.HBM)
 LOCAL = pl.BlockSpec(memory_space=pltpu.VMEM)
 PIECES = 2 * LINE
 MARKS = 16
@@ -33,44 +32,30 @@
     return route
 
 
-def pack_kernel(image, text, matches, out, sems):
-    features, rows = image.shape
-    copies = [
-        pltpu.make_async_copy(
-            source, out.at[pl.ds(0, features), pl.ds(i * rows, rows)], sems.at[i]
-        )
-        for i, source in enumerate((image, text))
-    ]
-    for copy in copies:
-        copy.start()
-    marks = jnp.broadcast_to(matches[...], (MARKS, rows)).astype(F32).astype(BF16)
-    out[features:, :rows] = marks
-    out[features:, rows:] = marks
-    for copy in copies:
-        copy.wait()
-
-
-def deal_kernel(mine, other, chunks, spread, marks):
-    rows = spread.shape[2] // CORES
-    features = spread.shape[1]
+def deal_kernel(mine, other, chunks):
     n = chunks.shape[2]
     first = lax.axis_index("core") == 0
-    image, text = mine[:features, :rows], mine[:features, rows:]
-    other_image, other_text = other[:features, :rows], other[:features, rows:]
     parts = (
-        jnp.where(first, image, other_text),
-        jnp.where(first, other_image, text),
+        jnp.where(first, mine[...], other[...]),
+        jnp.where(first, other[...], mine[...]),
     )
     for i in range(LEVELS * WIDTH):
         q = i % WIDTH
         chunks[i] = parts[q // 2][:, (q % 2) * n : (q % 2 + 1) * n]
-    own_marks, other_marks = mine[features:, :rows].astype(F32), other[features:, :rows].astype(F32)
-    marks[:, :rows] = jnp.where(first, own_marks, other_marks)
-    marks[:, rows:] = jnp.where(first, other_marks, own_marks)
-    full = (jnp.where(first, text, other_image), jnp.where(first, other_text, image))
+
+
+def spread_kernel(mine, matches, other, spread, marks):
+    features, rows = mine.shape
+    first = lax.axis_index("core") == 0
+    own, others = mine[...], other[:features, :]
+    full = (jnp.where(first, own, others), jnp.where(first, others, own))
     for i in range(WIDTH):
         spread[i, :, :rows] = full[0]
         spread[i, :, rows:] = full[1]
+    own_marks = jnp.broadcast_to(matches[...].astype(F32), (MARKS, rows))
+    other_marks = other[features:, :].astype(F32)
+    marks[:, :rows] = jnp.where(first, own_marks, other_marks)
+    marks[:, rows:] = jnp.where(first, other_marks, own_marks)
 
 
 def weighed(pieces, held, scale, bias):
@@ -78,6 +63,13 @@
         pieces, held[...], (((0,), (0,)), ((), ())), preferred_element_type=F32
     )
     return jax.nn.sigmoid(scale[0] * logits + bias[0])
+
+
+def halo_kernel(pair, far, *outs):
+    x, level = lax.axis_index("x"), lax.axis_index("level")
+    for d, out in enumerate(outs, 1):
+        higher = lax.rem(x + d, LINE) > x
+        out[...] = jnp.where(higher == (level == 0), pair[...], far[...])
 
 
 def label_of(marks, n):
@@ -131,7 +123,6 @@
 
 
 def per_device(images, texts, matches, scale, shift_bias):
-    x = lax.axis_index("x")
     level = lax.axis_index("level")
     features, rows = images.shape[1], images.shape[0]
     span = CORES * rows
@@ -139,26 +130,30 @@
     whole = WIDTH * features
 
     image, text = images.T, texts.T
-    mine = pl.pallas_call(
-        pack_kernel,
-        out_shape=jax.ShapeDtypeStruct((features + MARKS, CORES * rows), BF16),
-        in_specs=[HBM, HBM, LOCAL],
+    first = lax.axis_index("core") == 0
+    to_deal, to_spread = jnp.where(first, image, text), jnp.where(first, text, image)
+    noted = jnp.broadcast_to(matches.astype(BF16), (MARKS, rows))
+    to_deal, to_spread = lax.optimization_barrier((to_deal, to_spread))
+    dealt_other = swap_cores(to_spread)
+    spread_other = swap_cores(jnp.concatenate([to_deal, noted], 0))
+    params = pltpu.CompilerParams(vmem_limit_bytes=6 << 20)
+    chunks = pl.pallas_call(
+        deal_kernel,
+        out_shape=jax.ShapeDtypeStruct((LEVELS * WIDTH, features, quarter), BF16),
+        in_specs=[LOCAL] * 2,
         out_specs=LOCAL,
-        scratch_shapes=[pltpu.SemaphoreType.DMA((2,))],
-        compiler_params=pltpu.CompilerParams(vmem_limit_bytes=6 << 20),
-    )(image, text, matches)
-    other = swap_cores(mine)
-    chunks, spread, marks = pl.pallas_call(
-        deal_kernel,
+        compiler_params=params,
+    )(to_deal, dealt_other)
+    spread, marks = pl.pallas_call(
+        spread_kernel,
         out_shape=[
-            jax.ShapeDtypeStruct((LEVELS * WIDTH, features, quarter), BF16),
             jax.ShapeDtypeStruct((WIDTH, features, span), BF16),
             jax.ShapeDtypeStruct((MARKS, span), F32),
         ],
-        in_specs=[LOCAL] * 2,
-        out_specs=[LOCAL] * 3,
-        compiler_params=pltpu.CompilerParams(vmem_limit_bytes=6 << 20),
-    )(mine, other)
+        in_specs=[LOCAL] * 3,
+        out_specs=[LOCAL] * 2,
+        compiler_params=params,
+    )(to_spread, matches, spread_other)
     dealt = lax.all_to_all(chunks, ("level", "width"), 0, 0).reshape(LEVELS, whole, quarter)
     own = lax.dynamic_index_in_dim(dealt, level, 0, False)
     pair = lax.dynamic_index_in_dim(dealt, 1 - level, 0, False)
@@ -168,11 +163,16 @@
     far = lax.ppermute(pair, ("row", "level"), far_route(lax.axis_size("row")))
     l1, l2, l3 = (along_line(own, d) for d in (1, 2, 3))
 
-    def to_send(d):
-        higher = (x + d) % LINE > x
-        return jnp.where(higher == (level == 0), pair, far)
-
-    h1, h2, h3 = (along_line(to_send(LINE - d), d) for d in (1, 2, 3))
+    piece = jax.ShapeDtypeStruct((whole, quarter), BF16)
+    s1, s2, s3 = pl.pallas_call(
+        halo_kernel,
+        out_shape=[piece] * 3,
+        in_specs=[LOCAL] * 2,
+        out_specs=[LOCAL] * 3,
+        compiler_params=params,
+        cost_estimate=pl.CostEstimate(flops=10 * 10**9, bytes_accessed=2 << 20, transcendentals=0),
+    )(pair, far)
+    h1, h2, h3 = along_line(s3, 1), along_line(s2, 2), along_line(s1, 3)
 
     cost = pl.CostEstimate(
         flops=2 * whole * PIECES * quarter * span, bytes_accessed=5 << 20, transcendentals=0

time: 119 us -> 116 us (0.975)
  blocking collectives: 56.5 us -> 34.5 us
  waiting for transfers between devices: 12.8 us -> 23.6 us
  starting transfers between devices: 35.1 us -> 44.3 us
  local copies, waits for them, and re-layouts: 4.01 us -> 1.42 us
  Pallas kernels: 5.36 us -> 7.41 us
    all_to_all x1 -> x0, blocking collectives: 24.1 us -> none  [per_device(): lax.all_to_all(chunks, ('level', 'width'), 0, 0)]
    all_to_all x0 -> x1, waiting for transfers between devices: none -> 11.9 us  [per_device(): lax.all_to_all(chunks, ('level', 'width'), 0, 0)]
    all_to_all x0 -> x1, starting transfers between devices: none -> 6.99 us  [per_device(): lax.all_to_all(chunks, ('level', 'width'), 0, 0)]
    ppermute x1 -> x2, starting transfers between devices: 2.58 us -> 5.42 us  [swap_cores(): return lax.ppermute(block, 'core', [(0, 1), (1, 0)])]
    all_to_all x1, blocking collectives: 32.4 us -> 34.5 us  [per_device(): terms = lax.all_to_all(partial, ('core', 'width'), 0, 0).astype(F32)]
    pallas_call x2 -> x3, Pallas kernels: 1.22 us -> 3.26 us  [the longest x1 1.16 us: per_device(): pl.pallas_call(spread_kernel, out_shape=[jax.ShapeDtypeStruct((WIDTH, fea...]
    unnamed x10 -> x6, local copies, waits for them, and re-layouts: 3.25 us -> 1.37 us
    ppermute x6, waiting for transfers between devices: 11.6 us -> 9.72 us  [along_line(): lax.ppermute(block, 'x', [((i + distance) % LINE, i) for i in range(LINE)])]
  transfers between devices with their start and end apart: 9 -> 11, of which waited for: 3 -> 6; matrix products, arithmetic and copies ran while one was open for 1% -> 0% of each run, Pallas kernels for 1% -> 3%
where the time goes in v4:
time: 116 us
  starting transfers between devices  44.3 us (38%)
  blocking collectives  34.5 us (30%)
  waiting for transfers between devices  23.6 us (20%)
  Pallas kernels  7.41 us (6%)
  other arithmetic  2.21 us (2%)
  between operations  2.1 us (2%)
  local copies, waits for them, and re-layouts  1.42 us (1%)
    all_to_all x1, blocking collectives, per_device(): terms = lax.all_to_all(partial, ('core', 'width'), 0, 0).astype(F32)  34.5 us
    ppermute x6, starting transfers between devices, along_line(): lax.ppermute(block, 'x', [((i + distance) % LINE, i) for i in range(LINE)])  17.7 us
    all_to_all x1, waiting for transfers between devices, per_device(): lax.all_to_all(chunks, ('level', 'width'), 0, 0)  11.9 us
    ppermute x1, starting transfers between devices, per_device(): far = lax.ppermute(pair, ('row', 'level'), far_route(lax.axis_size('row')))  10.7 us
    ppermute x6, waiting for transfers between devices, along_line(): lax.ppermute(block, 'x', [((i + distance) % LINE, i) for i in range(LINE)])  9.72 us
    all_to_all x1, starting transfers between devices, per_device(): lax.all_to_all(chunks, ('level', 'width'), 0, 0)  6.99 us
    ppermute x2, starting transfers between devices, swap_cores(): return lax.ppermute(block, 'core', [(0, 1), (1, 0)])  5.42 us
    all_to_all x1, starting transfers between devices, per_device(): held = lax.all_to_all(spread, 'width', 0, 0)  3.53 us
  transfers between devices with their start and end apart: 11, of which 6 were waited for; matrix products, arithmetic and copies ran while one was open for 0% of the time, Pallas kernels for 3%

profile of v4, /device:TPU:11, one launch (start us, length us, event | category | flops | bytes accessed | tf_op | source)
XLA Modules:
  0.0 115.5 jit_solution(4162364777371497137)
XLA Ops:
  0.6 1.0 select_bitcast_fusion
  1.6 0.0 copy-start.2
  1.7 2.6 %collective-permute-start = (bf16[288,256]{1,0:T(8,128)(2,1)S(1)}, bf16[288,256]{1,0:T(8,128)(2,1)S(1)}, u32[]{:S(2)}, u32[]{:S(2)}) collective-permute-start(bf16[288,256]{1,0:T(8,128)(2,1)S(1)} %get-tuple-element.10.mine), channel_id=1, source_target_pairs={{0,4},{4,0},{1,5},{5,1},{2,6},{6,2},{3,7},{7,3},{8,12},{12,8},{9,1... | collective-permute-start | bytes 442376 | tf_op jit(solution)/shard_map/ppermute | solution.py:21
  4.2 1.0 collective-permute-done.other
  5.2 0.9 shard_map.68
  6.2 7.0 %all-to-all-start = ((bf16[8,288,128]{2,1,0:T(8,128)(2,1)}), bf16[8,288,128]{2,1,0:T(8,128)(2,1)S(1)}, u32[]{:S(2)}, u32[]{:S(2)}) async-start(bf16[8,288,128]{2,1,0:T(8,128)(2,1)} %shard_map.68), calls=%async_computation | async-start | bytes 1179648 | tf_op jit(solution)/shard_map/all_to_all | solution.py:157
  13.2 2.8 %collective-permute-start.5 = (bf16[304,256]{1,0:T(8,128)(2,1)S(1)}, bf16[304,256]{1,0:T(8,128)(2,1)S(1)}, u32[]{:S(2)}, u32[]{:S(2)}) collective-permute-start(bf16[304,256]{1,0:T(8,128)(2,1)S(1)} %pad_maximum_fusion), channel_id=1, source_target_pairs={{0,4},{4,0},{1,5},{5,1},{2,6},{6,2},{3,7},{7,3},{8,12},{12,8},{9,1... | collective-permute-start | bytes 466952 | tf_op jit(solution)/shard_map/ppermute | solution.py:21
  16.1 1.0 collective-permute-done.5.other
  17.1 1.2 %shard_map.70 = (bf16[4,288,512]{2,1,0:T(8,128)(2,1)}, f32[16,512]{1,0:T(8,128)S(1)}) custom-call(bf16[288,256]{1,0:T(8,128)(2,1)S(1)} %get-tuple-element.10.mine, s32[1,256]{1,0:T(1,128)S(1)} %copy-done.2, bf16[304,256]{1,0:T(8,128)(2,1)S(1)} %collective-permute-done.5.other), custom_call_target="tpu_custom_call" | custom-call | tf_op jit(solution)/shard_map/pallas_call | solution.py:147
  18.2 0.6 copy-done
  18.8 11.9 %all-to-all-done = bf16[8,288,128]{2,1,0:T(8,128)(2,1)S(1)} async-done(((bf16[8,288,128]{2,1,0:T(8,128)(2,1)}), bf16[8,288,128]{2,1,0:T(8,128)(2,1)S(1)}, u32[]{:S(2)}, u32[]{:S(2)}) %all-to-all-start) | async-done | bytes 589856 | tf_op jit(solution)/shard_map/all_to_all | solution.py:157
  30.7 3.5 %all-to-all-start.1 = ((bf16[4,288,512]{2,1,0:T(8,128)(2,1)}), bf16[4,288,512]{2,1,0:T(8,128)(2,1)S(1)}, u32[]{:S(2)}, u32[]{:S(2)}) async-start(bf16[4,288,512]{2,1,0:T(8,128)(2,1)} %get-tuple-element.14), calls=%async_computation.1 | async-start | bytes 2359296 | tf_op jit(solution)/shard_map/all_to_all | solution.py:161
  34.3 10.7 %collective-permute-start.1 = (bf16[1152,128]{1,0:T(8,128)(2,1)S(1)}, bf16[1152,128]{1,0:T(8,128)(2,1)S(1)}, u32[]{:S(2)}, u32[]{:S(2)}) collective-permute-start(bf16[1152,128]{1,0:T(8,128)(2,1)S(1)} %get-tuple-element.19.pair), channel_id=1, source_target_pairs={{0,64},{32,480},{64,128},{96,32},{128,192},{160,96},{192,256},{224... | collective-permute-start | bytes 884744 | tf_op jit(solution)/shard_map/ppermute | solution.py:163
  45.0 3.1 %collective-permute-start.8 = (bf16[1152,128]{1,0:T(8,128)(2,1)S(1)}, bf16[1152,128]{1,0:T(8,128)(2,1)S(1)}, u32[]{:S(2)}, u32[]{:S(2)}) collective-permute-start(bf16[1152,128]{1,0:T(8,128)(2,1)S(1)} %get-tuple-element.18), channel_id=1, source_target_pairs={{24,0},{0,8},{8,16},{16,24},{25,1},{1,9},{9,17},{17,25},{26,2},{2,... | collective-permute-start | bytes 884744 | tf_op jit(solution)/shard_map/ppermute | solution.py:25
  48.1 2.7 %collective-permute-start.7 = (bf16[1152,128]{1,0:T(8,128)(2,1)S(1)}, bf16[1152,128]{1,0:T(8,128)(2,1)S(1)}, u32[]{:S(2)}, u32[]{:S(2)}) collective-permute-start(bf16[1152,128]{1,0:T(8,128)(2,1)S(1)} %get-tuple-element.18), channel_id=1, source_target_pairs={{16,0},{24,8},{0,16},{8,24},{17,1},{25,9},{1,17},{9,25},{18,2},{26... | collective-permute-start | bytes 884744 | tf_op jit(solution)/shard_map/ppermute | solution.py:25
  50.8 3.8 %collective-permute-start.6 = (bf16[1152,128]{1,0:T(8,128)(2,1)S(1)}, bf16[1152,128]{1,0:T(8,128)(2,1)S(1)}, u32[]{:S(2)}, u32[]{:S(2)}) collective-permute-start(bf16[1152,128]{1,0:T(8,128)(2,1)S(1)} %get-tuple-element.18), channel_id=1, source_target_pairs={{8,0},{16,8},{24,16},{0,24},{9,1},{17,9},{25,17},{1,25},{10,2},{18... | collective-permute-start | bytes 884744 | tf_op jit(solution)/shard_map/ppermute | solution.py:25
  54.6 0.0 collective-permute-done.1.far
  54.6 1.2 %shard_map.69 = (bf16[1152,128]{1,0:T(8,128)(2,1)}, bf16[1152,128]{1,0:T(8,128)(2,1)}, bf16[1152,128]{1,0:T(8,128)(2,1)}) custom-call(bf16[1152,128]{1,0:T(8,128)(2,1)S(1)} %get-tuple-element.19.pair, bf16[1152,128]{1,0:T(8,128)(2,1)S(1)} %collective-permute-done.1.far), custom_call_target="tpu_custom_call" | custom-call | flops 10000000000 | bytes 2097152 | tf_op jit(solution)/shard_map/pallas_call | solution.py:167
  55.8 3.0 %collective-permute-start.2 = (bf16[1152,128]{1,0:T(8,128)(2,1)}, bf16[1152,128]{1,0:T(8,128)(2,1)S(1)}, u32[]{:S(2)}, u32[]{:S(2)}) collective-permute-start(bf16[1152,128]{1,0:T(8,128)(2,1)} %get-tuple-element.11), channel_id=1, source_target_pairs={{8,0},{16,8},{24,16},{0,24},{9,1},{17,9},{25,17},{1,25},{10,2},{18... | collective-permute-start | bytes 884744 | tf_op jit(solution)/shard_map/ppermute | solution.py:25
  58.9 1.9 %collective-permute-start.3 = (bf16[1152,128]{1,0:T(8,128)(2,1)}, bf16[1152,128]{1,0:T(8,128)(2,1)S(1)}, u32[]{:S(2)}, u32[]{:S(2)}) collective-permute-start(bf16[1152,128]{1,0:T(8,128)(2,1)} %get-tuple-element.12), channel_id=1, source_target_pairs={{16,0},{24,8},{0,16},{8,24},{17,1},{25,9},{1,17},{9,25},{18,2},{26... | collective-permute-start | bytes 884744 | tf_op jit(solution)/shard_map/ppermute | solution.py:25
  60.8 0.0 collective-permute-done.8.l3
  60.8 3.1 %collective-permute-start.4 = (bf16[1152,128]{1,0:T(8,128)(2,1)}, bf16[1152,128]{1,0:T(8,128)(2,1)}, u32[]{:S(2)}, u32[]{:S(2)}) collective-permute-start(bf16[1152,128]{1,0:T(8,128)(2,1)} %get-tuple-element.13), channel_id=1, source_target_pairs={{24,0},{0,8},{8,16},{16,24},{25,1},{1,9},{9,17},{17,25},{26,2},{2,... | collective-permute-start | bytes 884744 | tf_op jit(solution)/shard_map/ppermute | solution.py:25
  65.2 1.5 %collective-permute-done.6.l1 = bf16[1152,128]{1,0:T(8,128)(2,1)S(1)} collective-permute-done((bf16[1152,128]{1,0:T(8,128)(2,1)S(1)}, bf16[1152,128]{1,0:T(8,128)(2,1)S(1)}, u32[]{:S(2)}, u32[]{:S(2)}) %collective-permute-start.6) | collective-permute-done | bytes 294944 | tf_op jit(solution)/shard_map/ppermute | solution.py:25
  66.7 0.8 copy-done.1
  67.5 1.6 %shard_map.71.near = f32[1152,512]{1,0:T(8,128)S(1)} custom-call(f32[1]{0:T(128)} %copy.7.scale, f32[1]{0:T(128)S(6)} %copy.8.bias, f32[16,512]{1,0:T(8,128)S(1)} %copy-done.1, bf16[2,1152,128]{2,1,0:T(8,128)(2,1)S(1)} %bitcast.23, bf16[1152,128]{1,0:T(8,128)(2,1)S(1)} %collective-permute-done.6.l1, bf16[1152,128]{1,0:T(8,128)(2,1)S(1)} %collective-permute-done.7.l2, ...), custom_call_target="tpu_custom_call" | custom-call | flops 1207959552 | bytes 5242880 | tf_op jit(solution)/shard_map/pallas_call | solution.py:181
  69.1 6.2 %collective-permute-done.2.h1 = bf16[1152,128]{1,0:T(8,128)(2,1)S(1)} collective-permute-done((bf16[1152,128]{1,0:T(8,128)(2,1)}, bf16[1152,128]{1,0:T(8,128)(2,1)S(1)}, u32[]{:S(2)}, u32[]{:S(2)}) %collective-permute-start.2) | collective-permute-done | bytes 294944 | tf_op jit(solution)/shard_map/ppermute | solution.py:25
  75.3 2.0 %collective-permute-done.3.h2 = bf16[1152,128]{1,0:T(8,128)(2,1)S(1)} collective-permute-done((bf16[1152,128]{1,0:T(8,128)(2,1)}, bf16[1152,128]{1,0:T(8,128)(2,1)S(1)}, u32[]{:S(2)}, u32[]{:S(2)}) %collective-permute-start.3) | collective-permute-done | bytes 294944 | tf_op jit(solution)/shard_map/ppermute | solution.py:25
  77.3 0.0 collective-permute-done.4.h3
  77.3 2.6 %shard_map.72 = bf16[8,288,256]{2,1,0:T(8,128)(2,1)S(1)} custom-call(f32[1]{0:T(128)} %copy.7.scale, f32[1]{0:T(128)S(6)} %copy.8.bias, bf16[2,1152,128]{2,1,0:T(8,128)(2,1)S(1)} %bitcast.24, bf16[1152,128]{1,0:T(8,128)(2,1)S(1)} %collective-permute-done.1.far, bf16[1152,128]{1,0:T(8,128)(2,1)S(1)} %collective-permute-done.2.h1, ...), custom_call_target="tpu_custom_call" | custom-call | flops 1207959552 | bytes 5242880 | tf_op jit(solution)/shard_map/pallas_call | solution.py:189
  79.8 34.5 %all_to_all.15 = bf16[8,288,256]{2,1,0:T(8,128)(2,1)S(1)} all-to-all(bf16[8,288,256]{2,1,0:T(8,128)(2,1)S(1)} %shard_map.72), channel_id=1, replica_groups=mesh['row'=8,'level'=2,'x'=4,'core'=2,'width'=4] {'core','width'}, dimensions={0} | all-to-all | bytes 2359296 | tf_op jit(solution)/shard_map/all_to_all | solution.py:197
  114.3 0.2 convert_element_type.7
  114.5 1.0 fusion.1
  (9 shorter events, 0.1 us)
Async XLA Ops:
  1.6 11.5 %copy-start.2 = (s32[1,256]{1,0:T(1,128)S(1)}, s32[1,256]{1,0:T(1,128)}, u32[]{:S(2)}) copy-start(s32[1,256]{1,0:T(1,128)} %matches.1) | copy-start | bytes 3076
  1.7 3.6 %collective-permute-start = (bf16[288,256]{1,0:T(8,128)(2,1)S(1)}, bf16[288,256]{1,0:T(8,128)(2,1)S(1)}, u32[]{:S(2)}, u32[]{:S(2)}) collective-permute-start(bf16[288,256]{1,0:T(8,128)(2,1)S(1)} %get-tuple-element.10.mine), channel_id=1, source_target_pairs={{0,4},{4,0},{1,5},{5,1},{2,6},{6,2},{3,7},{7,3},{8,12},{12,8},{9,1... | collective-permute-start | bytes 442376 | tf_op jit(solution)/shard_map/ppermute | solution.py:21
  6.2 24.5 %all-to-all-start = ((bf16[8,288,128]{2,1,0:T(8,128)(2,1)}), bf16[8,288,128]{2,1,0:T(8,128)(2,1)S(1)}, u32[]{:S(2)}, u32[]{:S(2)}) async-start(bf16[8,288,128]{2,1,0:T(8,128)(2,1)} %shard_map.68), calls=%async_computation | async-start | bytes 1179648 | tf_op jit(solution)/shard_map/all_to_all | solution.py:157
  13.2 3.8 %collective-permute-start.5 = (bf16[304,256]{1,0:T(8,128)(2,1)S(1)}, bf16[304,256]{1,0:T(8,128)(2,1)S(1)}, u32[]{:S(2)}, u32[]{:S(2)}) collective-permute-start(bf16[304,256]{1,0:T(8,128)(2,1)S(1)} %pad_maximum_fusion), channel_id=1, source_target_pairs={{0,4},{4,0},{1,5},{5,1},{2,6},{6,2},{3,7},{7,3},{8,12},{12,8},{9,1... | collective-permute-start | bytes 466952 | tf_op jit(solution)/shard_map/ppermute | solution.py:21
  18.2 0.6 copy-start
  30.7 36.0 %all-to-all-start.1 = ((bf16[4,288,512]{2,1,0:T(8,128)(2,1)}), bf16[4,288,512]{2,1,0:T(8,128)(2,1)S(1)}, u32[]{:S(2)}, u32[]{:S(2)}) async-start(bf16[4,288,512]{2,1,0:T(8,128)(2,1)} %get-tuple-element.14), calls=%async_computation.1 | async-start | bytes 2359296 | tf_op jit(solution)/shard_map/all_to_all | solution.py:161
  34.3 20.3 %collective-permute-start.1 = (bf16[1152,128]{1,0:T(8,128)(2,1)S(1)}, bf16[1152,128]{1,0:T(8,128)(2,1)S(1)}, u32[]{:S(2)}, u32[]{:S(2)}) collective-permute-start(bf16[1152,128]{1,0:T(8,128)(2,1)S(1)} %get-tuple-element.19.pair), channel_id=1, source_target_pairs={{0,64},{32,480},{64,128},{96,32},{128,192},{160,96},{192,256},{224... | collective-permute-start | bytes 884744 | tf_op jit(solution)/shard_map/ppermute | solution.py:163
  45.0 15.8 %collective-permute-start.8 = (bf16[1152,128]{1,0:T(8,128)(2,1)S(1)}, bf16[1152,128]{1,0:T(8,128)(2,1)S(1)}, u32[]{:S(2)}, u32[]{:S(2)}) collective-permute-start(bf16[1152,128]{1,0:T(8,128)(2,1)S(1)} %get-tuple-element.18), channel_id=1, source_target_pairs={{24,0},{0,8},{8,16},{16,24},{25,1},{1,9},{9,17},{17,25},{26,2},{2,... | collective-permute-start | bytes 884744 | tf_op jit(solution)/shard_map/ppermute | solution.py:25
  48.1 17.1 %collective-permute-start.7 = (bf16[1152,128]{1,0:T(8,128)(2,1)S(1)}, bf16[1152,128]{1,0:T(8,128)(2,1)S(1)}, u32[]{:S(2)}, u32[]{:S(2)}) collective-permute-start(bf16[1152,128]{1,0:T(8,128)(2,1)S(1)} %get-tuple-element.18), channel_id=1, source_target_pairs={{16,0},{24,8},{0,16},{8,24},{17,1},{25,9},{1,17},{9,25},{18,2},{26... | collective-permute-start | bytes 884744 | tf_op jit(solution)/shard_map/ppermute | solution.py:25
  50.8 15.9 %collective-permute-start.6 = (bf16[1152,128]{1,0:T(8,128)(2,1)S(1)}, bf16[1152,128]{1,0:T(8,128)(2,1)S(1)}, u32[]{:S(2)}, u32[]{:S(2)}) collective-permute-start(bf16[1152,128]{1,0:T(8,128)(2,1)S(1)} %get-tuple-element.18), channel_id=1, source_target_pairs={{8,0},{16,8},{24,16},{0,24},{9,1},{17,9},{25,17},{1,25},{10,2},{18... | collective-permute-start | bytes 884744 | tf_op jit(solution)/shard_map/ppermute | solution.py:25
  55.8 19.5 %collective-permute-start.2 = (bf16[1152,128]{1,0:T(8,128)(2,1)}, bf16[1152,128]{1,0:T(8,128)(2,1)S(1)}, u32[]{:S(2)}, u32[]{:S(2)}) collective-permute-start(bf16[1152,128]{1,0:T(8,128)(2,1)} %get-tuple-element.11), channel_id=1, source_target_pairs={{8,0},{16,8},{24,16},{0,24},{9,1},{17,9},{25,17},{1,25},{10,2},{18... | collective-permute-start | bytes 884744 | tf_op jit(solution)/shard_map/ppermute | solution.py:25
  58.9 18.4 %collective-permute-start.3 = (bf16[1152,128]{1,0:T(8,128)(2,1)}, bf16[1152,128]{1,0:T(8,128)(2,1)S(1)}, u32[]{:S(2)}, u32[]{:S(2)}) collective-permute-start(bf16[1152,128]{1,0:T(8,128)(2,1)} %get-tuple-element.12), channel_id=1, source_target_pairs={{16,0},{24,8},{0,16},{8,24},{17,1},{25,9},{1,17},{9,25},{18,2},{26... | collective-permute-start | bytes 884744 | tf_op jit(solution)/shard_map/ppermute | solution.py:25
  60.8 16.5 %collective-permute-start.4 = (bf16[1152,128]{1,0:T(8,128)(2,1)}, bf16[1152,128]{1,0:T(8,128)(2,1)}, u32[]{:S(2)}, u32[]{:S(2)}) collective-permute-start(bf16[1152,128]{1,0:T(8,128)(2,1)} %get-tuple-element.13), channel_id=1, source_target_pairs={{24,0},{0,8},{8,16},{16,24},{25,1},{1,9},{9,17},{17,25},{26,2},{2,... | collective-permute-start | bytes 884744 | tf_op jit(solution)/shard_map/ppermute | solution.py:25
  66.7 0.8 copy-start.1

commit v5 on v4

v5 whole, which is shorter than its diff:
```python
import jax
import jax.numpy as jnp
from jax import lax
from jax.experimental import pallas as pl
from jax.experimental.pallas import tpu as pltpu
from jax.sharding import Mesh, PartitionSpec as P

CORES = 2
WIDTH = 4
LEVELS = 2
LINE = 4
BF16 = jnp.bfloat16
F32 = jnp.float32
SMEM = pl.BlockSpec(memory_space=pltpu.SMEM)
LOCAL = pl.BlockSpec(memory_space=pltpu.VMEM)
HBM = pl.BlockSpec(memory_space=pl.ANY)
PIECES = 2 * LINE
MARKS = 16


def swap_cores(block):
    return lax.ppermute(block, "core", [(0, 1), (1, 0)])


def along_line(block, turn):
    return lax.ppermute(block, "x", [(i ^ turn, i) for i in range(LINE)])


def far_route(rows):
    route = []
    for i in range(rows):
        route += [(2 * i, 2 * ((i + 1) % rows)), (2 * i + 1, 2 * ((i - 1) % rows) + 1)]
    return route


def deal_kernel(image, text, chunks, held, sems):
    features, rows = image.shape
    n, half = rows // WIDTH, features // 2
    copies = [
        pltpu.make_async_copy(source, held.at[i], sems.at[i])
        for i, source in enumerate((image, text))
    ]
    for copy in copies:
        copy.start()
    for core in range(CORES):
        copies[core].wait()
        for w in range(WIDTH):
            part = held[core, :, w * n : (w + 1) * n]
            part = jnp.concatenate([part[:half], part[half:]], 1)
            for level in range(LEVELS):
                chunks[(level * CORES + core) * WIDTH + w] = part


def gather_kernel(dealt, own, pair):
    half, n = dealt.shape[1], dealt.shape[2] // 2
    level = lax.axis_index("level")
    for out, at in ((own, level), (pair, 1 - level)):
        for w in range(WIDTH):
            left = dealt[at * CORES * WIDTH + w]
            right = dealt[(at * CORES + 1) * WIDTH + w]
            out[2 * w * half : (2 * w + 1) * half] = jnp.concatenate([left[:, :n], right[:, :n]], 1)
            out[(2 * w + 1) * half : (2 * w + 2) * half] = jnp.concatenate(
                [left[:, n:], right[:, n:]], 1
            )


def spread_kernel(mine, matches, other, spread, marks):
    features, rows = mine.shape
    first = lax.axis_index("core") == 0
    own, others = mine[...], other[:features, :]
    full = (jnp.where(first, own, others), jnp.where(first, others, own))
    for i in range(WIDTH):
        spread[i, :, :rows] = full[0]
        spread[i, :, rows:] = full[1]
    own_marks = jnp.broadcast_to(matches[...].astype(F32), (MARKS, rows))
    other_marks = other[features:, :].astype(F32)
    marks[:, :rows] = jnp.where(first, own_marks, other_marks)
    marks[:, rows:] = jnp.where(first, other_marks, own_marks)


def weighed(pieces, held, scale, bias):
    logits = lax.dot_general(
        pieces, held[...], (((0,), (0,)), ((), ())), preferred_element_type=F32
    )
    return jax.nn.sigmoid(scale[0] * logits + bias[0])


def halo_kernel(pair, far, *outs):
    x, level = lax.axis_index("x"), lax.axis_index("level")
    for turn, out in enumerate(outs, 1):
        higher = (x ^ turn) > x
        out[...] = jnp.where(higher == (level == 0), pair[...], far[...])


def label_of(marks, n):
    span = marks.shape[1]
    rows = span // CORES
    first, w = lax.axis_index("core") == 0, lax.axis_index("width")
    down = lax.broadcasted_iota(jnp.int32, (n, 1), 0)
    lane = lax.broadcasted_iota(jnp.int32, (1, span), 1)
    part = n // CORES
    block, row = down // part, w * part + down % part
    mark = jnp.where(lane == block * rows + row, marks[0:1, :], 0.0)
    have = jnp.where(first, jnp.sum(mark, axis=1, keepdims=True), row.astype(F32))
    goal = jnp.where(first, (lane % rows).astype(F32), marks[0:1, :])
    return ((have == goal) & (lane // rows == block)).astype(F32)


def weighed(pieces, held, scale, bias):
    logits = lax.dot_general(
        pieces, held[...], (((0,), (0,)), ((), ())), preferred_element_type=F32
    )
    return jax.nn.sigmoid(scale[0] * logits + bias[0])


def halo_kernel(pair, far, *outs):
    x, level = lax.axis_index("x"), lax.axis_index("level")
    for turn, out in enumerate(outs, 1):
        higher = (x ^ turn) > x
        out[...] = jnp.where(higher == (level == 0), pair[...], far[...])


def near_kernel(scale, bias, marks, own, l2, l3, l1, held, out):
    n = l1.shape[1]
    pieces = jnp.concatenate([own[...], l1[...], l2[...], l3[...]], 1)
    probs = weighed(pieces, held, scale, bias)
    weights = jnp.concatenate([(probs[:n] - label_of(marks, n)).astype(BF16), probs[n:].astype(BF16)], 0)
    out[...] = jnp.dot(pieces, weights, preferred_element_type=F32)


def far_kernel(scale, bias, pair, far, h2, h1, h3, held, near, out):
    whole, n = h1.shape
    span = held.shape[1]
    rows = span // CORES
    features = whole // WIDTH
    level = lax.axis_index("level")
    side = lax.broadcasted_iota(jnp.int32, (whole, n), 1) < n // CORES
    last = jnp.where(side == (level == 0), pair[...], far[...])
    pieces = jnp.concatenate([last, h1[...], h2[...], h3[...]], 1)
    probs = weighed(pieces, held, scale, bias)
    lane = lax.broadcasted_iota(jnp.int32, (n, span), 1)
    down = lax.broadcasted_iota(jnp.int32, (n, span), 0)
    met = lane // rows != down // (n // CORES)
    weights = jnp.concatenate(
        [
            jnp.where(met, probs[:n], 0.0).astype(BF16),
            probs[n:].astype(BF16),
        ],
        0,
    )
    for to in range(WIDTH):
        at = slice(to * features, (to + 1) * features)
        total = near[at, :] + jnp.dot(pieces[at], weights, preferred_element_type=F32)
        total = total.astype(BF16)
        for core in range(CORES):
            out[core * WIDTH + to] = total[:, core * rows : (core + 1) * rows]


def per_device(images, texts, matches, scale, shift_bias):
    features, rows = images.shape[1], images.shape[0]
    span = CORES * rows
    quarter = span // WIDTH
    whole = WIDTH * features

    image, text = images.T, texts.T
    piece = jax.ShapeDtypeStruct((whole, quarter), BF16)
    chunks = pl.pallas_call(
        deal_kernel,
        out_shape=jax.ShapeDtypeStruct((LEVELS * CORES * WIDTH, features // 2, quarter), BF16),
        in_specs=[HBM] * 2,
        out_specs=LOCAL,
        scratch_shapes=[
            pltpu.VMEM((CORES, features, rows), BF16),
            pltpu.SemaphoreType.DMA((CORES,)),
        ],
        compiler_params=pltpu.CompilerParams(vmem_limit_bytes=60 << 20),
    )(image, text)
    dealt = lax.all_to_all(chunks, ("level", "core", "width"), 0, 0)

    params = pltpu.CompilerParams(vmem_limit_bytes=6 << 20)
    first = lax.axis_index("core") == 0
    noted = jnp.broadcast_to(matches.astype(BF16), (MARKS, rows))
    other = swap_cores(jnp.concatenate([jnp.where(first, image, text), noted], 0))
    spread, marks = pl.pallas_call(
        spread_kernel,
        out_shape=[
            jax.ShapeDtypeStruct((WIDTH, features, span), BF16),
            jax.ShapeDtypeStruct((MARKS, span), F32),
        ],
        in_specs=[LOCAL] * 3,
        out_specs=[LOCAL] * 2,
        compiler_params=params,
    )(jnp.where(first, text, image), matches, other)
    own, pair = pl.pallas_call(
        gather_kernel,
        out_shape=[piece] * 2,
        in_specs=[LOCAL],
        out_specs=[LOCAL] * 2,
        compiler_params=params,
    )(dealt)

    held = lax.all_to_all(spread, "width", 0, 0)
    held = held.reshape(whole, span)
    far = lax.ppermute(pair, ("row", "level"), far_route(lax.axis_size("row")))
    l1, l2, l3 = (along_line(own, d) for d in (1, 2, 3))

    s1, s2, s3 = pl.pallas_call(
        halo_kernel,
        out_shape=[piece] * 3,
        in_specs=[LOCAL] * 2,
        out_specs=[LOCAL] * 3,
        compiler_params=params,
        cost_estimate=pl.CostEstimate(flops=10 * 10**9, bytes_accessed=2 << 20, transcendentals=0),
    )(pair, far)
    h1, h2, h3 = along_line(s1, 1), along_line(s2, 2), along_line(s3, 3)

    cost = pl.CostEstimate(
        flops=2 * whole * PIECES * quarter * span, bytes_accessed=5 << 20, transcendentals=0
    )
    params = pltpu.CompilerParams(vmem_limit_bytes=12 << 20)
    near = pl.pallas_call(
        near_kernel,
        out_shape=jax.ShapeDtypeStruct((whole, span), F32),
        in_specs=[SMEM, SMEM] + [LOCAL] * 6,
        out_specs=LOCAL,
        compiler_params=params,
        cost_estimate=cost,
    )(scale, shift_bias, marks, own, l2, l3, l1, held)
    partial = pl.pallas_call(
        far_kernel,
        out_shape=jax.ShapeDtypeStruct((CORES * WIDTH, features, rows), BF16),
        in_specs=[SMEM, SMEM] + [LOCAL] * 7,
        out_specs=LOCAL,
        compiler_params=params,
        cost_estimate=cost,
    )(scale, shift_bias, pair, far, h2, h1, h3, held, near)
    terms = lax.all_to_all(partial, ("core", "width"), 0, 0).astype(F32)
    grad_text = terms[0] + terms[1] + terms[2] + terms[3]
    grad_image = terms[4] + terms[5] + terms[6] + terms[7]
    return (scale[0] * grad_image).T, (scale[0] * grad_text).T


def solution(mesh):
    deep = mesh.shape["tour"] // (LEVELS * LINE * CORES)
    fine = Mesh(
        mesh.devices.reshape(deep, LEVELS, LINE, CORES, WIDTH),
        ("row", "level", "x", "core", "width"),
    )
    rows, split = ("row", "level", "x", "core"), "width"
    return jax.shard_map(
        per_device,
        mesh=fine,
        in_specs=(P(rows, split), P(rows, split), P(rows, None), P(), P()),
        out_specs=(P(rows, split), P(rows, split)),
        check_vma=False,
    )
```

time: 116 us -> 113 us (0.974)
  the two profiles are of different devices: /device:TPU:11 before, /device:TPU:57 now
where the time goes in v5:
time: 113 us; the launch traced here: 112 us
  starting transfers between devices  46.4 us (41%)
  blocking collectives  33.7 us (30%)
  waiting for transfers between devices  18.2 us (16%)
  Pallas kernels  7.7 us (7%)
  local copies, waits for them, and re-layouts  3.05 us (3%)
  between operations  2.13 us (2%)
  other arithmetic  1.24 us (1%)
    all_to_all x1, blocking collectives, per_device(): terms = lax.all_to_all(partial, ('core', 'width'), 0, 0).astype(F32)  33.7 us
    ppermute x6, starting transfers between devices, along_line(): return lax.ppermute(block, 'x', [(i ^ turn, i) for i in range(LINE)])  18.9 us
    all_to_all x1, waiting for transfers between devices, per_device(): dealt = lax.all_to_all(chunks, ('level', 'core', 'width'), 0, 0)  10.2 us
    ppermute x1, starting transfers between devices, per_device(): far = lax.ppermute(pair, ('row', 'level'), far_route(lax.axis_size('row')))  8.97 us
    all_to_all x1, starting transfers between devices, per_device(): dealt = lax.all_to_all(chunks, ('level', 'core', 'width'), 0, 0)  8.91 us
    all_to_all x1, starting transfers between devices, per_device(): held = lax.all_to_all(spread, 'width', 0, 0)  7.35 us
    ppermute x6, waiting for transfers between devices, along_line(): return lax.ppermute(block, 'x', [(i ^ turn, i) for i in range(LINE)])  6.97 us
    unnamed x14, local copies, waits for them, and re-layouts  3.04 us
  transfers between devices with their start and end apart: 10, of which 5 were waited for; matrix products, arithmetic and copies ran while one was open for 0% of the time, Pallas kernels for 4%

profile of v5, /device:TPU:57, one launch (start us, length us, event | category | flops | bytes accessed | tf_op | source)
XLA Modules:
  0.0 112.4 jit_solution(17905067836287615368)
XLA Ops:
  0.7 2.0 %shard_map.68 = bf16[16,144,128]{2,1,0:T(8,128)(2,1)} custom-call(bf16[288,256]{1,0:T(8,128)(2,1)} %bitcast.19, bf16[288,256]{1,0:T(8,128)(2,1)} %bitcast.20), custom_call_target="tpu_custom_call" | custom-call | tf_op jit(solution)/shard_map/pallas_call | solution.py:167
  2.7 8.9 %all-to-all-start = ((bf16[16,144,128]{2,1,0:T(8,128)(2,1)}), bf16[16,144,128]{2,1,0:T(8,128)(2,1)S(1)}, u32[]{:S(2)}, u32[]{:S(2)}) async-start(bf16[16,144,128]{2,1,0:T(8,128)(2,1)} %shard_map.68), calls=%async_computation | async-start | bytes 1179648 | tf_op jit(solution)/shard_map/all_to_all | solution.py:178
  11.7 2.3 %collective-permute-start.4 = (bf16[304,256]{1,0:T(8,128)(2,1)S(1)}, bf16[304,256]{1,0:T(8,128)(2,1)S(1)}, u32[]{:S(2)}, u32[]{:S(2)}) collective-permute-start(bf16[304,256]{1,0:T(8,128)(2,1)S(1)} %pad_maximum_fusion), channel_id=1, source_target_pairs={{0,4},{4,0},{1,5},{5,1},{2,6},{6,2},{3,7},{7,3},{8,12},{12,8},{9,1... | collective-permute-start | bytes 466952 | tf_op jit(solution)/shard_map/ppermute | solution.py:22
  14.0 1.0 collective-permute-done.4.other
  15.0 1.1 %shard_map.71 = (bf16[4,288,512]{2,1,0:T(8,128)(2,1)}, f32[16,512]{1,0:T(8,128)S(1)}) custom-call(bf16[288,256]{1,0:T(8,128)(2,1)S(1)} %get-tuple-element.19.mine, s32[1,256]{1,0:T(1,128)S(1)} %copy-done.4, bf16[304,256]{1,0:T(8,128)(2,1)S(1)} %collective-permute-done.4.other), custom_call_target="tpu_custom_call" | custom-call | tf_op jit(solution)/shard_map/pallas_call | solution.py:184
  16.1 0.6 copy-done.2
  16.7 10.2 %all-to-all-done.dealt = bf16[16,144,128]{2,1,0:T(8,128)(2,1)S(1)} async-done(((bf16[16,144,128]{2,1,0:T(8,128)(2,1)}), bf16[16,144,128]{2,1,0:T(8,128)(2,1)S(1)}, u32[]{:S(2)}, u32[]{:S(2)}) %all-to-all-start) | async-done | bytes 589856 | tf_op jit(solution)/shard_map/all_to_all | solution.py:178
  26.9 7.3 %all-to-all-start.1 = ((bf16[4,288,512]{2,1,0:T(8,128)(2,1)}), bf16[4,288,512]{2,1,0:T(8,128)(2,1)S(1)}, u32[]{:S(2)}, u32[]{:S(2)}) async-start(bf16[4,288,512]{2,1,0:T(8,128)(2,1)} %get-tuple-element.13), calls=%async_computation.1 | async-start | bytes 2359296 | tf_op jit(solution)/shard_map/all_to_all | solution.py:202
  34.3 0.2 shard_map.69
  34.5 9.0 %collective-permute-start = (bf16[1152,128]{1,0:T(8,128)(2,1)S(1)}, bf16[1152,128]{1,0:T(8,128)(2,1)S(1)}, u32[]{:S(2)}, u32[]{:S(2)}) collective-permute-start(bf16[1152,128]{1,0:T(8,128)(2,1)S(1)} %get-tuple-element.9.pair), channel_id=1, source_target_pairs={{0,64},{32,480},{64,128},{96,32},{128,192},{160,96},{192,256},{224... | collective-permute-start | bytes 884744 | tf_op jit(solution)/shard_map/ppermute | solution.py:204
  43.5 4.7 %collective-permute-start.5 = (bf16[1152,128]{1,0:T(8,128)(2,1)S(1)}, bf16[1152,128]{1,0:T(8,128)(2,1)S(1)}, u32[]{:S(2)}, u32[]{:S(2)}) collective-permute-start(bf16[1152,128]{1,0:T(8,128)(2,1)S(1)} %get-tuple-element.15.own), channel_id=1, source_target_pairs={{16,0},{24,8},{0,16},{8,24},{17,1},{25,9},{1,17},{9,25},{18,2},{26... | collective-permute-start | bytes 884744 | tf_op jit(solution)/shard_map/ppermute | solution.py:26
  48.1 2.8 %collective-permute-start.6 = (bf16[1152,128]{1,0:T(8,128)(2,1)S(1)}, bf16[1152,128]{1,0:T(8,128)(2,1)S(1)}, u32[]{:S(2)}, u32[]{:S(2)}) collective-permute-start(bf16[1152,128]{1,0:T(8,128)(2,1)S(1)} %get-tuple-element.15.own), channel_id=1, source_target_pairs={{24,0},{16,8},{8,16},{0,24},{25,1},{17,9},{9,17},{1,25},{26,2},{18... | collective-permute-start | bytes 884744 | tf_op jit(solution)/shard_map/ppermute | solution.py:26
  50.9 1.9 %collective-permute-start.7 = (bf16[1152,128]{1,0:T(8,128)(2,1)S(1)}, bf16[1152,128]{1,0:T(8,128)(2,1)S(1)}, u32[]{:S(2)}, u32[]{:S(2)}) collective-permute-start(bf16[1152,128]{1,0:T(8,128)(2,1)S(1)} %get-tuple-element.15.own), channel_id=1, source_target_pairs={{8,0},{0,8},{24,16},{16,24},{9,1},{1,9},{25,17},{17,25},{10,2},{2,... | collective-permute-start | bytes 884744 | tf_op jit(solution)/shard_map/ppermute | solution.py:26
  52.8 0.0 collective-permute-done.far
  52.8 1.1 %shard_map.70 = (bf16[1152,128]{1,0:T(8,128)(2,1)}, bf16[1152,128]{1,0:T(8,128)(2,1)}, bf16[1152,128]{1,0:T(8,128)(2,1)}) custom-call(bf16[1152,128]{1,0:T(8,128)(2,1)S(1)} %get-tuple-element.9.pair, bf16[1152,128]{1,0:T(8,128)(2,1)S(1)} %collective-permute-done.far), custom_call_target="tpu_custom_call" | custom-call | flops 10000000000 | bytes 2097152 | tf_op jit(solution)/shard_map/pallas_call | solution.py:207
  54.0 4.9 %collective-permute-start.1 = (bf16[1152,128]{1,0:T(8,128)(2,1)}, bf16[1152,128]{1,0:T(8,128)(2,1)S(1)}, u32[]{:S(2)}, u32[]{:S(2)}) collective-permute-start(bf16[1152,128]{1,0:T(8,128)(2,1)} %get-tuple-element.10), channel_id=1, source_target_pairs={{16,0},{24,8},{0,16},{8,24},{17,1},{25,9},{1,17},{9,25},{18,2},{26... | collective-permute-start | bytes 884744 | tf_op jit(solution)/shard_map/ppermute | solution.py:26
  58.9 1.9 %collective-permute-start.2 = (bf16[1152,128]{1,0:T(8,128)(2,1)}, bf16[1152,128]{1,0:T(8,128)(2,1)S(1)}, u32[]{:S(2)}, u32[]{:S(2)}) collective-permute-start(bf16[1152,128]{1,0:T(8,128)(2,1)} %get-tuple-element.11), channel_id=1, source_target_pairs={{8,0},{0,8},{24,16},{16,24},{9,1},{1,9},{25,17},{17,25},{10,2},{2,... | collective-permute-start | bytes 884744 | tf_op jit(solution)/shard_map/ppermute | solution.py:26
  60.8 0.0 collective-permute-done.5.l2
  60.8 2.8 %collective-permute-start.3 = (bf16[1152,128]{1,0:T(8,128)(2,1)}, bf16[1152,128]{1,0:T(8,128)(2,1)S(1)}, u32[]{:S(2)}, u32[]{:S(2)}) collective-permute-start(bf16[1152,128]{1,0:T(8,128)(2,1)} %get-tuple-element.12), channel_id=1, source_target_pairs={{24,0},{16,8},{8,16},{0,24},{25,1},{17,9},{9,17},{1,25},{26,2},{18... | collective-permute-start | bytes 884744 | tf_op jit(solution)/shard_map/ppermute | solution.py:26
  64.9 0.0 collective-permute-done.6.l3
  64.9 0.0 collective-permute-done.7.l1
  64.9 0.7 copy-done
  65.6 1.0 copy-done.1
  66.6 0.8 copy-done.3
  67.3 1.6 %shard_map.72.near = f32[1152,512]{1,0:T(8,128)S(1)} custom-call(f32[1]{0:T(128)} %copy.7.scale, f32[1]{0:T(128)S(6)} %copy.8.bias, f32[16,512]{1,0:T(8,128)S(1)} %copy-done.3, bf16[1152,128]{1,0:T(8,128)(2,1)S(1)} %get-tuple-element.15.own, bf16[1152,128]{1,0:T(8,128)(2,1)S(1)} %collective-permute-done.5.l2, ...), custom_call_target="tpu_custom_call" | custom-call | flops 1207959552 | bytes 5242880 | tf_op jit(solution)/shard_map/pallas_call | solution.py:221
  68.9 0.2 collective-permute-done.1.h2
  69.1 5.7 %collective-permute-done.2.h1 = bf16[1152,128]{1,0:T(8,128)(2,1)S(1)} collective-permute-done((bf16[1152,128]{1,0:T(8,128)(2,1)}, bf16[1152,128]{1,0:T(8,128)(2,1)S(1)}, u32[]{:S(2)}, u32[]{:S(2)}) %collective-permute-start.2) | collective-permute-done | bytes 294944 | tf_op jit(solution)/shard_map/ppermute | solution.py:26
  74.8 1.1 collective-permute-done.3.h3
  75.9 1.6 %shard_map.73 = bf16[8,288,256]{2,1,0:T(8,128)(2,1)S(1)} custom-call(f32[1]{0:T(128)} %copy.7.scale, f32[1]{0:T(128)S(6)} %copy.8.bias, bf16[1152,128]{1,0:T(8,128)(2,1)S(1)} %get-tuple-element.9.pair, bf16[1152,128]{1,0:T(8,128)(2,1)S(1)} %collective-permute-done.far, bf16[1152,128]{1,0:T(8,128)(2,1)S(1)} %collective-permute-done.1.h2, ...), custom_call_target="tpu_custom_call" | custom-call | flops 1207959552 | bytes 5242880 | tf_op jit(solution)/shard_map/pallas_call | solution.py:229
  77.5 33.7 %all_to_all.15 = bf16[8,288,256]{2,1,0:T(8,128)(2,1)S(1)} all-to-all(bf16[8,288,256]{2,1,0:T(8,128)(2,1)S(1)} %shard_map.73), channel_id=1, replica_groups=mesh['row'=8,'level'=2,'x'=4,'core'=2,'width'=4] {'core','width'}, dimensions={0} | all-to-all | bytes 2359296 | tf_op jit(solution)/shard_map/all_to_all | solution.py:237
  111.2 0.2 convert_element_type.7
  111.4 1.0 fusion.1
  (15 shorter events, 0.1 us)
Async XLA Ops:
  0.6 11.0 %copy-start.5 = (bf16[256,288]{0,1:T(8,128)(2,1)S(1)}, bf16[256,288]{0,1:T(8,128)(2,1)}, u32[]{:S(2)}) copy-start(bf16[256,288]{0,1:T(8,128)(2,1)} %param.5) | copy-start | bytes 442372
  0.6 11.0 %copy-start.6 = (bf16[256,288]{0,1:T(8,128)(2,1)S(1)}, bf16[256,288]{0,1:T(8,128)(2,1)}, u32[]{:S(2)}) copy-start(bf16[256,288]{0,1:T(8,128)(2,1)} %param.6) | copy-start | bytes 442372
  0.6 11.0 %copy-start.4 = (s32[1,256]{1,0:T(1,128)S(1)}, s32[1,256]{1,0:T(1,128)}, u32[]{:S(2)}) copy-start(s32[1,256]{1,0:T(1,128)} %matches.1) | copy-start | bytes 3076
  2.7 24.2 %all-to-all-start = ((bf16[16,144,128]{2,1,0:T(8,128)(2,1)}), bf16[16,144,128]{2,1,0:T(8,128)(2,1)S(1)}, u32[]{:S(2)}, u32[]{:S(2)}) async-start(bf16[16,144,128]{2,1,0:T(8,128)(2,1)} %shard_map.68), calls=%async_computation | async-start | bytes 1179648 | tf_op jit(solution)/shard_map/all_to_all | solution.py:178
  11.7 3.3 %collective-permute-start.4 = (bf16[304,256]{1,0:T(8,128)(2,1)S(1)}, bf16[304,256]{1,0:T(8,128)(2,1)S(1)}, u32[]{:S(2)}, u32[]{:S(2)}) collective-permute-start(bf16[304,256]{1,0:T(8,128)(2,1)S(1)} %pad_maximum_fusion), channel_id=1, source_target_pairs={{0,4},{4,0},{1,5},{5,1},{2,6},{6,2},{3,7},{7,3},{8,12},{12,8},{9,1... | collective-permute-start | bytes 466952 | tf_op jit(solution)/shard_map/ppermute | solution.py:22
  16.1 0.6 copy-start.2
  26.9 38.7 %all-to-all-start.1 = ((bf16[4,288,512]{2,1,0:T(8,128)(2,1)}), bf16[4,288,512]{2,1,0:T(8,128)(2,1)S(1)}, u32[]{:S(2)}, u32[]{:S(2)}) async-start(bf16[4,288,512]{2,1,0:T(8,128)(2,1)} %get-tuple-element.13), calls=%async_computation.1 | async-start | bytes 2359296 | tf_op jit(solution)/shard_map/all_to_all | solution.py:202
  34.5 18.3 %collective-permute-start = (bf16[1152,128]{1,0:T(8,128)(2,1)S(1)}, bf16[1152,128]{1,0:T(8,128)(2,1)S(1)}, u32[]{:S(2)}, u32[]{:S(2)}) collective-permute-start(bf16[1152,128]{1,0:T(8,128)(2,1)S(1)} %get-tuple-element.9.pair), channel_id=1, source_target_pairs={{0,64},{32,480},{64,128},{96,32},{128,192},{160,96},{192,256},{224... | collective-permute-start | bytes 884744 | tf_op jit(solution)/shard_map/ppermute | solution.py:204
  43.5 17.3 %collective-permute-start.5 = (bf16[1152,128]{1,0:T(8,128)(2,1)S(1)}, bf16[1152,128]{1,0:T(8,128)(2,1)S(1)}, u32[]{:S(2)}, u32[]{:S(2)}) collective-permute-start(bf16[1152,128]{1,0:T(8,128)(2,1)S(1)} %get-tuple-element.15.own), channel_id=1, source_target_pairs={{16,0},{24,8},{0,16},{8,24},{17,1},{25,9},{1,17},{9,25},{18,2},{26... | collective-permute-start | bytes 884744 | tf_op jit(solution)/shard_map/ppermute | solution.py:26
  48.1 16.8 %collective-permute-start.6 = (bf16[1152,128]{1,0:T(8,128)(2,1)S(1)}, bf16[1152,128]{1,0:T(8,128)(2,1)S(1)}, u32[]{:S(2)}, u32[]{:S(2)}) collective-permute-start(bf16[1152,128]{1,0:T(8,128)(2,1)S(1)} %get-tuple-element.15.own), channel_id=1, source_target_pairs={{24,0},{16,8},{8,16},{0,24},{25,1},{17,9},{9,17},{1,25},{26,2},{18... | collective-permute-start | bytes 884744 | tf_op jit(solution)/shard_map/ppermute | solution.py:26
  50.9 14.0 %collective-permute-start.7 = (bf16[1152,128]{1,0:T(8,128)(2,1)S(1)}, bf16[1152,128]{1,0:T(8,128)(2,1)S(1)}, u32[]{:S(2)}, u32[]{:S(2)}) collective-permute-start(bf16[1152,128]{1,0:T(8,128)(2,1)S(1)} %get-tuple-element.15.own), channel_id=1, source_target_pairs={{8,0},{0,8},{24,16},{16,24},{9,1},{1,9},{25,17},{17,25},{10,2},{2,... | collective-permute-start | bytes 884744 | tf_op jit(solution)/shard_map/ppermute | solution.py:26
  54.0 15.1 %collective-permute-start.1 = (bf16[1152,128]{1,0:T(8,128)(2,1)}, bf16[1152,128]{1,0:T(8,128)(2,1)S(1)}, u32[]{:S(2)}, u32[]{:S(2)}) collective-permute-start(bf16[1152,128]{1,0:T(8,128)(2,1)} %get-tuple-element.10), channel_id=1, source_target_pairs={{16,0},{24,8},{0,16},{8,24},{17,1},{25,9},{1,17},{9,25},{18,2},{26... | collective-permute-start | bytes 884744 | tf_op jit(solution)/shard_map/ppermute | solution.py:26
  58.9 16.0 %collective-permute-start.2 = (bf16[1152,128]{1,0:T(8,128)(2,1)}, bf16[1152,128]{1,0:T(8,128)(2,1)S(1)}, u32[]{:S(2)}, u32[]{:S(2)}) collective-permute-start(bf16[1152,128]{1,0:T(8,128)(2,1)} %get-tuple-element.11), channel_id=1, source_target_pairs={{8,0},{0,8},{24,16},{16,24},{9,1},{1,9},{25,17},{17,25},{10,2},{2,... | collective-permute-start | bytes 884744 | tf_op jit(solution)/shard_map/ppermute | solution.py:26
  60.8 15.1 %collective-permute-start.3 = (bf16[1152,128]{1,0:T(8,128)(2,1)}, bf16[1152,128]{1,0:T(8,128)(2,1)S(1)}, u32[]{:S(2)}, u32[]{:S(2)}) collective-permute-start(bf16[1152,128]{1,0:T(8,128)(2,1)} %get-tuple-element.12), channel_id=1, source_target_pairs={{24,0},{16,8},{8,16},{0,24},{25,1},{17,9},{9,17},{1,25},{26,2},{18... | collective-permute-start | bytes 884744 | tf_op jit(solution)/shard_map/ppermute | solution.py:26
  64.9 0.7 copy-start
  65.6 1.0 copy-start.1
  66.6 0.8 copy-start.3

commit v6 on v5

--- a/solution.py
+++ b/solution.py
@@ -104,20 +104,6 @@
     have = jnp.where(first, jnp.sum(mark, axis=1, keepdims=True), row.astype(F32))
     goal = jnp.where(first, (lane % rows).astype(F32), marks[0:1, :])
     return ((have == goal) & (lane // rows == block)).astype(F32)
-
-
-def weighed(pieces, held, scale, bias):
-    logits = lax.dot_general(
-        pieces, held[...], (((0,), (0,)), ((), ())), preferred_element_type=F32
-    )
-    return jax.nn.sigmoid(scale[0] * logits + bias[0])
-
-
-def halo_kernel(pair, far, *outs):
-    x, level = lax.axis_index("x"), lax.axis_index("level")
-    for turn, out in enumerate(outs, 1):
-        higher = (x ^ turn) > x
-        out[...] = jnp.where(higher == (level == 0), pair[...], far[...])
 
 
 def near_kernel(scale, bias, marks, own, l2, l3, l1, held, out):
@@ -191,6 +177,7 @@
         out_specs=[LOCAL] * 2,
         compiler_params=params,
     )(jnp.where(first, text, image), matches, other)
+    dealt, spread = lax.optimization_barrier((dealt, spread))
     own, pair = pl.pallas_call(
         gather_kernel,
         out_shape=[piece] * 2,
@@ -210,7 +197,7 @@
         in_specs=[LOCAL] * 2,
         out_specs=[LOCAL] * 3,
         compiler_params=params,
-        cost_estimate=pl.CostEstimate(flops=10 * 10**9, bytes_accessed=2 << 20, transcendentals=0),
+        cost_estimate=pl.CostEstimate(flops=15 * 10**9, bytes_accessed=2 << 20, transcendentals=0),
     )(pair, far)
     h1, h2, h3 = along_line(s1, 1), along_line(s2, 2), along_line(s3, 3)
 

time: 113 us -> 111 us (0.982)
  blocking collectives: 33.7 us -> 31 us
    all_to_all x1, blocking collectives: 33.7 us -> 31 us  [per_device(): terms = lax.all_to_all(partial, ('core', 'width'), 0, 0).astype(F32)]
    ppermute x6, waiting for transfers between devices: 6.97 us -> 4.7 us  [along_line(): return lax.ppermute(block, 'x', [(i ^ turn, i) for i in range(LINE)])]
    all_to_all x1, waiting for transfers between devices: 0.01 us -> 2.26 us  [per_device(): held = lax.all_to_all(spread, 'width', 0, 0)]
where the time goes in v6:
time: 111 us; the launch traced here: 110 us
  starting transfers between devices  46.4 us (42%)
  blocking collectives  31 us (28%)
  waiting for transfers between devices  18.1 us (16%)
  Pallas kernels  7.7 us (7%)
  local copies, waits for them, and re-layouts  3.05 us (3%)
  between operations  2.14 us (2%)
  other arithmetic  1.24 us (1%)
    all_to_all x1, blocking collectives, per_device(): terms = lax.all_to_all(partial, ('core', 'width'), 0, 0).astype(F32)  31 us
    ppermute x6, starting transfers between devices, along_line(): return lax.ppermute(block, 'x', [(i ^ turn, i) for i in range(LINE)])  18.9 us
    all_to_all x1, waiting for transfers between devices, per_device(): dealt = lax.all_to_all(chunks, ('level', 'core', 'width'), 0, 0)  10.2 us
    ppermute x1, starting transfers between devices, per_device(): far = lax.ppermute(pair, ('row', 'level'), far_route(lax.axis_size('row')))  9.06 us
    all_to_all x1, starting transfers between devices, per_device(): dealt = lax.all_to_all(chunks, ('level', 'core', 'width'), 0, 0)  8.91 us
    all_to_all x1, starting transfers between devices, per_device(): held = lax.all_to_all(spread, 'width', 0, 0)  7.27 us
    ppermute x6, waiting for transfers between devices, along_line(): return lax.ppermute(block, 'x', [(i ^ turn, i) for i in range(LINE)])  4.7 us
    unnamed x14, local copies, waits for them, and re-layouts  3.04 us
  transfers between devices with their start and end apart: 10, of which 5 were waited for; matrix products, arithmetic and copies ran while one was open for 0% of the time, Pallas kernels for 4%

profile of v6, /device:TPU:57, one launch (start us, length us, event | category | flops | bytes accessed | tf_op | source)
XLA Modules:
  0.0 109.7 jit_solution(11559354475046131298)
XLA Ops:
  0.7 2.0 %shard_map.68 = bf16[16,144,128]{2,1,0:T(8,128)(2,1)} custom-call(bf16[288,256]{1,0:T(8,128)(2,1)} %bitcast.19, bf16[288,256]{1,0:T(8,128)(2,1)} %bitcast.20), custom_call_target="tpu_custom_call" | custom-call | tf_op jit(solution)/shard_map/pallas_call | solution.py:153
  2.7 8.9 %all-to-all-start = ((bf16[16,144,128]{2,1,0:T(8,128)(2,1)}), bf16[16,144,128]{2,1,0:T(8,128)(2,1)S(1)}, u32[]{:S(2)}, u32[]{:S(2)}) async-start(bf16[16,144,128]{2,1,0:T(8,128)(2,1)} %shard_map.68), calls=%async_computation | async-start | bytes 1179648 | tf_op jit(solution)/shard_map/all_to_all | solution.py:164
  11.7 2.3 %collective-permute-start = (bf16[304,256]{1,0:T(8,128)(2,1)S(1)}, bf16[304,256]{1,0:T(8,128)(2,1)S(1)}, u32[]{:S(2)}, u32[]{:S(2)}) collective-permute-start(bf16[304,256]{1,0:T(8,128)(2,1)S(1)} %pad_maximum_fusion), channel_id=1, source_target_pairs={{0,4},{4,0},{1,5},{5,1},{2,6},{6,2},{3,7},{7,3},{8,12},{12,8},{9,1... | collective-permute-start | bytes 466952 | tf_op jit(solution)/shard_map/ppermute | solution.py:22
  14.0 1.0 collective-permute-done.other
  15.0 1.1 %shard_map.69 = (bf16[4,288,512]{2,1,0:T(8,128)(2,1)}, f32[16,512]{1,0:T(8,128)S(1)}) custom-call(bf16[288,256]{1,0:T(8,128)(2,1)S(1)} %get-tuple-element.23.mine, s32[1,256]{1,0:T(1,128)S(1)} %copy-done.4, bf16[304,256]{1,0:T(8,128)(2,1)S(1)} %collective-permute-done.other), custom_call_target="tpu_custom_call" | custom-call | tf_op jit(solution)/shard_map/pallas_call | solution.py:170
  16.1 0.6 copy-done.2
  16.7 10.2 %all-to-all-done.dealt = bf16[16,144,128]{2,1,0:T(8,128)(2,1)S(1)} async-done(((bf16[16,144,128]{2,1,0:T(8,128)(2,1)}), bf16[16,144,128]{2,1,0:T(8,128)(2,1)S(1)}, u32[]{:S(2)}, u32[]{:S(2)}) %all-to-all-start) | async-done | bytes 589856 | tf_op jit(solution)/shard_map/all_to_all | solution.py:164
  26.9 0.2 shard_map.70
  27.1 9.1 %collective-permute-start.1 = (bf16[1152,128]{1,0:T(8,128)(2,1)S(1)}, bf16[1152,128]{1,0:T(8,128)(2,1)S(1)}, u32[]{:S(2)}, u32[]{:S(2)}) collective-permute-start(bf16[1152,128]{1,0:T(8,128)(2,1)S(1)} %get-tuple-element.13.pair), channel_id=1, source_target_pairs={{0,64},{32,480},{64,128},{96,32},{128,192},{160,96},{192,256},{224... | collective-permute-start | bytes 884744 | tf_op jit(solution)/shard_map/ppermute | solution.py:191
  36.2 7.3 %all-to-all-start.1 = ((bf16[4,288,512]{2,1,0:T(8,128)(2,1)}), bf16[4,288,512]{2,1,0:T(8,128)(2,1)S(1)}, u32[]{:S(2)}, u32[]{:S(2)}) async-start(bf16[4,288,512]{2,1,0:T(8,128)(2,1)} %get-tuple-element.17), calls=%async_computation.1 | async-start | bytes 2359296 | tf_op jit(solution)/shard_map/all_to_all | solution.py:189
  43.5 4.6 %collective-permute-start.5 = (bf16[1152,128]{1,0:T(8,128)(2,1)S(1)}, bf16[1152,128]{1,0:T(8,128)(2,1)S(1)}, u32[]{:S(2)}, u32[]{:S(2)}) collective-permute-start(bf16[1152,128]{1,0:T(8,128)(2,1)S(1)} %get-tuple-element.19.own), channel_id=1, source_target_pairs={{16,0},{24,8},{0,16},{8,24},{17,1},{25,9},{1,17},{9,25},{18,2},{26... | collective-permute-start | bytes 884744 | tf_op jit(solution)/shard_map/ppermute | solution.py:26
  48.1 2.8 %collective-permute-start.6 = (bf16[1152,128]{1,0:T(8,128)(2,1)S(1)}, bf16[1152,128]{1,0:T(8,128)(2,1)S(1)}, u32[]{:S(2)}, u32[]{:S(2)}) collective-permute-start(bf16[1152,128]{1,0:T(8,128)(2,1)S(1)} %get-tuple-element.19.own), channel_id=1, source_target_pairs={{24,0},{16,8},{8,16},{0,24},{25,1},{17,9},{9,17},{1,25},{26,2},{18... | collective-permute-start | bytes 884744 | tf_op jit(solution)/shard_map/ppermute | solution.py:26
  50.9 1.9 %collective-permute-start.7 = (bf16[1152,128]{1,0:T(8,128)(2,1)S(1)}, bf16[1152,128]{1,0:T(8,128)(2,1)S(1)}, u32[]{:S(2)}, u32[]{:S(2)}) collective-permute-start(bf16[1152,128]{1,0:T(8,128)(2,1)S(1)} %get-tuple-element.19.own), channel_id=1, source_target_pairs={{8,0},{0,8},{24,16},{16,24},{9,1},{1,9},{25,17},{17,25},{10,2},{2,... | collective-permute-start | bytes 884744 | tf_op jit(solution)/shard_map/ppermute | solution.py:26
  52.8 0.0 collective-permute-done.1.far
  52.8 1.1 %shard_map.71 = (bf16[1152,128]{1,0:T(8,128)(2,1)}, bf16[1152,128]{1,0:T(8,128)(2,1)}, bf16[1152,128]{1,0:T(8,128)(2,1)}) custom-call(bf16[1152,128]{1,0:T(8,128)(2,1)S(1)} %get-tuple-element.13.pair, bf16[1152,128]{1,0:T(8,128)(2,1)S(1)} %collective-permute-done.1.far), custom_call_target="tpu_custom_call" | custom-call | flops 15000000512 | bytes 2097152 | tf_op jit(solution)/shard_map/pallas_call | solution.py:194
  54.0 4.9 %collective-permute-start.2 = (bf16[1152,128]{1,0:T(8,128)(2,1)}, bf16[1152,128]{1,0:T(8,128)(2,1)S(1)}, u32[]{:S(2)}, u32[]{:S(2)}) collective-permute-start(bf16[1152,128]{1,0:T(8,128)(2,1)} %get-tuple-element.14), channel_id=1, source_target_pairs={{16,0},{24,8},{0,16},{8,24},{17,1},{25,9},{1,17},{9,25},{18,2},{26... | collective-permute-start | bytes 884744 | tf_op jit(solution)/shard_map/ppermute | solution.py:26
  58.9 1.9 %collective-permute-start.3 = (bf16[1152,128]{1,0:T(8,128)(2,1)}, bf16[1152,128]{1,0:T(8,128)(2,1)S(1)}, u32[]{:S(2)}, u32[]{:S(2)}) collective-permute-start(bf16[1152,128]{1,0:T(8,128)(2,1)} %get-tuple-element.15), channel_id=1, source_target_pairs={{8,0},{0,8},{24,16},{16,24},{9,1},{1,9},{25,17},{17,25},{10,2},{2,... | collective-permute-start | bytes 884744 | tf_op jit(solution)/shard_map/ppermute | solution.py:26
  60.8 0.0 collective-permute-done.5.l2
  60.8 2.8 %collective-permute-start.4 = (bf16[1152,128]{1,0:T(8,128)(2,1)}, bf16[1152,128]{1,0:T(8,128)(2,1)S(1)}, u32[]{:S(2)}, u32[]{:S(2)}) collective-permute-start(bf16[1152,128]{1,0:T(8,128)(2,1)} %get-tuple-element.16), channel_id=1, source_target_pairs={{24,0},{16,8},{8,16},{0,24},{25,1},{17,9},{9,17},{1,25},{26,2},{18... | collective-permute-start | bytes 884744 | tf_op jit(solution)/shard_map/ppermute | solution.py:26
  64.9 0.0 collective-permute-done.6.l3
  64.9 0.0 collective-permute-done.7.l1
  64.9 0.7 copy-done
  65.6 2.3 %all-to-all-done.1 = bf16[4,288,512]{2,1,0:T(8,128)(2,1)S(1)} async-done(((bf16[4,288,512]{2,1,0:T(8,128)(2,1)}), bf16[4,288,512]{2,1,0:T(8,128)(2,1)S(1)}, u32[]{:S(2)}, u32[]{:S(2)}) %all-to-all-start.1) | async-done | bytes 1179680 | tf_op jit(solution)/shard_map/all_to_all | solution.py:189
  67.9 1.0 copy-done.1
  68.8 0.8 copy-done.3
  69.6 1.6 %shard_map.72.near = f32[1152,512]{1,0:T(8,128)S(1)} custom-call(f32[1]{0:T(128)} %copy.7.scale, f32[1]{0:T(128)S(6)} %copy.8.bias, f32[16,512]{1,0:T(8,128)S(1)} %copy-done.3, bf16[1152,128]{1,0:T(8,128)(2,1)S(1)} %get-tuple-element.19.own, bf16[1152,128]{1,0:T(8,128)(2,1)S(1)} %collective-permute-done.5.l2, ...), custom_call_target="tpu_custom_call" | custom-call | flops 1207959552 | bytes 5242880 | tf_op jit(solution)/shard_map/pallas_call | solution.py:208
  71.2 3.6 %collective-permute-done.3.h1 = bf16[1152,128]{1,0:T(8,128)(2,1)S(1)} collective-permute-done((bf16[1152,128]{1,0:T(8,128)(2,1)}, bf16[1152,128]{1,0:T(8,128)(2,1)S(1)}, u32[]{:S(2)}, u32[]{:S(2)}) %collective-permute-start.3) | collective-permute-done | bytes 294944 | tf_op jit(solution)/shard_map/ppermute | solution.py:26
  74.8 1.1 collective-permute-done.4.h3
  75.9 1.6 %shard_map.73 = bf16[8,288,256]{2,1,0:T(8,128)(2,1)S(1)} custom-call(f32[1]{0:T(128)} %copy.7.scale, f32[1]{0:T(128)S(6)} %copy.8.bias, bf16[1152,128]{1,0:T(8,128)(2,1)S(1)} %get-tuple-element.13.pair, bf16[1152,128]{1,0:T(8,128)(2,1)S(1)} %collective-permute-done.1.far, bf16[1152,128]{1,0:T(8,128)(2,1)S(1)} %collective-permute-done.2.h2, ...), custom_call_target="tpu_custom_call" | custom-call | flops 1207959552 | bytes 5242880 | tf_op jit(solution)/shard_map/pallas_call | solution.py:216
  77.5 31.0 %all_to_all.15 = bf16[8,288,256]{2,1,0:T(8,128)(2,1)S(1)} all-to-all(bf16[8,288,256]{2,1,0:T(8,128)(2,1)S(1)} %shard_map.73), channel_id=1, replica_groups=mesh['row'=8,'level'=2,'x'=4,'core'=2,'width'=4] {'core','width'}, dimensions={0} | all-to-all | bytes 2359296 | tf_op jit(solution)/shard_map/all_to_all | solution.py:224
  108.5 0.2 convert_element_type.7
  108.7 1.0 fusion.1
  (15 shorter events, 0.1 us)
Async XLA Ops:
  0.6 11.0 %copy-start.5 = (bf16[256,288]{0,1:T(8,128)(2,1)S(1)}, bf16[256,288]{0,1:T(8,128)(2,1)}, u32[]{:S(2)}) copy-start(bf16[256,288]{0,1:T(8,128)(2,1)} %param.5) | copy-start | bytes 442372
  0.6 11.0 %copy-start.6 = (bf16[256,288]{0,1:T(8,128)(2,1)S(1)}, bf16[256,288]{0,1:T(8,128)(2,1)}, u32[]{:S(2)}) copy-start(bf16[256,288]{0,1:T(8,128)(2,1)} %param.6) | copy-start | bytes 442372
  0.6 11.0 %copy-start.4 = (s32[1,256]{1,0:T(1,128)S(1)}, s32[1,256]{1,0:T(1,128)}, u32[]{:S(2)}) copy-start(s32[1,256]{1,0:T(1,128)} %matches.1) | copy-start | bytes 3076
  2.7 24.2 %all-to-all-start = ((bf16[16,144,128]{2,1,0:T(8,128)(2,1)}), bf16[16,144,128]{2,1,0:T(8,128)(2,1)S(1)}, u32[]{:S(2)}, u32[]{:S(2)}) async-start(bf16[16,144,128]{2,1,0:T(8,128)(2,1)} %shard_map.68), calls=%async_computation | async-start | bytes 1179648 | tf_op jit(solution)/shard_map/all_to_all | solution.py:164
  11.7 3.3 %collective-permute-start = (bf16[304,256]{1,0:T(8,128)(2,1)S(1)}, bf16[304,256]{1,0:T(8,128)(2,1)S(1)}, u32[]{:S(2)}, u32[]{:S(2)}) collective-permute-start(bf16[304,256]{1,0:T(8,128)(2,1)S(1)} %pad_maximum_fusion), channel_id=1, source_target_pairs={{0,4},{4,0},{1,5},{5,1},{2,6},{6,2},{3,7},{7,3},{8,12},{12,8},{9,1... | collective-permute-start | bytes 466952 | tf_op jit(solution)/shard_map/ppermute | solution.py:22
  16.1 0.6 copy-start.2
  27.1 25.7 %collective-permute-start.1 = (bf16[1152,128]{1,0:T(8,128)(2,1)S(1)}, bf16[1152,128]{1,0:T(8,128)(2,1)S(1)}, u32[]{:S(2)}, u32[]{:S(2)}) collective-permute-start(bf16[1152,128]{1,0:T(8,128)(2,1)S(1)} %get-tuple-element.13.pair), channel_id=1, source_target_pairs={{0,64},{32,480},{64,128},{96,32},{128,192},{160,96},{192,256},{224... | collective-permute-start | bytes 884744 | tf_op jit(solution)/shard_map/ppermute | solution.py:191
  36.2 31.7 %all-to-all-start.1 = ((bf16[4,288,512]{2,1,0:T(8,128)(2,1)}), bf16[4,288,512]{2,1,0:T(8,128)(2,1)S(1)}, u32[]{:S(2)}, u32[]{:S(2)}) async-start(bf16[4,288,512]{2,1,0:T(8,128)(2,1)} %get-tuple-element.17), calls=%async_computation.1 | async-start | bytes 2359296 | tf_op jit(solution)/shard_map/all_to_all | solution.py:189
  43.5 17.3 %collective-permute-start.5 = (bf16[1152,128]{1,0:T(8,128)(2,1)S(1)}, bf16[1152,128]{1,0:T(8,128)(2,1)S(1)}, u32[]{:S(2)}, u32[]{:S(2)}) collective-permute-start(bf16[1152,128]{1,0:T(8,128)(2,1)S(1)} %get-tuple-element.19.own), channel_id=1, source_target_pairs={{16,0},{24,8},{0,16},{8,24},{17,1},{25,9},{1,17},{9,25},{18,2},{26... | collective-permute-start | bytes 884744 | tf_op jit(solution)/shard_map/ppermute | solution.py:26
  48.1 16.8 %collective-permute-start.6 = (bf16[1152,128]{1,0:T(8,128)(2,1)S(1)}, bf16[1152,128]{1,0:T(8,128)(2,1)S(1)}, u32[]{:S(2)}, u32[]{:S(2)}) collective-permute-start(bf16[1152,128]{1,0:T(8,128)(2,1)S(1)} %get-tuple-element.19.own), channel_id=1, source_target_pairs={{24,0},{16,8},{8,16},{0,24},{25,1},{17,9},{9,17},{1,25},{26,2},{18... | collective-permute-start | bytes 884744 | tf_op jit(solution)/shard_map/ppermute | solution.py:26
  50.9 14.0 %collective-permute-start.7 = (bf16[1152,128]{1,0:T(8,128)(2,1)S(1)}, bf16[1152,128]{1,0:T(8,128)(2,1)S(1)}, u32[]{:S(2)}, u32[]{:S(2)}) collective-permute-start(bf16[1152,128]{1,0:T(8,128)(2,1)S(1)} %get-tuple-element.19.own), channel_id=1, source_target_pairs={{8,0},{0,8},{24,16},{16,24},{9,1},{1,9},{25,17},{17,25},{10,2},{2,... | collective-permute-start | bytes 884744 | tf_op jit(solution)/shard_map/ppermute | solution.py:26
  54.0 17.2 %collective-permute-start.2 = (bf16[1152,128]{1,0:T(8,128)(2,1)}, bf16[1152,128]{1,0:T(8,128)(2,1)S(1)}, u32[]{:S(2)}, u32[]{:S(2)}) collective-permute-start(bf16[1152,128]{1,0:T(8,128)(2,1)} %get-tuple-element.14), channel_id=1, source_target_pairs={{16,0},{24,8},{0,16},{8,24},{17,1},{25,9},{1,17},{9,25},{18,2},{26... | collective-permute-start | bytes 884744 | tf_op jit(solution)/shard_map/ppermute | solution.py:26
  58.9 16.0 %collective-permute-start.3 = (bf16[1152,128]{1,0:T(8,128)(2,1)}, bf16[1152,128]{1,0:T(8,128)(2,1)S(1)}, u32[]{:S(2)}, u32[]{:S(2)}) collective-permute-start(bf16[1152,128]{1,0:T(8,128)(2,1)} %get-tuple-element.15), channel_id=1, source_target_pairs={{8,0},{0,8},{24,16},{16,24},{9,1},{1,9},{25,17},{17,25},{10,2},{2,... | collective-permute-start | bytes 884744 | tf_op jit(solution)/shard_map/ppermute | solution.py:26
  60.8 15.1 %collective-permute-start.4 = (bf16[1152,128]{1,0:T(8,128)(2,1)}, bf16[1152,128]{1,0:T(8,128)(2,1)S(1)}, u32[]{:S(2)}, u32[]{:S(2)}) collective-permute-start(bf16[1152,128]{1,0:T(8,128)(2,1)} %get-tuple-element.16), channel_id=1, source_target_pairs={{24,0},{16,8},{8,16},{0,24},{25,1},{17,9},{9,17},{1,25},{26,2},{18... | collective-permute-start | bytes 884744 | tf_op jit(solution)/shard_map/ppermute | solution.py:26
  64.9 0.7 copy-start
  67.9 1.0 copy-start.1
  68.8 0.8 copy-start.3

commit v7 on v6

--- a/solution.py
+++ b/solution.py
@@ -23,7 +23,7 @@
 
 
 def along_line(block, turn):
-    return lax.ppermute(block, "x", [(i ^ turn, i) for i in range(LINE)])
+    return lax.ppermute(block, "x", [((i + turn) % LINE, i) for i in range(LINE)])
 
 
 def far_route(rows):
@@ -88,7 +88,7 @@
 def halo_kernel(pair, far, *outs):
     x, level = lax.axis_index("x"), lax.axis_index("level")
     for turn, out in enumerate(outs, 1):
-        higher = (x ^ turn) > x
+        higher = lax.rem(x + LINE - turn, LINE) > x
         out[...] = jnp.where(higher == (level == 0), pair[...], far[...])
 
 

time: 111 us -> 110 us (level)
  transfers between devices with their start and end apart: 10 -> 10, of which waited for: 5 -> 4; matrix products, arithmetic and copies ran while one was open for 0% -> 0% of each run, Pallas kernels for 4% -> 4%
where the time goes in v7:
time: 110 us; the launch traced here: 109 us
  starting transfers between devices  45.9 us (42%)
  blocking collectives  31 us (28%)
  waiting for transfers between devices  17.7 us (16%)
  Pallas kernels  7.7 us (7%)
  local copies, waits for them, and re-layouts  3.05 us (3%)
  between operations  2.14 us (2%)
  other arithmetic  1.24 us (1%)
    all_to_all x1, blocking collectives, per_device(): terms = lax.all_to_all(partial, ('core', 'width'), 0, 0).astype(F32)  31 us
    ppermute x6, starting transfers between devices, along_line(): lax.ppermute(block, 'x', [((i + turn) % LINE, i) for i in range(LINE)])  18.4 us
    all_to_all x1, waiting for transfers between devices, per_device(): dealt = lax.all_to_all(chunks, ('level', 'core', 'width'), 0, 0)  10.2 us
    ppermute x1, starting transfers between devices, per_device(): far = lax.ppermute(pair, ('row', 'level'), far_route(lax.axis_size('row')))  9.06 us
    all_to_all x1, starting transfers between devices, per_device(): dealt = lax.all_to_all(chunks, ('level', 'core', 'width'), 0, 0)  8.91 us
    all_to_all x1, starting transfers between devices, per_device(): held = lax.all_to_all(spread, 'width', 0, 0)  7.27 us
    ppermute x6, waiting for transfers between devices, along_line(): lax.ppermute(block, 'x', [((i + turn) % LINE, i) for i in range(LINE)])  3.7 us
    unnamed x14, local copies, waits for them, and re-layouts  3.04 us
  transfers between devices with their start and end apart: 10, of which 4 were waited for; matrix products, arithmetic and copies ran while one was open for 0% of the time, Pallas kernels for 4%

profile of v7, /device:TPU:57, one launch (start us, length us, event | category | flops | bytes accessed | tf_op | source)
XLA Modules:
  0.0 108.7 jit_solution(18082853309349663597)
XLA Ops:
  0.7 2.0 %shard_map.68 = bf16[16,144,128]{2,1,0:T(8,128)(2,1)} custom-call(bf16[288,256]{1,0:T(8,128)(2,1)} %bitcast.19, bf16[288,256]{1,0:T(8,128)(2,1)} %bitcast.20), custom_call_target="tpu_custom_call" | custom-call | tf_op jit(solution)/shard_map/pallas_call | solution.py:153
  2.7 8.9 %all-to-all-start = ((bf16[16,144,128]{2,1,0:T(8,128)(2,1)}), bf16[16,144,128]{2,1,0:T(8,128)(2,1)S(1)}, u32[]{:S(2)}, u32[]{:S(2)}) async-start(bf16[16,144,128]{2,1,0:T(8,128)(2,1)} %shard_map.68), calls=%async_computation | async-start | bytes 1179648 | tf_op jit(solution)/shard_map/all_to_all | solution.py:164
  11.7 2.3 %collective-permute-start = (bf16[304,256]{1,0:T(8,128)(2,1)S(1)}, bf16[304,256]{1,0:T(8,128)(2,1)S(1)}, u32[]{:S(2)}, u32[]{:S(2)}) collective-permute-start(bf16[304,256]{1,0:T(8,128)(2,1)S(1)} %pad_maximum_fusion), channel_id=1, source_target_pairs={{0,4},{4,0},{1,5},{5,1},{2,6},{6,2},{3,7},{7,3},{8,12},{12,8},{9,1... | collective-permute-start | bytes 466952 | tf_op jit(solution)/shard_map/ppermute | solution.py:22
  14.0 1.0 collective-permute-done.other
  15.0 1.1 %shard_map.69 = (bf16[4,288,512]{2,1,0:T(8,128)(2,1)}, f32[16,512]{1,0:T(8,128)S(1)}) custom-call(bf16[288,256]{1,0:T(8,128)(2,1)S(1)} %get-tuple-element.23.mine, s32[1,256]{1,0:T(1,128)S(1)} %copy-done.4, bf16[304,256]{1,0:T(8,128)(2,1)S(1)} %collective-permute-done.other), custom_call_target="tpu_custom_call" | custom-call | tf_op jit(solution)/shard_map/pallas_call | solution.py:170
  16.1 0.6 copy-done.2
  16.7 10.2 %all-to-all-done.dealt = bf16[16,144,128]{2,1,0:T(8,128)(2,1)S(1)} async-done(((bf16[16,144,128]{2,1,0:T(8,128)(2,1)}), bf16[16,144,128]{2,1,0:T(8,128)(2,1)S(1)}, u32[]{:S(2)}, u32[]{:S(2)}) %all-to-all-start) | async-done | bytes 589856 | tf_op jit(solution)/shard_map/all_to_all | solution.py:164
  26.9 0.2 shard_map.70
  27.1 9.1 %collective-permute-start.1 = (bf16[1152,128]{1,0:T(8,128)(2,1)S(1)}, bf16[1152,128]{1,0:T(8,128)(2,1)S(1)}, u32[]{:S(2)}, u32[]{:S(2)}) collective-permute-start(bf16[1152,128]{1,0:T(8,128)(2,1)S(1)} %get-tuple-element.13.pair), channel_id=1, source_target_pairs={{0,64},{32,480},{64,128},{96,32},{128,192},{160,96},{192,256},{224... | collective-permute-start | bytes 884744 | tf_op jit(solution)/shard_map/ppermute | solution.py:191
  36.2 7.3 %all-to-all-start.1 = ((bf16[4,288,512]{2,1,0:T(8,128)(2,1)}), bf16[4,288,512]{2,1,0:T(8,128)(2,1)S(1)}, u32[]{:S(2)}, u32[]{:S(2)}) async-start(bf16[4,288,512]{2,1,0:T(8,128)(2,1)} %get-tuple-element.17), calls=%async_computation.1 | async-start | bytes 2359296 | tf_op jit(solution)/shard_map/all_to_all | solution.py:189
  43.5 4.6 %collective-permute-start.5 = (bf16[1152,128]{1,0:T(8,128)(2,1)S(1)}, bf16[1152,128]{1,0:T(8,128)(2,1)S(1)}, u32[]{:S(2)}, u32[]{:S(2)}) collective-permute-start(bf16[1152,128]{1,0:T(8,128)(2,1)S(1)} %get-tuple-element.19.own), channel_id=1, source_target_pairs={{16,0},{24,8},{0,16},{8,24},{17,1},{25,9},{1,17},{9,25},{18,2},{26... | collective-permute-start | bytes 884744 | tf_op jit(solution)/shard_map/ppermute | solution.py:26
  48.1 2.2 %collective-permute-start.6 = (bf16[1152,128]{1,0:T(8,128)(2,1)S(1)}, bf16[1152,128]{1,0:T(8,128)(2,1)S(1)}, u32[]{:S(2)}, u32[]{:S(2)}) collective-permute-start(bf16[1152,128]{1,0:T(8,128)(2,1)S(1)} %get-tuple-element.19.own), channel_id=1, source_target_pairs={{24,0},{0,8},{8,16},{16,24},{25,1},{1,9},{9,17},{17,25},{26,2},{2,... | collective-permute-start | bytes 884744 | tf_op jit(solution)/shard_map/ppermute | solution.py:26
  50.4 4.3 %collective-permute-start.7 = (bf16[1152,128]{1,0:T(8,128)(2,1)S(1)}, bf16[1152,128]{1,0:T(8,128)(2,1)S(1)}, u32[]{:S(2)}, u32[]{:S(2)}) collective-permute-start(bf16[1152,128]{1,0:T(8,128)(2,1)S(1)} %get-tuple-element.19.own), channel_id=1, source_target_pairs={{8,0},{16,8},{24,16},{0,24},{9,1},{17,9},{25,17},{1,25},{10,2},{18... | collective-permute-start | bytes 884744 | tf_op jit(solution)/shard_map/ppermute | solution.py:26
  54.6 1.1 %shard_map.71 = (bf16[1152,128]{1,0:T(8,128)(2,1)}, bf16[1152,128]{1,0:T(8,128)(2,1)}, bf16[1152,128]{1,0:T(8,128)(2,1)}) custom-call(bf16[1152,128]{1,0:T(8,128)(2,1)S(1)} %get-tuple-element.13.pair, bf16[1152,128]{1,0:T(8,128)(2,1)S(1)} %collective-permute-done.1.far), custom_call_target="tpu_custom_call" | custom-call | flops 15000000512 | bytes 2097152 | tf_op jit(solution)/shard_map/pallas_call | solution.py:194
  55.8 1.9 %collective-permute-start.2 = (bf16[1152,128]{1,0:T(8,128)(2,1)}, bf16[1152,128]{1,0:T(8,128)(2,1)S(1)}, u32[]{:S(2)}, u32[]{:S(2)}) collective-permute-start(bf16[1152,128]{1,0:T(8,128)(2,1)} %get-tuple-element.14), channel_id=1, source_target_pairs={{16,0},{24,8},{0,16},{8,24},{17,1},{25,9},{1,17},{9,25},{18,2},{26... | collective-permute-start | bytes 884744 | tf_op jit(solution)/shard_map/ppermute | solution.py:26
  57.7 3.4 %collective-permute-start.3 = (bf16[1152,128]{1,0:T(8,128)(2,1)}, bf16[1152,128]{1,0:T(8,128)(2,1)S(1)}, u32[]{:S(2)}, u32[]{:S(2)}) collective-permute-start(bf16[1152,128]{1,0:T(8,128)(2,1)} %get-tuple-element.15), channel_id=1, source_target_pairs={{8,0},{16,8},{24,16},{0,24},{9,1},{17,9},{25,17},{1,25},{10,2},{18... | collective-permute-start | bytes 884744 | tf_op jit(solution)/shard_map/ppermute | solution.py:26
  61.1 0.0 collective-permute-done.5.l2
  61.1 1.9 %collective-permute-start.4 = (bf16[1152,128]{1,0:T(8,128)(2,1)}, bf16[1152,128]{1,0:T(8,128)(2,1)S(1)}, u32[]{:S(2)}, u32[]{:S(2)}) collective-permute-start(bf16[1152,128]{1,0:T(8,128)(2,1)} %get-tuple-element.16), channel_id=1, source_target_pairs={{24,0},{0,8},{8,16},{16,24},{25,1},{1,9},{9,17},{17,25},{26,2},{2,... | collective-permute-start | bytes 884744 | tf_op jit(solution)/shard_map/ppermute | solution.py:26
  64.3 0.0 collective-permute-done.6.l3
  64.3 0.0 collective-permute-done.7.l1
  64.4 0.7 copy-done
  65.1 2.8 %all-to-all-done.1 = bf16[4,288,512]{2,1,0:T(8,128)(2,1)S(1)} async-done(((bf16[4,288,512]{2,1,0:T(8,128)(2,1)}), bf16[4,288,512]{2,1,0:T(8,128)(2,1)S(1)}, u32[]{:S(2)}, u32[]{:S(2)}) %all-to-all-start.1) | async-done | bytes 1179680 | tf_op jit(solution)/shard_map/all_to_all | solution.py:189
  67.9 1.0 copy-done.1
  68.8 0.8 copy-done.3
  69.6 1.6 %shard_map.72.near = f32[1152,512]{1,0:T(8,128)S(1)} custom-call(f32[1]{0:T(128)} %copy.7.scale, f32[1]{0:T(128)S(6)} %copy.8.bias, f32[16,512]{1,0:T(8,128)S(1)} %copy-done.3, bf16[1152,128]{1,0:T(8,128)(2,1)S(1)} %get-tuple-element.19.own, bf16[1152,128]{1,0:T(8,128)(2,1)S(1)} %collective-permute-done.5.l2, ...), custom_call_target="tpu_custom_call" | custom-call | flops 1207959552 | bytes 5242880 | tf_op jit(solution)/shard_map/pallas_call | solution.py:208
  71.2 0.0 collective-permute-done.2.h2
  71.2 3.7 %collective-permute-done.3.h1 = bf16[1152,128]{1,0:T(8,128)(2,1)S(1)} collective-permute-done((bf16[1152,128]{1,0:T(8,128)(2,1)}, bf16[1152,128]{1,0:T(8,128)(2,1)S(1)}, u32[]{:S(2)}, u32[]{:S(2)}) %collective-permute-start.3) | collective-permute-done | bytes 294944 | tf_op jit(solution)/shard_map/ppermute | solution.py:26
  74.9 0.0 collective-permute-done.4.h3
  74.9 1.6 %shard_map.73 = bf16[8,288,256]{2,1,0:T(8,128)(2,1)S(1)} custom-call(f32[1]{0:T(128)} %copy.7.scale, f32[1]{0:T(128)S(6)} %copy.8.bias, bf16[1152,128]{1,0:T(8,128)(2,1)S(1)} %get-tuple-element.13.pair, bf16[1152,128]{1,0:T(8,128)(2,1)S(1)} %collective-permute-done.1.far, bf16[1152,128]{1,0:T(8,128)(2,1)S(1)} %collective-permute-done.2.h2, ...), custom_call_target="tpu_custom_call" | custom-call | flops 1207959552 | bytes 5242880 | tf_op jit(solution)/shard_map/pallas_call | solution.py:216
  76.5 31.0 %all_to_all.15 = bf16[8,288,256]{2,1,0:T(8,128)(2,1)S(1)} all-to-all(bf16[8,288,256]{2,1,0:T(8,128)(2,1)S(1)} %shard_map.73), channel_id=1, replica_groups=mesh['row'=8,'level'=2,'x'=4,'core'=2,'width'=4] {'core','width'}, dimensions={0} | all-to-all | bytes 2359296 | tf_op jit(solution)/shard_map/all_to_all | solution.py:224
  107.5 0.2 convert_element_type.7
  107.7 1.0 fusion.1
  (15 shorter events, 0.1 us)
Async XLA Ops:
  0.6 11.0 %copy-start.5 = (bf16[256,288]{0,1:T(8,128)(2,1)S(1)}, bf16[256,288]{0,1:T(8,128)(2,1)}, u32[]{:S(2)}) copy-start(bf16[256,288]{0,1:T(8,128)(2,1)} %param.5) | copy-start | bytes 442372
  0.6 11.0 %copy-start.6 = (bf16[256,288]{0,1:T(8,128)(2,1)S(1)}, bf16[256,288]{0,1:T(8,128)(2,1)}, u32[]{:S(2)}) copy-start(bf16[256,288]{0,1:T(8,128)(2,1)} %param.6) | copy-start | bytes 442372
  0.6 11.0 %copy-start.4 = (s32[1,256]{1,0:T(1,128)S(1)}, s32[1,256]{1,0:T(1,128)}, u32[]{:S(2)}) copy-start(s32[1,256]{1,0:T(1,128)} %matches.1) | copy-start | bytes 3076
  2.7 24.2 %all-to-all-start = ((bf16[16,144,128]{2,1,0:T(8,128)(2,1)}), bf16[16,144,128]{2,1,0:T(8,128)(2,1)S(1)}, u32[]{:S(2)}, u32[]{:S(2)}) async-start(bf16[16,144,128]{2,1,0:T(8,128)(2,1)} %shard_map.68), calls=%async_computation | async-start | bytes 1179648 | tf_op jit(solution)/shard_map/all_to_all | solution.py:164
  11.7 3.3 %collective-permute-start = (bf16[304,256]{1,0:T(8,128)(2,1)S(1)}, bf16[304,256]{1,0:T(8,128)(2,1)S(1)}, u32[]{:S(2)}, u32[]{:S(2)}) collective-permute-start(bf16[304,256]{1,0:T(8,128)(2,1)S(1)} %pad_maximum_fusion), channel_id=1, source_target_pairs={{0,4},{4,0},{1,5},{5,1},{2,6},{6,2},{3,7},{7,3},{8,12},{12,8},{9,1... | collective-permute-start | bytes 466952 | tf_op jit(solution)/shard_map/ppermute | solution.py:22
  16.1 0.6 copy-start.2
  27.1 27.5 %collective-permute-start.1 = (bf16[1152,128]{1,0:T(8,128)(2,1)S(1)}, bf16[1152,128]{1,0:T(8,128)(2,1)S(1)}, u32[]{:S(2)}, u32[]{:S(2)}) collective-permute-start(bf16[1152,128]{1,0:T(8,128)(2,1)S(1)} %get-tuple-element.13.pair), channel_id=1, source_target_pairs={{0,64},{32,480},{64,128},{96,32},{128,192},{160,96},{192,256},{224... | collective-permute-start | bytes 884744 | tf_op jit(solution)/shard_map/ppermute | solution.py:191
  36.2 31.7 %all-to-all-start.1 = ((bf16[4,288,512]{2,1,0:T(8,128)(2,1)}), bf16[4,288,512]{2,1,0:T(8,128)(2,1)S(1)}, u32[]{:S(2)}, u32[]{:S(2)}) async-start(bf16[4,288,512]{2,1,0:T(8,128)(2,1)} %get-tuple-element.17), calls=%async_computation.1 | async-start | bytes 2359296 | tf_op jit(solution)/shard_map/all_to_all | solution.py:189
  43.5 17.6 %collective-permute-start.5 = (bf16[1152,128]{1,0:T(8,128)(2,1)S(1)}, bf16[1152,128]{1,0:T(8,128)(2,1)S(1)}, u32[]{:S(2)}, u32[]{:S(2)}) collective-permute-start(bf16[1152,128]{1,0:T(8,128)(2,1)S(1)} %get-tuple-element.19.own), channel_id=1, source_target_pairs={{16,0},{24,8},{0,16},{8,24},{17,1},{25,9},{1,17},{9,25},{18,2},{26... | collective-permute-start | bytes 884744 | tf_op jit(solution)/shard_map/ppermute | solution.py:26
  48.1 16.2 %collective-permute-start.6 = (bf16[1152,128]{1,0:T(8,128)(2,1)S(1)}, bf16[1152,128]{1,0:T(8,128)(2,1)S(1)}, u32[]{:S(2)}, u32[]{:S(2)}) collective-permute-start(bf16[1152,128]{1,0:T(8,128)(2,1)S(1)} %get-tuple-element.19.own), channel_id=1, source_target_pairs={{24,0},{0,8},{8,16},{16,24},{25,1},{1,9},{9,17},{17,25},{26,2},{2,... | collective-permute-start | bytes 884744 | tf_op jit(solution)/shard_map/ppermute | solution.py:26
  50.4 14.0 %collective-permute-start.7 = (bf16[1152,128]{1,0:T(8,128)(2,1)S(1)}, bf16[1152,128]{1,0:T(8,128)(2,1)S(1)}, u32[]{:S(2)}, u32[]{:S(2)}) collective-permute-start(bf16[1152,128]{1,0:T(8,128)(2,1)S(1)} %get-tuple-element.19.own), channel_id=1, source_target_pairs={{8,0},{16,8},{24,16},{0,24},{9,1},{17,9},{25,17},{1,25},{10,2},{18... | collective-permute-start | bytes 884744 | tf_op jit(solution)/shard_map/ppermute | solution.py:26
  55.8 15.4 %collective-permute-start.2 = (bf16[1152,128]{1,0:T(8,128)(2,1)}, bf16[1152,128]{1,0:T(8,128)(2,1)S(1)}, u32[]{:S(2)}, u32[]{:S(2)}) collective-permute-start(bf16[1152,128]{1,0:T(8,128)(2,1)} %get-tuple-element.14), channel_id=1, source_target_pairs={{16,0},{24,8},{0,16},{8,24},{17,1},{25,9},{1,17},{9,25},{18,2},{26... | collective-permute-start | bytes 884744 | tf_op jit(solution)/shard_map/ppermute | solution.py:26
  57.7 17.2 %collective-permute-start.3 = (bf16[1152,128]{1,0:T(8,128)(2,1)}, bf16[1152,128]{1,0:T(8,128)(2,1)S(1)}, u32[]{:S(2)}, u32[]{:S(2)}) collective-permute-start(bf16[1152,128]{1,0:T(8,128)(2,1)} %get-tuple-element.15), channel_id=1, source_target_pairs={{8,0},{16,8},{24,16},{0,24},{9,1},{17,9},{25,17},{1,25},{10,2},{18... | collective-permute-start | bytes 884744 | tf_op jit(solution)/shard_map/ppermute | solution.py:26
  61.1 13.8 %collective-permute-start.4 = (bf16[1152,128]{1,0:T(8,128)(2,1)}, bf16[1152,128]{1,0:T(8,128)(2,1)S(1)}, u32[]{:S(2)}, u32[]{:S(2)}) collective-permute-start(bf16[1152,128]{1,0:T(8,128)(2,1)} %get-tuple-element.16), channel_id=1, source_target_pairs={{24,0},{0,8},{8,16},{16,24},{25,1},{1,9},{9,17},{17,25},{26,2},{2,... | collective-permute-start | bytes 884744 | tf_op jit(solution)/shard_map/ppermute | solution.py:26
  64.4 0.7 copy-start
  67.9 1.0 copy-start.1
  68.8 0.8 copy-start.3

commit v8 on v7

--- a/solution.py
+++ b/solution.py
@@ -33,7 +33,7 @@
     return route
 
 
-def deal_kernel(image, text, chunks, held, sems):
+def deal_kernel(image, text, chunks, held, staged, sems, out_sems):
     features, rows = image.shape
     n, half = rows // WIDTH, features // 2
     copies = [
@@ -42,13 +42,20 @@
     ]
     for copy in copies:
         copy.start()
+    sent = []
     for core in range(CORES):
         copies[core].wait()
         for w in range(WIDTH):
             part = held[core, :, w * n : (w + 1) * n]
-            part = jnp.concatenate([part[:half], part[half:]], 1)
-            for level in range(LEVELS):
-                chunks[(level * CORES + core) * WIDTH + w] = part
+            staged[core, w] = jnp.concatenate([part[:half], part[half:]], 1)
+        for level in range(LEVELS):
+            to = chunks.at[pl.ds((level * CORES + core) * WIDTH, WIDTH)]
+            sent.append(
+                pltpu.make_async_copy(staged.at[core], to, out_sems.at[level * CORES + core])
+            )
+            sent[-1].start()
+    for copy in sent:
+        copy.wait()
 
 
 def gather_kernel(dealt, own, pair):
@@ -85,11 +92,18 @@
     return jax.nn.sigmoid(scale[0] * logits + bias[0])
 
 
-def halo_kernel(pair, far, *outs):
+def halo_kernel(pair, far, o1, o2, o3, sems):
     x, level = lax.axis_index("x"), lax.axis_index("level")
-    for turn, out in enumerate(outs, 1):
-        higher = lax.rem(x + LINE - turn, LINE) > x
-        out[...] = jnp.where(higher == (level == 0), pair[...], far[...])
+    copies = []
+    for turn, out in ((1, o1), (2, o2), (3, o3)):
+        of_pair = (lax.rem(x + LINE - turn, LINE) > x) == (level == 0)
+        mine = pltpu.make_async_copy(pair, out, sems.at[turn - 1])
+        other = pltpu.make_async_copy(far, out, sems.at[turn - 1])
+        pl.when(of_pair)(mine.start)
+        pl.when(jnp.logical_not(of_pair))(other.start)
+        copies.append(mine)
+    for copy in copies:
+        copy.wait()
 
 
 def label_of(marks, n):
@@ -154,10 +168,12 @@
         deal_kernel,
         out_shape=jax.ShapeDtypeStruct((LEVELS * CORES * WIDTH, features // 2, quarter), BF16),
         in_specs=[HBM] * 2,
-        out_specs=LOCAL,
+        out_specs=HBM,
         scratch_shapes=[
             pltpu.VMEM((CORES, features, rows), BF16),
+            pltpu.VMEM((CORES, WIDTH, features // 2, quarter), BF16),
             pltpu.SemaphoreType.DMA((CORES,)),
+            pltpu.SemaphoreType.DMA((LEVELS * CORES,)),
         ],
         compiler_params=pltpu.CompilerParams(vmem_limit_bytes=60 << 20),
     )(image, text)
@@ -194,8 +210,9 @@
     s1, s2, s3 = pl.pallas_call(
         halo_kernel,
         out_shape=[piece] * 3,
-        in_specs=[LOCAL] * 2,
-        out_specs=[LOCAL] * 3,
+        in_specs=[HBM] * 2,
+        out_specs=[HBM] * 3,
+        scratch_shapes=[pltpu.SemaphoreType.DMA((LINE - 1,))],
         compiler_params=params,
         cost_estimate=pl.CostEstimate(flops=15 * 10**9, bytes_accessed=2 << 20, transcendentals=0),
     )(pair, far)

time: 110 us -> 110 us (level)
  transfers between devices with their start and end apart: 10 -> 10, of which waited for: 4 -> 4; matrix products, arithmetic and copies ran while one was open for 0% -> 0% of each run, Pallas kernels for 4% -> 3%
where the time goes in v8:
time: 110 us; the launch traced here: 109 us
  starting transfers between devices  45.9 us (42%)
  blocking collectives  31 us (28%)
  waiting for transfers between devices  17.9 us (16%)
  Pallas kernels  7.45 us (7%)
  local copies, waits for them, and re-layouts  3.05 us (3%)
  between operations  2.15 us (2%)
  other arithmetic  1.24 us (1%)
    all_to_all x1, blocking collectives, per_device(): terms = lax.all_to_all(partial, ('core', 'width'), 0, 0).astype(F32)  31 us
    ppermute x6, starting transfers between devices, along_line(): lax.ppermute(block, 'x', [((i + turn) % LINE, i) for i in range(LINE)])  18.4 us
    all_to_all x1, waiting for transfers between devices, per_device(): dealt = lax.all_to_all(chunks, ('level', 'core', 'width'), 0, 0)  10.2 us
    ppermute x1, starting transfers between devices, per_device(): far = lax.ppermute(pair, ('row', 'level'), far_route(lax.axis_size('row')))  9.06 us
    all_to_all x1, starting transfers between devices, per_device(): dealt = lax.all_to_all(chunks, ('level', 'core', 'width'), 0, 0)  8.91 us
    all_to_all x1, starting transfers between devices, per_device(): held = lax.all_to_all(spread, 'width', 0, 0)  7.27 us
    ppermute x6, waiting for transfers between devices, along_line(): lax.ppermute(block, 'x', [((i + turn) % LINE, i) for i in range(LINE)])  3.7 us
    unnamed x14, local copies, waits for them, and re-layouts  3.04 us
  transfers between devices with their start and end apart: 10, of which 4 were waited for; matrix products, arithmetic and copies ran while one was open for 0% of the time, Pallas kernels for 3%

profile of v8, /device:TPU:57, one launch (start us, length us, event | category | flops | bytes accessed | tf_op | source)
XLA Modules:
  0.0 108.6 jit_solution(9723555487096925055)
XLA Ops:
  0.7 2.0 %shard_map.68 = bf16[16,144,128]{2,1,0:T(8,128)(2,1)} custom-call(bf16[288,256]{1,0:T(8,128)(2,1)} %bitcast.19, bf16[288,256]{1,0:T(8,128)(2,1)} %bitcast.20), custom_call_target="tpu_custom_call" | custom-call | tf_op jit(solution)/shard_map/pallas_call | solution.py:167
  2.6 8.9 %all-to-all-start = ((bf16[16,144,128]{2,1,0:T(8,128)(2,1)}), bf16[16,144,128]{2,1,0:T(8,128)(2,1)S(1)}, u32[]{:S(2)}, u32[]{:S(2)}) async-start(bf16[16,144,128]{2,1,0:T(8,128)(2,1)} %shard_map.68), calls=%async_computation | async-start | bytes 1179648 | tf_op jit(solution)/shard_map/all_to_all | solution.py:180
  11.7 2.3 %collective-permute-start = (bf16[304,256]{1,0:T(8,128)(2,1)S(1)}, bf16[304,256]{1,0:T(8,128)(2,1)S(1)}, u32[]{:S(2)}, u32[]{:S(2)}) collective-permute-start(bf16[304,256]{1,0:T(8,128)(2,1)S(1)} %pad_maximum_fusion), channel_id=1, source_target_pairs={{0,4},{4,0},{1,5},{5,1},{2,6},{6,2},{3,7},{7,3},{8,12},{12,8},{9,1... | collective-permute-start | bytes 466952 | tf_op jit(solution)/shard_map/ppermute | solution.py:22
  13.9 1.0 collective-permute-done.other
  14.9 1.1 %shard_map.69 = (bf16[4,288,512]{2,1,0:T(8,128)(2,1)}, f32[16,512]{1,0:T(8,128)S(1)}) custom-call(bf16[288,256]{1,0:T(8,128)(2,1)S(1)} %get-tuple-element.23.mine, s32[1,256]{1,0:T(1,128)S(1)} %copy-done.4, bf16[304,256]{1,0:T(8,128)(2,1)S(1)} %collective-permute-done.other), custom_call_target="tpu_custom_call" | custom-call | tf_op jit(solution)/shard_map/pallas_call | solution.py:186
  16.1 0.6 copy-done.2
  16.7 10.2 %all-to-all-done.dealt = bf16[16,144,128]{2,1,0:T(8,128)(2,1)S(1)} async-done(((bf16[16,144,128]{2,1,0:T(8,128)(2,1)}), bf16[16,144,128]{2,1,0:T(8,128)(2,1)S(1)}, u32[]{:S(2)}, u32[]{:S(2)}) %all-to-all-start) | async-done | bytes 589856 | tf_op jit(solution)/shard_map/all_to_all | solution.py:180
  26.9 0.2 shard_map.70
  27.1 9.1 %collective-permute-start.1 = (bf16[1152,128]{1,0:T(8,128)(2,1)S(1)}, bf16[1152,128]{1,0:T(8,128)(2,1)S(1)}, u32[]{:S(2)}, u32[]{:S(2)}) collective-permute-start(bf16[1152,128]{1,0:T(8,128)(2,1)S(1)} %get-tuple-element.13.pair), channel_id=1, source_target_pairs={{0,64},{32,480},{64,128},{96,32},{128,192},{160,96},{192,256},{224... | collective-permute-start | bytes 884744 | tf_op jit(solution)/shard_map/ppermute | solution.py:207
  36.1 7.3 %all-to-all-start.1 = ((bf16[4,288,512]{2,1,0:T(8,128)(2,1)}), bf16[4,288,512]{2,1,0:T(8,128)(2,1)S(1)}, u32[]{:S(2)}, u32[]{:S(2)}) async-start(bf16[4,288,512]{2,1,0:T(8,128)(2,1)} %get-tuple-element.17), calls=%async_computation.1 | async-start | bytes 2359296 | tf_op jit(solution)/shard_map/all_to_all | solution.py:205
  43.4 4.6 %collective-permute-start.5 = (bf16[1152,128]{1,0:T(8,128)(2,1)S(1)}, bf16[1152,128]{1,0:T(8,128)(2,1)S(1)}, u32[]{:S(2)}, u32[]{:S(2)}) collective-permute-start(bf16[1152,128]{1,0:T(8,128)(2,1)S(1)} %get-tuple-element.19.own), channel_id=1, source_target_pairs={{16,0},{24,8},{0,16},{8,24},{17,1},{25,9},{1,17},{9,25},{18,2},{26... | collective-permute-start | bytes 884744 | tf_op jit(solution)/shard_map/ppermute | solution.py:26
  48.1 2.2 %collective-permute-start.6 = (bf16[1152,128]{1,0:T(8,128)(2,1)S(1)}, bf16[1152,128]{1,0:T(8,128)(2,1)S(1)}, u32[]{:S(2)}, u32[]{:S(2)}) collective-permute-start(bf16[1152,128]{1,0:T(8,128)(2,1)S(1)} %get-tuple-element.19.own), channel_id=1, source_target_pairs={{24,0},{0,8},{8,16},{16,24},{25,1},{1,9},{9,17},{17,25},{26,2},{2,... | collective-permute-start | bytes 884744 | tf_op jit(solution)/shard_map/ppermute | solution.py:26
  50.3 4.3 %collective-permute-start.7 = (bf16[1152,128]{1,0:T(8,128)(2,1)S(1)}, bf16[1152,128]{1,0:T(8,128)(2,1)S(1)}, u32[]{:S(2)}, u32[]{:S(2)}) collective-permute-start(bf16[1152,128]{1,0:T(8,128)(2,1)S(1)} %get-tuple-element.19.own), channel_id=1, source_target_pairs={{8,0},{16,8},{24,16},{0,24},{9,1},{17,9},{25,17},{1,25},{10,2},{18... | collective-permute-start | bytes 884744 | tf_op jit(solution)/shard_map/ppermute | solution.py:26
  54.6 0.0 collective-permute-done.1.far
  54.6 0.9 shard_map.71
  55.5 1.9 %collective-permute-start.2 = (bf16[1152,128]{1,0:T(8,128)(2,1)}, bf16[1152,128]{1,0:T(8,128)(2,1)S(1)}, u32[]{:S(2)}, u32[]{:S(2)}) collective-permute-start(bf16[1152,128]{1,0:T(8,128)(2,1)} %get-tuple-element.14), channel_id=1, source_target_pairs={{16,0},{24,8},{0,16},{8,24},{17,1},{25,9},{1,17},{9,25},{18,2},{26... | collective-permute-start | bytes 884744 | tf_op jit(solution)/shard_map/ppermute | solution.py:26
  57.5 3.4 %collective-permute-start.3 = (bf16[1152,128]{1,0:T(8,128)(2,1)}, bf16[1152,128]{1,0:T(8,128)(2,1)S(1)}, u32[]{:S(2)}, u32[]{:S(2)}) collective-permute-start(bf16[1152,128]{1,0:T(8,128)(2,1)} %get-tuple-element.15), channel_id=1, source_target_pairs={{8,0},{16,8},{24,16},{0,24},{9,1},{17,9},{25,17},{1,25},{10,2},{18... | collective-permute-start | bytes 884744 | tf_op jit(solution)/shard_map/ppermute | solution.py:26
  60.9 0.0 collective-permute-done.5.l2
  60.9 1.9 %collective-permute-start.4 = (bf16[1152,128]{1,0:T(8,128)(2,1)}, bf16[1152,128]{1,0:T(8,128)(2,1)S(1)}, u32[]{:S(2)}, u32[]{:S(2)}) collective-permute-start(bf16[1152,128]{1,0:T(8,128)(2,1)} %get-tuple-element.16), channel_id=1, source_target_pairs={{24,0},{0,8},{8,16},{16,24},{25,1},{1,9},{9,17},{17,25},{26,2},{2,... | collective-permute-start | bytes 884744 | tf_op jit(solution)/shard_map/ppermute | solution.py:26
  64.1 0.0 collective-permute-done.6.l3
  64.1 0.0 collective-permute-done.7.l1
  64.1 0.7 copy-done
  64.8 3.0 %all-to-all-done.1 = bf16[4,288,512]{2,1,0:T(8,128)(2,1)S(1)} async-done(((bf16[4,288,512]{2,1,0:T(8,128)(2,1)}), bf16[4,288,512]{2,1,0:T(8,128)(2,1)S(1)}, u32[]{:S(2)}, u32[]{:S(2)}) %all-to-all-start.1) | async-done | bytes 1179680 | tf_op jit(solution)/shard_map/all_to_all | solution.py:205
  67.8 1.0 copy-done.1
  68.8 0.8 copy-done.3
  69.5 1.6 %shard_map.72.near = f32[1152,512]{1,0:T(8,128)S(1)} custom-call(f32[1]{0:T(128)} %copy.7.scale, f32[1]{0:T(128)S(6)} %copy.8.bias, f32[16,512]{1,0:T(8,128)S(1)} %copy-done.3, bf16[1152,128]{1,0:T(8,128)(2,1)S(1)} %get-tuple-element.19.own, bf16[1152,128]{1,0:T(8,128)(2,1)S(1)} %collective-permute-done.5.l2, ...), custom_call_target="tpu_custom_call" | custom-call | flops 1207959552 | bytes 5242880 | tf_op jit(solution)/shard_map/pallas_call | solution.py:225
  71.1 0.0 collective-permute-done.2.h2
  71.1 3.7 %collective-permute-done.3.h1 = bf16[1152,128]{1,0:T(8,128)(2,1)S(1)} collective-permute-done((bf16[1152,128]{1,0:T(8,128)(2,1)}, bf16[1152,128]{1,0:T(8,128)(2,1)S(1)}, u32[]{:S(2)}, u32[]{:S(2)}) %collective-permute-start.3) | collective-permute-done | bytes 294944 | tf_op jit(solution)/shard_map/ppermute | solution.py:26
  74.8 1.6 %shard_map.73 = bf16[8,288,256]{2,1,0:T(8,128)(2,1)S(1)} custom-call(f32[1]{0:T(128)} %copy.7.scale, f32[1]{0:T(128)S(6)} %copy.8.bias, bf16[1152,128]{1,0:T(8,128)(2,1)S(1)} %get-tuple-element.13.pair, bf16[1152,128]{1,0:T(8,128)(2,1)S(1)} %collective-permute-done.1.far, bf16[1152,128]{1,0:T(8,128)(2,1)S(1)} %collective-permute-done.2.h2, ...), custom_call_target="tpu_custom_call" | custom-call | flops 1207959552 | bytes 5242880 | tf_op jit(solution)/shard_map/pallas_call | solution.py:233
  76.4 31.0 %all_to_all.15 = bf16[8,288,256]{2,1,0:T(8,128)(2,1)S(1)} all-to-all(bf16[8,288,256]{2,1,0:T(8,128)(2,1)S(1)} %shard_map.73), channel_id=1, replica_groups=mesh['row'=8,'level'=2,'x'=4,'core'=2,'width'=4] {'core','width'}, dimensions={0} | all-to-all | bytes 2359296 | tf_op jit(solution)/shard_map/all_to_all | solution.py:241
  107.5 0.2 convert_element_type.7
  107.7 1.0 fusion.1
  (15 shorter events, 0.1 us)
Async XLA Ops:
  0.6 10.9 %copy-start.5 = (bf16[256,288]{0,1:T(8,128)(2,1)S(1)}, bf16[256,288]{0,1:T(8,128)(2,1)}, u32[]{:S(2)}) copy-start(bf16[256,288]{0,1:T(8,128)(2,1)} %param.5) | copy-start | bytes 442372
  0.6 10.9 %copy-start.6 = (bf16[256,288]{0,1:T(8,128)(2,1)S(1)}, bf16[256,288]{0,1:T(8,128)(2,1)}, u32[]{:S(2)}) copy-start(bf16[256,288]{0,1:T(8,128)(2,1)} %param.6) | copy-start | bytes 442372
  0.6 10.9 %copy-start.4 = (s32[1,256]{1,0:T(1,128)S(1)}, s32[1,256]{1,0:T(1,128)}, u32[]{:S(2)}) copy-start(s32[1,256]{1,0:T(1,128)} %matches.1) | copy-start | bytes 3076
  2.6 24.2 %all-to-all-start = ((bf16[16,144,128]{2,1,0:T(8,128)(2,1)}), bf16[16,144,128]{2,1,0:T(8,128)(2,1)S(1)}, u32[]{:S(2)}, u32[]{:S(2)}) async-start(bf16[16,144,128]{2,1,0:T(8,128)(2,1)} %shard_map.68), calls=%async_computation | async-start | bytes 1179648 | tf_op jit(solution)/shard_map/all_to_all | solution.py:180
  11.7 3.3 %collective-permute-start = (bf16[304,256]{1,0:T(8,128)(2,1)S(1)}, bf16[304,256]{1,0:T(8,128)(2,1)S(1)}, u32[]{:S(2)}, u32[]{:S(2)}) collective-permute-start(bf16[304,256]{1,0:T(8,128)(2,1)S(1)} %pad_maximum_fusion), channel_id=1, source_target_pairs={{0,4},{4,0},{1,5},{5,1},{2,6},{6,2},{3,7},{7,3},{8,12},{12,8},{9,1... | collective-permute-start | bytes 466952 | tf_op jit(solution)/shard_map/ppermute | solution.py:22
  16.1 0.6 copy-start.2
  27.1 27.5 %collective-permute-start.1 = (bf16[1152,128]{1,0:T(8,128)(2,1)S(1)}, bf16[1152,128]{1,0:T(8,128)(2,1)S(1)}, u32[]{:S(2)}, u32[]{:S(2)}) collective-permute-start(bf16[1152,128]{1,0:T(8,128)(2,1)S(1)} %get-tuple-element.13.pair), channel_id=1, source_target_pairs={{0,64},{32,480},{64,128},{96,32},{128,192},{160,96},{192,256},{224... | collective-permute-start | bytes 884744 | tf_op jit(solution)/shard_map/ppermute | solution.py:207
  36.1 31.7 %all-to-all-start.1 = ((bf16[4,288,512]{2,1,0:T(8,128)(2,1)}), bf16[4,288,512]{2,1,0:T(8,128)(2,1)S(1)}, u32[]{:S(2)}, u32[]{:S(2)}) async-start(bf16[4,288,512]{2,1,0:T(8,128)(2,1)} %get-tuple-element.17), calls=%async_computation.1 | async-start | bytes 2359296 | tf_op jit(solution)/shard_map/all_to_all | solution.py:205
  43.4 17.5 %collective-permute-start.5 = (bf16[1152,128]{1,0:T(8,128)(2,1)S(1)}, bf16[1152,128]{1,0:T(8,128)(2,1)S(1)}, u32[]{:S(2)}, u32[]{:S(2)}) collective-permute-start(bf16[1152,128]{1,0:T(8,128)(2,1)S(1)} %get-tuple-element.19.own), channel_id=1, source_target_pairs={{16,0},{24,8},{0,16},{8,24},{17,1},{25,9},{1,17},{9,25},{18,2},{26... | collective-permute-start | bytes 884744 | tf_op jit(solution)/shard_map/ppermute | solution.py:26
  48.1 16.0 %collective-permute-start.6 = (bf16[1152,128]{1,0:T(8,128)(2,1)S(1)}, bf16[1152,128]{1,0:T(8,128)(2,1)S(1)}, u32[]{:S(2)}, u32[]{:S(2)}) collective-permute-start(bf16[1152,128]{1,0:T(8,128)(2,1)S(1)} %get-tuple-element.19.own), channel_id=1, source_target_pairs={{24,0},{0,8},{8,16},{16,24},{25,1},{1,9},{9,17},{17,25},{26,2},{2,... | collective-permute-start | bytes 884744 | tf_op jit(solution)/shard_map/ppermute | solution.py:26
  50.3 13.8 %collective-permute-start.7 = (bf16[1152,128]{1,0:T(8,128)(2,1)S(1)}, bf16[1152,128]{1,0:T(8,128)(2,1)S(1)}, u32[]{:S(2)}, u32[]{:S(2)}) collective-permute-start(bf16[1152,128]{1,0:T(8,128)(2,1)S(1)} %get-tuple-element.19.own), channel_id=1, source_target_pairs={{8,0},{16,8},{24,16},{0,24},{9,1},{17,9},{25,17},{1,25},{10,2},{18... | collective-permute-start | bytes 884744 | tf_op jit(solution)/shard_map/ppermute | solution.py:26
  55.5 15.6 %collective-permute-start.2 = (bf16[1152,128]{1,0:T(8,128)(2,1)}, bf16[1152,128]{1,0:T(8,128)(2,1)S(1)}, u32[]{:S(2)}, u32[]{:S(2)}) collective-permute-start(bf16[1152,128]{1,0:T(8,128)(2,1)} %get-tuple-element.14), channel_id=1, source_target_pairs={{16,0},{24,8},{0,16},{8,24},{17,1},{25,9},{1,17},{9,25},{18,2},{26... | collective-permute-start | bytes 884744 | tf_op jit(solution)/shard_map/ppermute | solution.py:26
  57.5 17.4 %collective-permute-start.3 = (bf16[1152,128]{1,0:T(8,128)(2,1)}, bf16[1152,128]{1,0:T(8,128)(2,1)S(1)}, u32[]{:S(2)}, u32[]{:S(2)}) collective-permute-start(bf16[1152,128]{1,0:T(8,128)(2,1)} %get-tuple-element.15), channel_id=1, source_target_pairs={{8,0},{16,8},{24,16},{0,24},{9,1},{17,9},{25,17},{1,25},{10,2},{18... | collective-permute-start | bytes 884744 | tf_op jit(solution)/shard_map/ppermute | solution.py:26
  60.9 14.0 %collective-permute-start.4 = (bf16[1152,128]{1,0:T(8,128)(2,1)}, bf16[1152,128]{1,0:T(8,128)(2,1)S(1)}, u32[]{:S(2)}, u32[]{:S(2)}) collective-permute-start(bf16[1152,128]{1,0:T(8,128)(2,1)} %get-tuple-element.16), channel_id=1, source_target_pairs={{24,0},{0,8},{8,16},{16,24},{25,1},{1,9},{9,17},{17,25},{26,2},{2,... | collective-permute-start | bytes 884744 | tf_op jit(solution)/shard_map/ppermute | solution.py:26
  64.1 0.7 copy-start
  67.8 1.0 copy-start.1
  68.8 0.8 copy-start.3

commit v9 on v7

--- a/solution.py
+++ b/solution.py
@@ -106,34 +106,34 @@
     return ((have == goal) & (lane // rows == block)).astype(F32)
 
 
-def near_kernel(scale, bias, marks, own, l2, l3, l1, held, out):
-    n = l1.shape[1]
-    pieces = jnp.concatenate([own[...], l1[...], l2[...], l3[...]], 1)
-    probs = weighed(pieces, held, scale, bias)
-    weights = jnp.concatenate([(probs[:n] - label_of(marks, n)).astype(BF16), probs[n:].astype(BF16)], 0)
-    out[...] = jnp.dot(pieces, weights, preferred_element_type=F32)
-
-
-def far_kernel(scale, bias, pair, far, h2, h1, h3, held, near, out):
-    whole, n = h1.shape
+def near_kernel(scale, bias, marks, own, pair, far, l2, l3, l1, held, out):
+    whole, n = l1.shape
     span = held.shape[1]
     rows = span // CORES
-    features = whole // WIDTH
-    level = lax.axis_index("level")
     side = lax.broadcasted_iota(jnp.int32, (whole, n), 1) < n // CORES
-    last = jnp.where(side == (level == 0), pair[...], far[...])
-    pieces = jnp.concatenate([last, h1[...], h2[...], h3[...]], 1)
+    last = jnp.where(side == (lax.axis_index("level") == 0), pair[...], far[...])
+    pieces = jnp.concatenate([own[...], l1[...], l2[...], l3[...], last], 1)
     probs = weighed(pieces, held, scale, bias)
     lane = lax.broadcasted_iota(jnp.int32, (n, span), 1)
     down = lax.broadcasted_iota(jnp.int32, (n, span), 0)
     met = lane // rows != down // (n // CORES)
+    end = probs.shape[0] - n
     weights = jnp.concatenate(
         [
-            jnp.where(met, probs[:n], 0.0).astype(BF16),
-            probs[n:].astype(BF16),
+            (probs[:n] - label_of(marks, n)).astype(BF16),
+            probs[n:end].astype(BF16),
+            jnp.where(met, probs[end:], 0.0).astype(BF16),
         ],
         0,
     )
+    out[...] = jnp.dot(pieces, weights, preferred_element_type=F32)
+
+
+def far_kernel(scale, bias, h2, h1, h3, held, near, out):
+    rows = held.shape[1] // CORES
+    features = h1.shape[0] // WIDTH
+    pieces = jnp.concatenate([h1[...], h2[...], h3[...]], 1)
+    weights = weighed(pieces, held, scale, bias).astype(BF16)
     for to in range(WIDTH):
         at = slice(to * features, (to + 1) * features)
         total = near[at, :] + jnp.dot(pieces[at], weights, preferred_element_type=F32)
@@ -208,19 +208,19 @@
     near = pl.pallas_call(
         near_kernel,
         out_shape=jax.ShapeDtypeStruct((whole, span), F32),
-        in_specs=[SMEM, SMEM] + [LOCAL] * 6,
+        in_specs=[SMEM, SMEM] + [LOCAL] * 8,
         out_specs=LOCAL,
         compiler_params=params,
         cost_estimate=cost,
-    )(scale, shift_bias, marks, own, l2, l3, l1, held)
+    )(scale, shift_bias, marks, own, pair, far, l2, l3, l1, held)
     partial = pl.pallas_call(
         far_kernel,
         out_shape=jax.ShapeDtypeStruct((CORES * WIDTH, features, rows), BF16),
-        in_specs=[SMEM, SMEM] + [LOCAL] * 7,
+        in_specs=[SMEM, SMEM] + [LOCAL] * 5,
         out_specs=LOCAL,
         compiler_params=params,
         cost_estimate=cost,
-    )(scale, shift_bias, pair, far, h2, h1, h3, held, near)
+    )(scale, shift_bias, h2, h1, h3, held, near)
     terms = lax.all_to_all(partial, ("core", "width"), 0, 0).astype(F32)
     grad_text = terms[0] + terms[1] + terms[2] + terms[3]
     grad_image = terms[4] + terms[5] + terms[6] + terms[7]

time: 110 us -> 111 us (level)
  local copies, waits for them, and re-layouts: 3.05 us -> 1.37 us
  waiting for transfers between devices: 17.7 us -> 19 us
  Pallas kernels: 7.7 us -> 8.98 us
    unnamed x14 -> x10, local copies, waits for them, and re-layouts: 3.04 us -> 1.37 us
where the time goes in v9:
time: 111 us; the launch traced here: 109 us
  starting transfers between devices  45.9 us (41%)
  blocking collectives  30.9 us (28%)
  waiting for transfers between devices  19 us (17%)
  Pallas kernels  8.98 us (8%)
  between operations  2.13 us (2%)
  local copies, waits for them, and re-layouts  1.37 us (1%)
  other arithmetic  1.24 us (1%)
    all_to_all x1, blocking collectives, per_device(): terms = lax.all_to_all(partial, ('core', 'width'), 0, 0).astype(F32)  30.9 us
    ppermute x6, starting transfers between devices, along_line(): lax.ppermute(block, 'x', [((i + turn) % LINE, i) for i in range(LINE)])  18.4 us
    all_to_all x1, waiting for transfers between devices, per_device(): dealt = lax.all_to_all(chunks, ('level', 'core', 'width'), 0, 0)  10.2 us
    ppermute x1, starting transfers between devices, per_device(): far = lax.ppermute(pair, ('row', 'level'), far_route(lax.axis_size('row')))  9.06 us
    all_to_all x1, starting transfers between devices, per_device(): dealt = lax.all_to_all(chunks, ('level', 'core', 'width'), 0, 0)  8.91 us
    all_to_all x1, starting transfers between devices, per_device(): held = lax.all_to_all(spread, 'width', 0, 0)  7.27 us
    ppermute x6, waiting for transfers between devices, along_line(): lax.ppermute(block, 'x', [((i + turn) % LINE, i) for i in range(LINE)])  4.32 us
    all_to_all x1, waiting for transfers between devices, per_device(): held = lax.all_to_all(spread, 'width', 0, 0)  3.53 us
  transfers between devices with their start and end apart: 10, of which 4 were waited for; matrix products, arithmetic and copies ran while one was open for 0% of the time, Pallas kernels for 4%

profile of v9, /device:TPU:57, one launch (start us, length us, event | category | flops | bytes accessed | tf_op | source)
XLA Modules:
  0.0 109.5 jit_solution(17997647004079279985)
XLA Ops:
  0.7 2.0 %shard_map.68 = bf16[16,144,128]{2,1,0:T(8,128)(2,1)} custom-call(bf16[288,256]{1,0:T(8,128)(2,1)} %bitcast.19, bf16[288,256]{1,0:T(8,128)(2,1)} %bitcast.20), custom_call_target="tpu_custom_call" | custom-call | tf_op jit(solution)/shard_map/pallas_call | solution.py:153
  2.7 8.9 %all-to-all-start = ((bf16[16,144,128]{2,1,0:T(8,128)(2,1)}), bf16[16,144,128]{2,1,0:T(8,128)(2,1)S(1)}, u32[]{:S(2)}, u32[]{:S(2)}) async-start(bf16[16,144,128]{2,1,0:T(8,128)(2,1)} %shard_map.68), calls=%async_computation | async-start | bytes 1179648 | tf_op jit(solution)/shard_map/all_to_all | solution.py:164
  11.7 0.0 copy-done.4
  11.7 2.3 %collective-permute-start = (bf16[304,256]{1,0:T(8,128)(2,1)S(1)}, bf16[304,256]{1,0:T(8,128)(2,1)S(1)}, u32[]{:S(2)}, u32[]{:S(2)}) collective-permute-start(bf16[304,256]{1,0:T(8,128)(2,1)S(1)} %pad_maximum_fusion), channel_id=1, source_target_pairs={{0,4},{4,0},{1,5},{5,1},{2,6},{6,2},{3,7},{7,3},{8,12},{12,8},{9,1... | collective-permute-start | bytes 466952 | tf_op jit(solution)/shard_map/ppermute | solution.py:22
  14.0 1.0 collective-permute-done.other
  15.0 1.2 %shard_map.69 = (bf16[4,288,512]{2,1,0:T(8,128)(2,1)}, f32[16,512]{1,0:T(8,128)S(1)}) custom-call(bf16[288,256]{1,0:T(8,128)(2,1)S(1)} %get-tuple-element.23.mine, s32[1,256]{1,0:T(1,128)S(1)} %copy-done.2, bf16[304,256]{1,0:T(8,128)(2,1)S(1)} %collective-permute-done.other), custom_call_target="tpu_custom_call" | custom-call | tf_op jit(solution)/shard_map/pallas_call | solution.py:170
  16.2 0.6 copy-done
  16.8 10.2 %all-to-all-done.dealt = bf16[16,144,128]{2,1,0:T(8,128)(2,1)S(1)} async-done(((bf16[16,144,128]{2,1,0:T(8,128)(2,1)}), bf16[16,144,128]{2,1,0:T(8,128)(2,1)S(1)}, u32[]{:S(2)}, u32[]{:S(2)}) %all-to-all-start) | async-done | bytes 589856 | tf_op jit(solution)/shard_map/all_to_all | solution.py:164
  26.9 0.2 shard_map.70
  27.1 9.1 %collective-permute-start.1 = (bf16[1152,128]{1,0:T(8,128)(2,1)S(1)}, bf16[1152,128]{1,0:T(8,128)(2,1)S(1)}, u32[]{:S(2)}, u32[]{:S(2)}) collective-permute-start(bf16[1152,128]{1,0:T(8,128)(2,1)S(1)} %get-tuple-element.13.pair), channel_id=1, source_target_pairs={{0,64},{32,480},{64,128},{96,32},{128,192},{160,96},{192,256},{224... | collective-permute-start | bytes 884744 | tf_op jit(solution)/shard_map/ppermute | solution.py:191
  36.2 7.3 %all-to-all-start.1 = ((bf16[4,288,512]{2,1,0:T(8,128)(2,1)}), bf16[4,288,512]{2,1,0:T(8,128)(2,1)S(1)}, u32[]{:S(2)}, u32[]{:S(2)}) async-start(bf16[4,288,512]{2,1,0:T(8,128)(2,1)} %get-tuple-element.17), calls=%async_computation.1 | async-start | bytes 2359296 | tf_op jit(solution)/shard_map/all_to_all | solution.py:189
  43.5 4.6 %collective-permute-start.5 = (bf16[1152,128]{1,0:T(8,128)(2,1)S(1)}, bf16[1152,128]{1,0:T(8,128)(2,1)S(1)}, u32[]{:S(2)}, u32[]{:S(2)}) collective-permute-start(bf16[1152,128]{1,0:T(8,128)(2,1)S(1)} %get-tuple-element.19.own), channel_id=1, source_target_pairs={{16,0},{24,8},{0,16},{8,24},{17,1},{25,9},{1,17},{9,25},{18,2},{26... | collective-permute-start | bytes 884744 | tf_op jit(solution)/shard_map/ppermute | solution.py:26
  48.1 2.2 %collective-permute-start.6 = (bf16[1152,128]{1,0:T(8,128)(2,1)S(1)}, bf16[1152,128]{1,0:T(8,128)(2,1)S(1)}, u32[]{:S(2)}, u32[]{:S(2)}) collective-permute-start(bf16[1152,128]{1,0:T(8,128)(2,1)S(1)} %get-tuple-element.19.own), channel_id=1, source_target_pairs={{24,0},{0,8},{8,16},{16,24},{25,1},{1,9},{9,17},{17,25},{26,2},{2,... | collective-permute-start | bytes 884744 | tf_op jit(solution)/shard_map/ppermute | solution.py:26
  50.4 4.3 %collective-permute-start.7 = (bf16[1152,128]{1,0:T(8,128)(2,1)S(1)}, bf16[1152,128]{1,0:T(8,128)(2,1)S(1)}, u32[]{:S(2)}, u32[]{:S(2)}) collective-permute-start(bf16[1152,128]{1,0:T(8,128)(2,1)S(1)} %get-tuple-element.19.own), channel_id=1, source_target_pairs={{8,0},{16,8},{24,16},{0,24},{9,1},{17,9},{25,17},{1,25},{10,2},{18... | collective-permute-start | bytes 884744 | tf_op jit(solution)/shard_map/ppermute | solution.py:26
  54.6 0.0 collective-permute-done.1.far
  54.7 1.1 %shard_map.71 = (bf16[1152,128]{1,0:T(8,128)(2,1)}, bf16[1152,128]{1,0:T(8,128)(2,1)}, bf16[1152,128]{1,0:T(8,128)(2,1)}) custom-call(bf16[1152,128]{1,0:T(8,128)(2,1)S(1)} %get-tuple-element.13.pair, bf16[1152,128]{1,0:T(8,128)(2,1)S(1)} %collective-permute-done.1.far), custom_call_target="tpu_custom_call" | custom-call | flops 15000000512 | bytes 2097152 | tf_op jit(solution)/shard_map/pallas_call | solution.py:194
  55.8 1.9 %collective-permute-start.2 = (bf16[1152,128]{1,0:T(8,128)(2,1)}, bf16[1152,128]{1,0:T(8,128)(2,1)S(1)}, u32[]{:S(2)}, u32[]{:S(2)}) collective-permute-start(bf16[1152,128]{1,0:T(8,128)(2,1)} %get-tuple-element.14), channel_id=1, source_target_pairs={{16,0},{24,8},{0,16},{8,24},{17,1},{25,9},{1,17},{9,25},{18,2},{26... | collective-permute-start | bytes 884744 | tf_op jit(solution)/shard_map/ppermute | solution.py:26
  57.7 3.4 %collective-permute-start.3 = (bf16[1152,128]{1,0:T(8,128)(2,1)}, bf16[1152,128]{1,0:T(8,128)(2,1)S(1)}, u32[]{:S(2)}, u32[]{:S(2)}) collective-permute-start(bf16[1152,128]{1,0:T(8,128)(2,1)} %get-tuple-element.15), channel_id=1, source_target_pairs={{8,0},{16,8},{24,16},{0,24},{9,1},{17,9},{25,17},{1,25},{10,2},{18... | collective-permute-start | bytes 884744 | tf_op jit(solution)/shard_map/ppermute | solution.py:26
  61.1 0.0 collective-permute-done.5.l2
  61.1 1.9 %collective-permute-start.4 = (bf16[1152,128]{1,0:T(8,128)(2,1)}, bf16[1152,128]{1,0:T(8,128)(2,1)}, u32[]{:S(2)}, u32[]{:S(2)}) collective-permute-start(bf16[1152,128]{1,0:T(8,128)(2,1)} %get-tuple-element.16), channel_id=1, source_target_pairs={{24,0},{0,8},{8,16},{16,24},{25,1},{1,9},{9,17},{17,25},{26,2},{2,... | collective-permute-start | bytes 884744 | tf_op jit(solution)/shard_map/ppermute | solution.py:26
  64.3 0.0 collective-permute-done.6.l3
  64.4 0.0 collective-permute-done.7.l1
  64.4 3.5 %all-to-all-done.1 = bf16[4,288,512]{2,1,0:T(8,128)(2,1)S(1)} async-done(((bf16[4,288,512]{2,1,0:T(8,128)(2,1)}), bf16[4,288,512]{2,1,0:T(8,128)(2,1)S(1)}, u32[]{:S(2)}, u32[]{:S(2)}) %all-to-all-start.1) | async-done | bytes 1179680 | tf_op jit(solution)/shard_map/all_to_all | solution.py:189
  67.9 0.8 copy-done.1
  68.7 2.0 %shard_map.72.near = f32[1152,512]{1,0:T(8,128)S(1)} custom-call(f32[1]{0:T(128)} %copy.7.scale, f32[1]{0:T(128)S(6)} %copy.8.bias, f32[16,512]{1,0:T(8,128)S(1)} %copy-done.1, bf16[1152,128]{1,0:T(8,128)(2,1)S(1)} %get-tuple-element.19.own, bf16[1152,128]{1,0:T(8,128)(2,1)S(1)} %get-tuple-element.13.pair, bf16[1152,128]{1,0:T(8,128)(2,1)S(1)} %collective-permute-done.1.far, ...), custom_call_target="tpu_custom_call" | custom-call | flops 1207959552 | bytes 5242880 | tf_op jit(solution)/shard_map/pallas_call | solution.py:208
  70.7 0.0 collective-permute-done.2.h2
  70.7 4.3 %collective-permute-done.3.h1 = bf16[1152,128]{1,0:T(8,128)(2,1)S(1)} collective-permute-done((bf16[1152,128]{1,0:T(8,128)(2,1)}, bf16[1152,128]{1,0:T(8,128)(2,1)S(1)}, u32[]{:S(2)}, u32[]{:S(2)}) %collective-permute-start.3) | collective-permute-done | bytes 294944 | tf_op jit(solution)/shard_map/ppermute | solution.py:26
  75.0 0.0 collective-permute-done.4.h3
  75.0 2.4 %shard_map.73 = bf16[8,288,256]{2,1,0:T(8,128)(2,1)S(1)} custom-call(f32[1]{0:T(128)} %copy.7.scale, f32[1]{0:T(128)S(6)} %copy.8.bias, bf16[1152,128]{1,0:T(8,128)(2,1)S(1)} %collective-permute-done.2.h2, bf16[1152,128]{1,0:T(8,128)(2,1)S(1)} %collective-permute-done.3.h1, bf16[1152,128]{1,0:T(8,128)(2,1)} %collective-permute-done.4.h3, ...), custom_call_target="tpu_custom_call" | custom-call | flops 1207959552 | bytes 5242880 | tf_op jit(solution)/shard_map/pallas_call | solution.py:216
  77.4 30.9 %all_to_all.15 = bf16[8,288,256]{2,1,0:T(8,128)(2,1)S(1)} all-to-all(bf16[8,288,256]{2,1,0:T(8,128)(2,1)S(1)} %shard_map.73), channel_id=1, replica_groups=mesh['row'=8,'level'=2,'x'=4,'core'=2,'width'=4] {'core','width'}, dimensions={0} | all-to-all | bytes 2359296 | tf_op jit(solution)/shard_map/all_to_all | solution.py:224
  108.3 0.2 convert_element_type.7
  108.5 1.0 fusion.1
  (11 shorter events, 0.1 us)
Async XLA Ops:
  0.6 11.0 %copy-start.3 = (bf16[256,288]{0,1:T(8,128)(2,1)S(1)}, bf16[256,288]{0,1:T(8,128)(2,1)}, u32[]{:S(2)}) copy-start(bf16[256,288]{0,1:T(8,128)(2,1)} %param.5) | copy-start | bytes 442372
  0.6 11.0 %copy-start.4 = (bf16[256,288]{0,1:T(8,128)(2,1)S(1)}, bf16[256,288]{0,1:T(8,128)(2,1)}, u32[]{:S(2)}) copy-start(bf16[256,288]{0,1:T(8,128)(2,1)} %param.6) | copy-start | bytes 442372
  0.6 11.0 %copy-start.2 = (s32[1,256]{1,0:T(1,128)S(1)}, s32[1,256]{1,0:T(1,128)}, u32[]{:S(2)}) copy-start(s32[1,256]{1,0:T(1,128)} %matches.1) | copy-start | bytes 3076
  2.7 24.2 %all-to-all-start = ((bf16[16,144,128]{2,1,0:T(8,128)(2,1)}), bf16[16,144,128]{2,1,0:T(8,128)(2,1)S(1)}, u32[]{:S(2)}, u32[]{:S(2)}) async-start(bf16[16,144,128]{2,1,0:T(8,128)(2,1)} %shard_map.68), calls=%async_computation | async-start | bytes 1179648 | tf_op jit(solution)/shard_map/all_to_all | solution.py:164
  11.7 3.3 %collective-permute-start = (bf16[304,256]{1,0:T(8,128)(2,1)S(1)}, bf16[304,256]{1,0:T(8,128)(2,1)S(1)}, u32[]{:S(2)}, u32[]{:S(2)}) collective-permute-start(bf16[304,256]{1,0:T(8,128)(2,1)S(1)} %pad_maximum_fusion), channel_id=1, source_target_pairs={{0,4},{4,0},{1,5},{5,1},{2,6},{6,2},{3,7},{7,3},{8,12},{12,8},{9,1... | collective-permute-start | bytes 466952 | tf_op jit(solution)/shard_map/ppermute | solution.py:22
  16.2 0.6 copy-start
  27.1 27.5 %collective-permute-start.1 = (bf16[1152,128]{1,0:T(8,128)(2,1)S(1)}, bf16[1152,128]{1,0:T(8,128)(2,1)S(1)}, u32[]{:S(2)}, u32[]{:S(2)}) collective-permute-start(bf16[1152,128]{1,0:T(8,128)(2,1)S(1)} %get-tuple-element.13.pair), channel_id=1, source_target_pairs={{0,64},{32,480},{64,128},{96,32},{128,192},{160,96},{192,256},{224... | collective-permute-start | bytes 884744 | tf_op jit(solution)/shard_map/ppermute | solution.py:191
  36.2 31.7 %all-to-all-start.1 = ((bf16[4,288,512]{2,1,0:T(8,128)(2,1)}), bf16[4,288,512]{2,1,0:T(8,128)(2,1)S(1)}, u32[]{:S(2)}, u32[]{:S(2)}) async-start(bf16[4,288,512]{2,1,0:T(8,128)(2,1)} %get-tuple-element.17), calls=%async_computation.1 | async-start | bytes 2359296 | tf_op jit(solution)/shard_map/all_to_all | solution.py:189
  43.5 17.6 %collective-permute-start.5 = (bf16[1152,128]{1,0:T(8,128)(2,1)S(1)}, bf16[1152,128]{1,0:T(8,128)(2,1)S(1)}, u32[]{:S(2)}, u32[]{:S(2)}) collective-permute-start(bf16[1152,128]{1,0:T(8,128)(2,1)S(1)} %get-tuple-element.19.own), channel_id=1, source_target_pairs={{16,0},{24,8},{0,16},{8,24},{17,1},{25,9},{1,17},{9,25},{18,2},{26... | collective-permute-start | bytes 884744 | tf_op jit(solution)/shard_map/ppermute | solution.py:26
  48.1 16.2 %collective-permute-start.6 = (bf16[1152,128]{1,0:T(8,128)(2,1)S(1)}, bf16[1152,128]{1,0:T(8,128)(2,1)S(1)}, u32[]{:S(2)}, u32[]{:S(2)}) collective-permute-start(bf16[1152,128]{1,0:T(8,128)(2,1)S(1)} %get-tuple-element.19.own), channel_id=1, source_target_pairs={{24,0},{0,8},{8,16},{16,24},{25,1},{1,9},{9,17},{17,25},{26,2},{2,... | collective-permute-start | bytes 884744 | tf_op jit(solution)/shard_map/ppermute | solution.py:26
  50.4 14.0 %collective-permute-start.7 = (bf16[1152,128]{1,0:T(8,128)(2,1)S(1)}, bf16[1152,128]{1,0:T(8,128)(2,1)S(1)}, u32[]{:S(2)}, u32[]{:S(2)}) collective-permute-start(bf16[1152,128]{1,0:T(8,128)(2,1)S(1)} %get-tuple-element.19.own), channel_id=1, source_target_pairs={{8,0},{16,8},{24,16},{0,24},{9,1},{17,9},{25,17},{1,25},{10,2},{18... | collective-permute-start | bytes 884744 | tf_op jit(solution)/shard_map/ppermute | solution.py:26
  55.8 14.9 %collective-permute-start.2 = (bf16[1152,128]{1,0:T(8,128)(2,1)}, bf16[1152,128]{1,0:T(8,128)(2,1)S(1)}, u32[]{:S(2)}, u32[]{:S(2)}) collective-permute-start(bf16[1152,128]{1,0:T(8,128)(2,1)} %get-tuple-element.14), channel_id=1, source_target_pairs={{16,0},{24,8},{0,16},{8,24},{17,1},{25,9},{1,17},{9,25},{18,2},{26... | collective-permute-start | bytes 884744 | tf_op jit(solution)/shard_map/ppermute | solution.py:26
  57.7 17.3 %collective-permute-start.3 = (bf16[1152,128]{1,0:T(8,128)(2,1)}, bf16[1152,128]{1,0:T(8,128)(2,1)S(1)}, u32[]{:S(2)}, u32[]{:S(2)}) collective-permute-start(bf16[1152,128]{1,0:T(8,128)(2,1)} %get-tuple-element.15), channel_id=1, source_target_pairs={{8,0},{16,8},{24,16},{0,24},{9,1},{17,9},{25,17},{1,25},{10,2},{18... | collective-permute-start | bytes 884744 | tf_op jit(solution)/shard_map/ppermute | solution.py:26
  61.1 13.9 %collective-permute-start.4 = (bf16[1152,128]{1,0:T(8,128)(2,1)}, bf16[1152,128]{1,0:T(8,128)(2,1)}, u32[]{:S(2)}, u32[]{:S(2)}) collective-permute-start(bf16[1152,128]{1,0:T(8,128)(2,1)} %get-tuple-element.16), channel_id=1, source_target_pairs={{24,0},{0,8},{8,16},{16,24},{25,1},{1,9},{9,17},{17,25},{26,2},{2,... | collective-permute-start | bytes 884744 | tf_op jit(solution)/shard_map/ppermute | solution.py:26
  67.9 0.8 copy-start.1

commit v10 on v7

--- a/solution.py
+++ b/solution.py
@@ -163,7 +163,7 @@
     )(image, text)
     dealt = lax.all_to_all(chunks, ("level", "core", "width"), 0, 0)
 
-    params = pltpu.CompilerParams(vmem_limit_bytes=6 << 20)
+    params = pltpu.CompilerParams(vmem_limit_bytes=4 << 20)
     first = lax.axis_index("core") == 0
     noted = jnp.broadcast_to(matches.astype(BF16), (MARKS, rows))
     other = swap_cores(jnp.concatenate([jnp.where(first, image, text), noted], 0))
@@ -204,7 +204,7 @@
     cost = pl.CostEstimate(
         flops=2 * whole * PIECES * quarter * span, bytes_accessed=5 << 20, transcendentals=0
     )
-    params = pltpu.CompilerParams(vmem_limit_bytes=12 << 20)
+    params = pltpu.CompilerParams(vmem_limit_bytes=4 << 20)
     near = pl.pallas_call(
         near_kernel,
         out_shape=jax.ShapeDtypeStruct((whole, span), F32),

time: 110 us -> 110 us (level)
  no operation moved by 1% of the time
where the time goes in v10:
time: 110 us; the launch traced here: 109 us
  starting transfers between devices  45.9 us (42%)
  blocking collectives  31 us (28%)
  waiting for transfers between devices  17.7 us (16%)
  Pallas kernels  7.7 us (7%)
  local copies, waits for them, and re-layouts  3.05 us (3%)
  between operations  2.14 us (2%)
  other arithmetic  1.24 us (1%)
    all_to_all x1, blocking collectives, per_device(): terms = lax.all_to_all(partial, ('core', 'width'), 0, 0).astype(F32)  31 us
    ppermute x6, starting transfers between devices, along_line(): lax.ppermute(block, 'x', [((i + turn) % LINE, i) for i in range(LINE)])  18.4 us
    all_to_all x1, waiting for transfers between devices, per_device(): dealt = lax.all_to_all(chunks, ('level', 'core', 'width'), 0, 0)  10.2 us
    ppermute x1, starting transfers between devices, per_device(): far = lax.ppermute(pair, ('row', 'level'), far_route(lax.axis_size('row')))  9.06 us
    all_to_all x1, starting transfers between devices, per_device(): dealt = lax.all_to_all(chunks, ('level', 'core', 'width'), 0, 0)  8.91 us
    all_to_all x1, starting transfers between devices, per_device(): held = lax.all_to_all(spread, 'width', 0, 0)  7.27 us
    ppermute x6, waiting for transfers between devices, along_line(): lax.ppermute(block, 'x', [((i + turn) % LINE, i) for i in range(LINE)])  3.7 us
    unnamed x14, local copies, waits for them, and re-layouts  3.04 us
  transfers between devices with their start and end apart: 10, of which 4 were waited for; matrix products, arithmetic and copies ran while one was open for 0% of the time, Pallas kernels for 4%

profile of v10, /device:TPU:57, one launch (start us, length us, event | category | flops | bytes accessed | tf_op | source)
XLA Modules:
  0.0 108.7 jit_solution(2701590600088877064)
XLA Ops:
  0.7 2.0 %shard_map.68 = bf16[16,144,128]{2,1,0:T(8,128)(2,1)} custom-call(bf16[288,256]{1,0:T(8,128)(2,1)} %bitcast.19, bf16[288,256]{1,0:T(8,128)(2,1)} %bitcast.20), custom_call_target="tpu_custom_call" | custom-call | tf_op jit(solution)/shard_map/pallas_call | solution.py:153
  2.7 8.9 %all-to-all-start = ((bf16[16,144,128]{2,1,0:T(8,128)(2,1)}), bf16[16,144,128]{2,1,0:T(8,128)(2,1)S(1)}, u32[]{:S(2)}, u32[]{:S(2)}) async-start(bf16[16,144,128]{2,1,0:T(8,128)(2,1)} %shard_map.68), calls=%async_computation | async-start | bytes 1179648 | tf_op jit(solution)/shard_map/all_to_all | solution.py:164
  11.7 2.3 %collective-permute-start = (bf16[304,256]{1,0:T(8,128)(2,1)S(1)}, bf16[304,256]{1,0:T(8,128)(2,1)S(1)}, u32[]{:S(2)}, u32[]{:S(2)}) collective-permute-start(bf16[304,256]{1,0:T(8,128)(2,1)S(1)} %pad_maximum_fusion), channel_id=1, source_target_pairs={{0,4},{4,0},{1,5},{5,1},{2,6},{6,2},{3,7},{7,3},{8,12},{12,8},{9,1... | collective-permute-start | bytes 466952 | tf_op jit(solution)/shard_map/ppermute | solution.py:22
  14.0 1.0 collective-permute-done.other
  15.0 1.1 %shard_map.69 = (bf16[4,288,512]{2,1,0:T(8,128)(2,1)}, f32[16,512]{1,0:T(8,128)S(1)}) custom-call(bf16[288,256]{1,0:T(8,128)(2,1)S(1)} %get-tuple-element.23.mine, s32[1,256]{1,0:T(1,128)S(1)} %copy-done.4, bf16[304,256]{1,0:T(8,128)(2,1)S(1)} %collective-permute-done.other), custom_call_target="tpu_custom_call" | custom-call | tf_op jit(solution)/shard_map/pallas_call | solution.py:170
  16.1 0.6 copy-done.2
  16.7 10.2 %all-to-all-done.dealt = bf16[16,144,128]{2,1,0:T(8,128)(2,1)S(1)} async-done(((bf16[16,144,128]{2,1,0:T(8,128)(2,1)}), bf16[16,144,128]{2,1,0:T(8,128)(2,1)S(1)}, u32[]{:S(2)}, u32[]{:S(2)}) %all-to-all-start) | async-done | bytes 589856 | tf_op jit(solution)/shard_map/all_to_all | solution.py:164
  26.9 0.2 shard_map.70
  27.1 9.1 %collective-permute-start.1 = (bf16[1152,128]{1,0:T(8,128)(2,1)S(1)}, bf16[1152,128]{1,0:T(8,128)(2,1)S(1)}, u32[]{:S(2)}, u32[]{:S(2)}) collective-permute-start(bf16[1152,128]{1,0:T(8,128)(2,1)S(1)} %get-tuple-element.13.pair), channel_id=1, source_target_pairs={{0,64},{32,480},{64,128},{96,32},{128,192},{160,96},{192,256},{224... | collective-permute-start | bytes 884744 | tf_op jit(solution)/shard_map/ppermute | solution.py:191
  36.2 7.3 %all-to-all-start.1 = ((bf16[4,288,512]{2,1,0:T(8,128)(2,1)}), bf16[4,288,512]{2,1,0:T(8,128)(2,1)S(1)}, u32[]{:S(2)}, u32[]{:S(2)}) async-start(bf16[4,288,512]{2,1,0:T(8,128)(2,1)} %get-tuple-element.17), calls=%async_computation.1 | async-start | bytes 2359296 | tf_op jit(solution)/shard_map/all_to_all | solution.py:189
  43.5 4.6 %collective-permute-start.5 = (bf16[1152,128]{1,0:T(8,128)(2,1)S(1)}, bf16[1152,128]{1,0:T(8,128)(2,1)S(1)}, u32[]{:S(2)}, u32[]{:S(2)}) collective-permute-start(bf16[1152,128]{1,0:T(8,128)(2,1)S(1)} %get-tuple-element.19.own), channel_id=1, source_target_pairs={{16,0},{24,8},{0,16},{8,24},{17,1},{25,9},{1,17},{9,25},{18,2},{26... | collective-permute-start | bytes 884744 | tf_op jit(solution)/shard_map/ppermute | solution.py:26
  48.1 2.2 %collective-permute-start.6 = (bf16[1152,128]{1,0:T(8,128)(2,1)S(1)}, bf16[1152,128]{1,0:T(8,128)(2,1)S(1)}, u32[]{:S(2)}, u32[]{:S(2)}) collective-permute-start(bf16[1152,128]{1,0:T(8,128)(2,1)S(1)} %get-tuple-element.19.own), channel_id=1, source_target_pairs={{24,0},{0,8},{8,16},{16,24},{25,1},{1,9},{9,17},{17,25},{26,2},{2,... | collective-permute-start | bytes 884744 | tf_op jit(solution)/shard_map/ppermute | solution.py:26
  50.4 4.3 %collective-permute-start.7 = (bf16[1152,128]{1,0:T(8,128)(2,1)S(1)}, bf16[1152,128]{1,0:T(8,128)(2,1)S(1)}, u32[]{:S(2)}, u32[]{:S(2)}) collective-permute-start(bf16[1152,128]{1,0:T(8,128)(2,1)S(1)} %get-tuple-element.19.own), channel_id=1, source_target_pairs={{8,0},{16,8},{24,16},{0,24},{9,1},{17,9},{25,17},{1,25},{10,2},{18... | collective-permute-start | bytes 884744 | tf_op jit(solution)/shard_map/ppermute | solution.py:26
  54.6 1.1 %shard_map.71 = (bf16[1152,128]{1,0:T(8,128)(2,1)}, bf16[1152,128]{1,0:T(8,128)(2,1)}, bf16[1152,128]{1,0:T(8,128)(2,1)}) custom-call(bf16[1152,128]{1,0:T(8,128)(2,1)S(1)} %get-tuple-element.13.pair, bf16[1152,128]{1,0:T(8,128)(2,1)S(1)} %collective-permute-done.1.far), custom_call_target="tpu_custom_call" | custom-call | flops 15000000512 | bytes 2097152 | tf_op jit(solution)/shard_map/pallas_call | solution.py:194
  55.8 1.9 %collective-permute-start.2 = (bf16[1152,128]{1,0:T(8,128)(2,1)}, bf16[1152,128]{1,0:T(8,128)(2,1)S(1)}, u32[]{:S(2)}, u32[]{:S(2)}) collective-permute-start(bf16[1152,128]{1,0:T(8,128)(2,1)} %get-tuple-element.14), channel_id=1, source_target_pairs={{16,0},{24,8},{0,16},{8,24},{17,1},{25,9},{1,17},{9,25},{18,2},{26... | collective-permute-start | bytes 884744 | tf_op jit(solution)/shard_map/ppermute | solution.py:26
  57.7 3.4 %collective-permute-start.3 = (bf16[1152,128]{1,0:T(8,128)(2,1)}, bf16[1152,128]{1,0:T(8,128)(2,1)S(1)}, u32[]{:S(2)}, u32[]{:S(2)}) collective-permute-start(bf16[1152,128]{1,0:T(8,128)(2,1)} %get-tuple-element.15), channel_id=1, source_target_pairs={{8,0},{16,8},{24,16},{0,24},{9,1},{17,9},{25,17},{1,25},{10,2},{18... | collective-permute-start | bytes 884744 | tf_op jit(solution)/shard_map/ppermute | solution.py:26
  61.1 0.0 collective-permute-done.5.l2
  61.1 1.9 %collective-permute-start.4 = (bf16[1152,128]{1,0:T(8,128)(2,1)}, bf16[1152,128]{1,0:T(8,128)(2,1)S(1)}, u32[]{:S(2)}, u32[]{:S(2)}) collective-permute-start(bf16[1152,128]{1,0:T(8,128)(2,1)} %get-tuple-element.16), channel_id=1, source_target_pairs={{24,0},{0,8},{8,16},{16,24},{25,1},{1,9},{9,17},{17,25},{26,2},{2,... | collective-permute-start | bytes 884744 | tf_op jit(solution)/shard_map/ppermute | solution.py:26
  64.3 0.0 collective-permute-done.6.l3
  64.3 0.0 collective-permute-done.7.l1
  64.4 0.7 copy-done
  65.1 2.8 %all-to-all-done.1 = bf16[4,288,512]{2,1,0:T(8,128)(2,1)S(1)} async-done(((bf16[4,288,512]{2,1,0:T(8,128)(2,1)}), bf16[4,288,512]{2,1,0:T(8,128)(2,1)S(1)}, u32[]{:S(2)}, u32[]{:S(2)}) %all-to-all-start.1) | async-done | bytes 1179680 | tf_op jit(solution)/shard_map/all_to_all | solution.py:189
  67.9 1.0 copy-done.1
  68.8 0.8 copy-done.3
  69.6 1.6 %shard_map.72.near = f32[1152,512]{1,0:T(8,128)S(1)} custom-call(f32[1]{0:T(128)} %copy.7.scale, f32[1]{0:T(128)S(6)} %copy.8.bias, f32[16,512]{1,0:T(8,128)S(1)} %copy-done.3, bf16[1152,128]{1,0:T(8,128)(2,1)S(1)} %get-tuple-element.19.own, bf16[1152,128]{1,0:T(8,128)(2,1)S(1)} %collective-permute-done.5.l2, ...), custom_call_target="tpu_custom_call" | custom-call | flops 1207959552 | bytes 5242880 | tf_op jit(solution)/shard_map/pallas_call | solution.py:208
  71.2 0.0 collective-permute-done.2.h2
  71.2 3.7 %collective-permute-done.3.h1 = bf16[1152,128]{1,0:T(8,128)(2,1)S(1)} collective-permute-done((bf16[1152,128]{1,0:T(8,128)(2,1)}, bf16[1152,128]{1,0:T(8,128)(2,1)S(1)}, u32[]{:S(2)}, u32[]{:S(2)}) %collective-permute-start.3) | collective-permute-done | bytes 294944 | tf_op jit(solution)/shard_map/ppermute | solution.py:26
  74.9 0.0 collective-permute-done.4.h3
  74.9 1.6 %shard_map.73 = bf16[8,288,256]{2,1,0:T(8,128)(2,1)S(1)} custom-call(f32[1]{0:T(128)} %copy.7.scale, f32[1]{0:T(128)S(6)} %copy.8.bias, bf16[1152,128]{1,0:T(8,128)(2,1)S(1)} %get-tuple-element.13.pair, bf16[1152,128]{1,0:T(8,128)(2,1)S(1)} %collective-permute-done.1.far, bf16[1152,128]{1,0:T(8,128)(2,1)S(1)} %collective-permute-done.2.h2, ...), custom_call_target="tpu_custom_call" | custom-call | flops 1207959552 | bytes 5242880 | tf_op jit(solution)/shard_map/pallas_call | solution.py:216
  76.5 31.0 %all_to_all.15 = bf16[8,288,256]{2,1,0:T(8,128)(2,1)S(1)} all-to-all(bf16[8,288,256]{2,1,0:T(8,128)(2,1)S(1)} %shard_map.73), channel_id=1, replica_groups=mesh['row'=8,'level'=2,'x'=4,'core'=2,'width'=4] {'core','width'}, dimensions={0} | all-to-all | bytes 2359296 | tf_op jit(solution)/shard_map/all_to_all | solution.py:224
  107.5 0.2 convert_element_type.7
  107.7 1.0 fusion.1
  (15 shorter events, 0.1 us)
Async XLA Ops:
  0.6 11.0 %copy-start.5 = (bf16[256,288]{0,1:T(8,128)(2,1)S(1)}, bf16[256,288]{0,1:T(8,128)(2,1)}, u32[]{:S(2)}) copy-start(bf16[256,288]{0,1:T(8,128)(2,1)} %param.5) | copy-start | bytes 442372
  0.6 11.0 %copy-start.6 = (bf16[256,288]{0,1:T(8,128)(2,1)S(1)}, bf16[256,288]{0,1:T(8,128)(2,1)}, u32[]{:S(2)}) copy-start(bf16[256,288]{0,1:T(8,128)(2,1)} %param.6) | copy-start | bytes 442372
  0.6 11.0 %copy-start.4 = (s32[1,256]{1,0:T(1,128)S(1)}, s32[1,256]{1,0:T(1,128)}, u32[]{:S(2)}) copy-start(s32[1,256]{1,0:T(1,128)} %matches.1) | copy-start | bytes 3076
  2.7 24.2 %all-to-all-start = ((bf16[16,144,128]{2,1,0:T(8,128)(2,1)}), bf16[16,144,128]{2,1,0:T(8,128)(2,1)S(1)}, u32[]{:S(2)}, u32[]{:S(2)}) async-start(bf16[16,144,128]{2,1,0:T(8,128)(2,1)} %shard_map.68), calls=%async_computation | async-start | bytes 1179648 | tf_op jit(solution)/shard_map/all_to_all | solution.py:164
  11.7 3.3 %collective-permute-start = (bf16[304,256]{1,0:T(8,128)(2,1)S(1)}, bf16[304,256]{1,0:T(8,128)(2,1)S(1)}, u32[]{:S(2)}, u32[]{:S(2)}) collective-permute-start(bf16[304,256]{1,0:T(8,128)(2,1)S(1)} %pad_maximum_fusion), channel_id=1, source_target_pairs={{0,4},{4,0},{1,5},{5,1},{2,6},{6,2},{3,7},{7,3},{8,12},{12,8},{9,1... | collective-permute-start | bytes 466952 | tf_op jit(solution)/shard_map/ppermute | solution.py:22
  16.1 0.6 copy-start.2
  27.1 27.5 %collective-permute-start.1 = (bf16[1152,128]{1,0:T(8,128)(2,1)S(1)}, bf16[1152,128]{1,0:T(8,128)(2,1)S(1)}, u32[]{:S(2)}, u32[]{:S(2)}) collective-permute-start(bf16[1152,128]{1,0:T(8,128)(2,1)S(1)} %get-tuple-element.13.pair), channel_id=1, source_target_pairs={{0,64},{32,480},{64,128},{96,32},{128,192},{160,96},{192,256},{224... | collective-permute-start | bytes 884744 | tf_op jit(solution)/shard_map/ppermute | solution.py:191
  36.2 31.7 %all-to-all-start.1 = ((bf16[4,288,512]{2,1,0:T(8,128)(2,1)}), bf16[4,288,512]{2,1,0:T(8,128)(2,1)S(1)}, u32[]{:S(2)}, u32[]{:S(2)}) async-start(bf16[4,288,512]{2,1,0:T(8,128)(2,1)} %get-tuple-element.17), calls=%async_computation.1 | async-start | bytes 2359296 | tf_op jit(solution)/shard_map/all_to_all | solution.py:189
  43.5 17.6 %collective-permute-start.5 = (bf16[1152,128]{1,0:T(8,128)(2,1)S(1)}, bf16[1152,128]{1,0:T(8,128)(2,1)S(1)}, u32[]{:S(2)}, u32[]{:S(2)}) collective-permute-start(bf16[1152,128]{1,0:T(8,128)(2,1)S(1)} %get-tuple-element.19.own), channel_id=1, source_target_pairs={{16,0},{24,8},{0,16},{8,24},{17,1},{25,9},{1,17},{9,25},{18,2},{26... | collective-permute-start | bytes 884744 | tf_op jit(solution)/shard_map/ppermute | solution.py:26
  48.1 16.2 %collective-permute-start.6 = (bf16[1152,128]{1,0:T(8,128)(2,1)S(1)}, bf16[1152,128]{1,0:T(8,128)(2,1)S(1)}, u32[]{:S(2)}, u32[]{:S(2)}) collective-permute-start(bf16[1152,128]{1,0:T(8,128)(2,1)S(1)} %get-tuple-element.19.own), channel_id=1, source_target_pairs={{24,0},{0,8},{8,16},{16,24},{25,1},{1,9},{9,17},{17,25},{26,2},{2,... | collective-permute-start | bytes 884744 | tf_op jit(solution)/shard_map/ppermute | solution.py:26
  50.4 14.0 %collective-permute-start.7 = (bf16[1152,128]{1,0:T(8,128)(2,1)S(1)}, bf16[1152,128]{1,0:T(8,128)(2,1)S(1)}, u32[]{:S(2)}, u32[]{:S(2)}) collective-permute-start(bf16[1152,128]{1,0:T(8,128)(2,1)S(1)} %get-tuple-element.19.own), channel_id=1, source_target_pairs={{8,0},{16,8},{24,16},{0,24},{9,1},{17,9},{25,17},{1,25},{10,2},{18... | collective-permute-start | bytes 884744 | tf_op jit(solution)/shard_map/ppermute | solution.py:26
  55.8 15.4 %collective-permute-start.2 = (bf16[1152,128]{1,0:T(8,128)(2,1)}, bf16[1152,128]{1,0:T(8,128)(2,1)S(1)}, u32[]{:S(2)}, u32[]{:S(2)}) collective-permute-start(bf16[1152,128]{1,0:T(8,128)(2,1)} %get-tuple-element.14), channel_id=1, source_target_pairs={{16,0},{24,8},{0,16},{8,24},{17,1},{25,9},{1,17},{9,25},{18,2},{26... | collective-permute-start | bytes 884744 | tf_op jit(solution)/shard_map/ppermute | solution.py:26
  57.7 17.2 %collective-permute-start.3 = (bf16[1152,128]{1,0:T(8,128)(2,1)}, bf16[1152,128]{1,0:T(8,128)(2,1)S(1)}, u32[]{:S(2)}, u32[]{:S(2)}) collective-permute-start(bf16[1152,128]{1,0:T(8,128)(2,1)} %get-tuple-element.15), channel_id=1, source_target_pairs={{8,0},{16,8},{24,16},{0,24},{9,1},{17,9},{25,17},{1,25},{10,2},{18... | collective-permute-start | bytes 884744 | tf_op jit(solution)/shard_map/ppermute | solution.py:26
  61.1 13.8 %collective-permute-start.4 = (bf16[1152,128]{1,0:T(8,128)(2,1)}, bf16[1152,128]{1,0:T(8,128)(2,1)S(1)}, u32[]{:S(2)}, u32[]{:S(2)}) collective-permute-start(bf16[1152,128]{1,0:T(8,128)(2,1)} %get-tuple-element.16), channel_id=1, source_target_pairs={{24,0},{0,8},{8,16},{16,24},{25,1},{1,9},{9,17},{17,25},{26,2},{2,... | collective-permute-start | bytes 884744 | tf_op jit(solution)/shard_map/ppermute | solution.py:26
  64.4 0.7 copy-start
  67.9 1.0 copy-start.1
  68.8 0.8 copy-start.3
